TPU v7x, 128 devices: a whole 4x4x4 slice. The times are simulated.
128 devices in a mesh: dp: 32 (over z, x, core), grp: 4 (over y).
Axes of the slice: x: 4, y: 4, z: 4, core: 2. Of those that a mesh axis runs over, the one named last changes fastest.
Arguments:
- queries: bfloat16 [256, 4, 128, 576], P(('dp', 'grp')), may hold values from -64 to 64
- new_latent: bfloat16 [256, 4, 576], P(('dp', 'grp')), may hold values from -8 to 8
- latent_cache: bfloat16 [8192, 64, 576], P(('dp', 'grp')), may hold values from -6 to 6
- block_table: int32 [256, 32], P(('dp', 'grp')), may hold values from 0 to 63, as said below
- lengths: int32 [256], replicated, may hold values from 1 to 2048, as said below
- migration: int32 [128], replicated, may hold values from 0 to 1
- residual: bfloat16 [256, 4, 7168], P('dp', None, 'grp'), may hold values from -10 to 10
- value_projection_weight: bfloat16 [128, 512, 128], P('dp'), may hold values from -2 to 2
- output_proj: bfloat16 [16384, 7168], P('dp', 'grp'), may hold values from -0.046875 to 0.046875
- norm_gain: bfloat16 [7168], P('grp'), may hold values from 0.25 to 1.75
- gate_proj: bfloat16 [7168, 18432], P('grp', 'dp'), may hold values from -0.0625 to 0.0625
- up_proj: bfloat16 [7168, 18432], P('grp', 'dp'), may hold values from -0.0625 to 0.0625
- down_projection_matrix: bfloat16 [18432, 7168], P('dp', 'grp'), may hold values from -0.046875 to 0.046875
Outputs:
- layer_out: bfloat16 [256, 4, 7168], P('dp', None, 'grp')
Inputs may be any that keep to these rules, and one draw needn't show every extreme that they name: `lengths`: some row has exactly 2048 cached tokens. `block_table`: the rows of one device together name each of its 64 pages exactly once.
All inputs are finite; a program needn't handle non-finite values.
Results may differ from a plain program's by a relative error of at most 0.007.
Values may be sent and summed in bfloat16 or wider, within the bound.
No kernel may reach another device: no remote copies, remote signals or barrier semaphores. Data moves between devices by JAX's collectives and lax.ppermute only.
A program may use at most 128 MiB of HBM per device.

v0:
```python
import jax
import jax.numpy as jnp
from jax import lax
from jax.sharding import PartitionSpec as P

D = 7168
KV = 512
PAGE = 64
MAXP = 32


score_scale = 0.07216878364870323
tiny_eps = 1e-06
neg_fill = -1e30


def swapped(block, axis, bit):
    count = lax.axis_size(axis)
    route = []
    for low in range(count):
        high = low | 1 << bit
        if high != low and high < count:
            route += [(low, high), (high, low)]
    return lax.ppermute(block, axis, route)


def attend(query_rows, fresh_keys, key_rows, length):
    step_count = query_rows.shape[0]
    head_count = query_rows.shape[1]
    query_flat = query_rows.reshape(step_count * head_count, query_rows.shape[2])
    past_scores = (
        jnp.einsum("qc,kc->qk", query_flat, key_rows, preferred_element_type=jnp.float32)
        * score_scale
    )
    valid_keys = jnp.arange(key_rows.shape[0], dtype=jnp.int32) < length
    past_scores = jnp.where(valid_keys[None, :], past_scores, neg_fill)
    own_scores = (
        jnp.einsum("thc,sc->ths", query_rows, fresh_keys, preferred_element_type=jnp.float32)
        * score_scale
    )
    causal = jnp.arange(step_count)[None, :] <= jnp.arange(step_count)[:, None]
    own_scores = jnp.where(causal[:, None, :], own_scores, neg_fill).reshape(
        step_count * head_count, step_count
    )
    row_max = jnp.maximum(jnp.max(past_scores, axis=1), jnp.max(own_scores, axis=1))
    past_weight = jnp.exp(past_scores - row_max[:, None])
    own_weight = jnp.exp(own_scores - row_max[:, None])
    row_total = jnp.sum(past_weight, axis=1) + jnp.sum(own_weight, axis=1)
    past_probs = (past_weight / row_total[:, None]).astype(jnp.bfloat16)
    own_probs = (own_weight / row_total[:, None]).astype(jnp.bfloat16)
    result = jnp.dot(past_probs, key_rows[:, :KV], preferred_element_type=jnp.float32)
    result = result + jnp.dot(own_probs, fresh_keys[:, :KV], preferred_element_type=jnp.float32)
    return result.reshape(step_count, head_count, KV).astype(jnp.bfloat16)


def attend_all(inputs):
    return attend(inputs[0], inputs[1], inputs[2], inputs[3])


def on_device(
    queries,
    new_latent,
    latent_cache,
    block_table,
    lengths,
    migration,
    residual,
    value_projection_weight,
    output_proj,
    norm_gain,
    gate_proj,
    up_proj,
    down_projection_matrix,
):
    data_parallel_count = lax.axis_size("dp")
    grp_count = lax.axis_size("grp")
    flip_bit = data_parallel_count.bit_length() - 2
    dp_place = lax.axis_index("dp")
    group_position = lax.axis_index("grp")
    row_count = queries.shape[0]
    device = dp_place * grp_count + group_position
    partner = (
        dp_place + data_parallel_count // 2
    ) % data_parallel_count * grp_count + group_position
    own_move = migration[device]
    other_move = migration[partner]
    slot_ids = jnp.arange(row_count, dtype=jnp.int32)
    home_rows = device * row_count + slot_ids
    moved_slot = slot_ids == own_move
    own_keys = latent_cache[block_table].reshape(row_count, MAXP * PAGE, latent_cache.shape[2])
    outgoing = lax.dynamic_index_in_dim(own_keys, own_move, 0, keepdims=False)
    arrived = swapped(outgoing, "dp", flip_bit)
    slot_keys = jnp.where(moved_slot[:, None, None], arrived[None], own_keys)
    slot_len = jnp.where(moved_slot, lengths[partner * row_count + other_move], lengths[home_rows])
    latent_output = lax.map(attend_all, (queries, new_latent, slot_keys, slot_len))
    sectioned = latent_output.reshape((1,) + latent_output.shape)
    grouped = lax.all_to_all(sectioned, "dp", split_axis=3, concat_axis=0, tiled=True)
    col_width = output_proj.shape[1]
    partition_slice = lax.all_gather(grouped[:, None], "grp", axis=1, tiled=True)
    per_head_output = jnp.einsum(
        "naybwe,wem->naybwm",
        partition_slice,
        value_projection_weight,
        preferred_element_type=jnp.float32,
    ).astype(jnp.bfloat16)
    head_flat = per_head_output.reshape(-1, output_proj.shape[0])
    product = jnp.dot(head_flat, output_proj, preferred_element_type=jnp.float32)
    partial_sum = product.reshape(partition_slice.shape[:4] + (col_width,))
    partial_sum = partial_sum.reshape((-1,) + partial_sum.shape[3:])
    local_rows = residual.shape[0]
    gain_rows = norm_gain.astype(jnp.float32)
    own_first = dp_place * local_rows
    placed = lax.dynamic_update_slice_in_dim(
        jnp.zeros(partial_sum.shape, jnp.float32), residual.astype(jnp.float32), own_first, 0
    )
    mixed_all = lax.psum(partial_sum + placed, "dp")
    square_sum = lax.psum(jnp.sum(mixed_all * mixed_all, axis=2), "grp")
    normed_all = (mixed_all * lax.rsqrt(square_sum / D + tiny_eps)[:, :, None] * gain_rows).astype(
        jnp.bfloat16
    )
    mixed_rows = lax.dynamic_slice_in_dim(mixed_all, own_first, local_rows, 0)
    normed_flat = normed_all.reshape(-1, normed_all.shape[2])
    gate_part = jnp.dot(normed_flat, gate_proj, preferred_element_type=jnp.float32)
    up_part = jnp.dot(normed_flat, up_proj, preferred_element_type=jnp.float32)
    gate_sum, up_sum = lax.psum((gate_part, up_part), "grp")
    hidden = (jax.nn.silu(gate_sum) * up_sum).astype(jnp.bfloat16)
    hidden = hidden.reshape(normed_all.shape[0], normed_all.shape[1], hidden.shape[1])
    product = jnp.dot(
        hidden.reshape(-1, hidden.shape[2]),
        down_projection_matrix,
        preferred_element_type=jnp.float32,
    )
    down_share = lax.psum_scatter(
        product.reshape(
            local_rows * lax.axis_size("dp"), hidden.shape[1], down_projection_matrix.shape[1]
        ),
        "dp",
        scatter_dimension=0,
        tiled=True,
    )
    return (mixed_rows + down_share).astype(jnp.bfloat16)


def solution(mesh):
    placed = (
        P(("dp", "grp"), None, None, None),
        P(("dp", "grp"), None, None),
        P(("dp", "grp"), None, None),
        P(("dp", "grp"), None),
        P(),
        P(),
        P("dp", None, "grp"),
        P("dp", None, None),
        P("dp", "grp"),
        P("grp"),
        P("grp", "dp"),
        P("grp", "dp"),
        P("dp", "grp"),
    )
    return jax.shard_map(
        on_device, mesh=mesh, in_specs=placed, out_specs=P("dp", None, "grp"), check_vma=False
    )
```

profile of v0, /device:TPU:0, one launch (start us, length us, event | category | flops | bytes accessed | tf_op | source)
XLA Modules:
  0.0 577.0 jit_solution(13819338012970000697)
XLA Ops:
  6.5 1.4 fusion.32
  9.1 0.7 compare_select_fusion
  9.8 0.1 reshape.111
  10.4 6.0 %gather_fusion.1 = bf16[64,64,576]{2,1,0:T(8,128)(2,1)} fusion(bf16[64,64,576]{2,1,0:T(8,128)(2,1)} %param.17, s32[1024]{0:T(1024)S(1)} %pad_clamp_fusion), kind=kCustom, calls=%fused_computation.1 | custom fusion | bytes 9437440 | tf_op jit(solution)/shard_map/gather | solution.py:90
  16.4 3.5 constant_dynamic-slice_fusion.2
  19.8 4.5 copy.26
  24.3 4.0 collective-permute-start
  28.9 0.6 dynamic_slice.34
  29.6 0.6 gather_fusion
  30.2 0.6 iota_compare_fusion.2
  30.8 1.2 broadcast_select_fusion.1
  32.0 47.9 %collective-permute-done = bf16[2048,576]{0,1:T(8,128)(2,1)} collective-permute-done((bf16[2048,576]{0,1:T(8,128)(2,1)}, bf16[2048,576]{0,1:T(8,128)(2,1)}, u32[]{:S(2)}, u32[]{:S(2)}) %collective-permute-start) | collective-permute-done | bytes 2359328 | tf_op jit(solution)/shard_map/ppermute | solution.py:24
  79.8 4.4 copy.27
  84.2 6.3 %broadcast_select_fusion = bf16[2,2048,576]{2,1,0:T(8,128)(2,1)} fusion(pred[2]{0:T(512)(128)(4,1)S(1)} %iota_compare_fusion.2, bf16[2048,576]{1,0:T(8,128)(2,1)} %copy.27, bf16[2,2048,576]{2,1,0:T(8,128)(2,1)} %bitcast.102), kind=kLoop, calls=%fused_computation.42 | loop fusion | flops 2359296 | bytes 11796482 | tf_op jit(solution)/shard_map/jit(_where)/select_n | solution.py:93
  90.5 20.7 %while.10 = (s32[]{:T(128)}, bf16[2,4,128,512]{3,1,0,2:T(4,128)(2,1)}, s32[2]{0:T(128)S(1)}, bf16[2,4,128,576]{2,3,1,0:T(8,128)(2,1)S(1)}, bf16[2,2048,576]{2,1,...) while((s32[]{:T(128)}, bf16[2,4,128,512]{3,1,0,2:T(4,128)(2,1)}, s32[2]{0:T(128)S(1)}, ...), condition=%wide.region_5.6_spmd, body=%wide.region_0.5_spmd.sunk | while | flops 2299282944 | bytes 37447356 | solution.py:95
  90.5 0.6 dynamic_slice.66
  91.1 0.6 iota_compare_fusion.5
  91.8 0.2 fusion.57
  92.1 0.5 copy.59
  92.5 2.0 dynamic-slice_bitcast_fusion.4
  94.5 2.1 fusion.56
  96.6 0.9 fusion.58
  97.6 1.4 fusion.59
  99.0 0.4 fusion.60
  99.4 0.4 copy_dynamic-update-slice_fusion.2
  99.8 1.0 copy-done.5
  100.8 0.6 dynamic_slice.66
  101.4 0.6 iota_compare_fusion.5
  102.1 0.2 fusion.57
  102.4 0.5 copy.59
  102.9 2.0 dynamic-slice_bitcast_fusion.4
  104.8 2.1 fusion.56
  107.0 0.9 fusion.58
  107.9 1.4 fusion.59
  109.4 0.4 fusion.60
  109.7 0.4 copy_dynamic-update-slice_fusion.2
  110.2 1.0 copy-done.5
  111.2 25.0 %all_to_all.15 = bf16[1,2,4,128,512]{4,2,1,0,3:T(4,128)(2,1)S(1)} all-to-all(bf16[1,2,4,128,512]{4,2,1,0,3:T(4,128)(2,1)} %bitcast.107), channel_id=1, replica_groups=mesh['dp'=32,'grp'=4] {'dp'}, dimensions={3} | all-to-all | bytes 2097152 | tf_op jit(solution)/shard_map/all_to_all | solution.py:97
  136.2 1.6 copy.53
  137.8 0.2 all-reduce.4.cloned.1.call-start
  138.0 46.0 %all-gather.2.cloned.1.call-done = bf16[32,4,2,4,4,512]{5,0,3,2,1,4:T(8,128)(2,1)} async-done(((bf16[32,1,2,4,4,512]{5,0,3,2,1,4:T(8,128)(2,1)}), bf16[32,4,2,4,4,512]{5,0,3,2,1,4:T(8,128)(2,1)}) %all-gather.2.cloned.1.call-update) | async-done | bytes 4194320 | tf_op jit(solution)/shard_map/all_gather | solution.py:99
  184.0 3.4 fusion.25
  187.5 0.8 copy.32
  188.3 1.2 dot_general.30
  189.5 6.9 %fusion.23 = f32[256,4,1792]{2,0,1:T(8,128)} fusion(bf16[256,4,512]{2,0,1:T(8,128)(2,1)} %dot_general.30, bf16[512,1792]{1,0:T(8,128)(2,1)} %param.23), kind=kOutput, calls=%fused_computation.44 | convolution fusion | flops 1879048192 | bytes 10223616 | tf_op jit(solution)/shard_map/dot_general | solution.py:107
  196.4 1.7 add_dynamic-update-slice_fusion
  198.1 0.0 all-reduce.6.cloned.1.call-start
  198.2 0.6 copy-done.9
  198.8 117.9 %all-reduce.4.cloned.1.call-done = f32[256,4,1792]{2,0,1:T(8,128)} async-done(((f32[256,4,1792]{2,0,1:T(8,128)}), f32[256,4,1792]{2,0,1:T(8,128)}) %all-reduce.4.cloned.1.call-update) | async-done | bytes 7340048 | tf_op jit(solution)/shard_map/psum | solution.py:116
  316.7 3.6 multiply_reduce_fusion
  320.3 10.5 %psum.29 = f32[256,4]{0,1:T(4,128)S(1)} all-reduce(f32[256,4]{0,1:T(4,128)S(1)} %multiply_reduce_fusion), channel_id=1, replica_groups=mesh['dp'=32,'grp'=4] {'grp'}, use_global_device_ids=true, to_apply=%region_8.9 | all-reduce | flops 1024 | bytes 8192 | tf_op jit(solution)/shard_map/psum | solution.py:117
  330.8 3.7 multiply_convert_fusion
  334.5 4.7 copy.34
  339.3 6.9 %reshape.99 = bf16[1024,1792]{1,0:T(8,128)(2,1)} reshape(bf16[256,4,1792]{2,1,0:T(4,128)(2,1)} %copy.34) | data formatting | bytes 7340032 | tf_op jit(solution)/shard_map/reshape | solution.py:122
  346.2 6.7 %fusion.34 = f32[1024,576]{0,1:T(8,128)} fusion(bf16[1024,1792]{1,0:T(8,128)(2,1)} %reshape.99, bf16[1792,576]{0,1:T(8,128)(2,1)} %param.26), kind=kOutput, calls=%fused_computation.67 | convolution fusion | flops 2113929216 | bytes 8093696 | tf_op jit(solution)/shard_map/dot_general | solution.py:124
  352.8 3.8 fusion.33
  356.6 0.3 reduce-scatter.2.cloned.1.call-start
  356.9 98.4 %all-reduce.6.cloned.1.call-done = (f32[1024,576]{0,1:T(8,128)}, f32[1024,576]{0,1:T(8,128)}) async-done(((f32[1024,576]{0,1:T(8,128)}, f32[1024,576]{0,1:T(8,128)}), (f32[1024,576]{0,1:T(8,128)}, f32[1024,576]{0,1:T(8,128)})) %all-reduce.6.cloned.1.call-update) | async-done | bytes 4718608 | tf_op jit(solution)/shard_map/psum | solution.py:125
  455.3 8.1 %fusion.26 = f32[1024,1792]{1,0:T(8,128)} fusion(bf16[576,1792]{1,0:T(8,128)(2,1)S(1)} %copy-done, f32[1024,576]{0,1:T(8,128)} %get-tuple-element.62, f32[1024,576]{0,1:T(8,128)} %get-tuple-element.63), kind=kOutput, calls=%fused_computation.48 | convolution fusion | flops 2117468160 | bytes 14123008 | tf_op jit(solution)/shard_map/dot_general | solution.py:128
  463.4 9.2 %reshape.100 = f32[256,4,1792]{2,1,0:T(4,128)} reshape(f32[1024,1792]{1,0:T(8,128)} %fusion.26) | data formatting | bytes 14680064 | tf_op jit(solution)/shard_map/reshape | solution.py:134
  472.7 7.5 %copy.35 = f32[256,4,1792]{2,0,1:T(8,128)} copy(f32[256,4,1792]{2,1,0:T(4,128)} %reshape.100) | data formatting | bytes 14680064 | tf_op jit(solution)/shard_map/reshape | solution.py:134
  480.2 88.5 %reduce-scatter.2.cloned.1.call-done = f32[8,4,1792]{2,0,1:T(8,128)} async-done(((f32[256,4,1792]{2,0,1:T(8,128)}), f32[8,4,1792]{2,0,1:T(8,128)}) %reduce-scatter.2.cloned.1.call-update) | async-done | bytes 229392 | tf_op jit(solution)/shard_map/reduce_scatter | solution.py:133
  568.7 1.1 add_convert_fusion
  569.8 0.7 copy.36
  (48 shorter events, 0.4 us)
Async XLA Ops:
  6.5 448.8 %copy-start = (bf16[576,1792]{1,0:T(8,128)(2,1)S(1)}, bf16[576,1792]{1,0:T(8,128)(2,1)}, u32[]{:S(2)}) copy-start(bf16[576,1792]{1,0:T(8,128)(2,1)} %param.27) | copy-start | bytes 6193156
  6.5 177.5 %all-gather.2.cloned.1.call-start = ((), (), s32[]{:S(2)}) async-start(), calls=%async_computation.2 | async-start | bytes 5242880 | tf_op jit(solution)/shard_map/all_gather | solution.py:99
  19.8 9.0 %copy-start.1 = (s32[256]{0:T(256)S(1)}, s32[256]{0:T(256)}, u32[]{:S(2)}) copy-start(s32[256]{0:T(256)} %param.19) | copy-start | bytes 3076
  24.3 55.5 %collective-permute-start = (bf16[2048,576]{0,1:T(8,128)(2,1)}, bf16[2048,576]{0,1:T(8,128)(2,1)}, u32[]{:S(2)}, u32[]{:S(2)}) collective-permute-start(bf16[2048,576]{0,1:T(8,128)(2,1)} %bitcast.106), channel_id=1, source_target_pairs={{0,64},{64,0},{4,68},{68,4},{8,72},{72,8},{12,76},{76,12},{16,80},... | collective-permute-start | bytes 7077896 | tf_op jit(solution)/shard_map/ppermute | solution.py:24
  84.2 6.3 %copy-start.2 = (bf16[2,4,128,576]{2,3,1,0:T(8,128)(2,1)S(1)}, bf16[2,4,128,576]{2,3,1,0:T(8,128)(2,1)}, u32[]{:S(2)}) copy-start(bf16[2,4,128,576]{2,3,1,0:T(8,128)(2,1)} %param.15) | copy-start | bytes 3538948
  84.2 6.3 %copy-start.7 = (bf16[2,4,576]{2,1,0:T(4,128)(2,1)S(1)}, bf16[2,4,576]{2,1,0:T(4,128)(2,1)}, u32[]{:S(2)}) copy-start(bf16[2,4,576]{2,1,0:T(4,128)(2,1)} %param.16) | copy-start | bytes 27652
  97.6 1.8 copy-start.4
  99.8 1.0 copy-start.5
  107.9 1.8 copy-start.4
  110.2 1.0 copy-start.5
  111.2 72.8 %copy-start.6 = (bf16[4,512,128]{2,1,0:T(8,128)(2,1)S(1)}, bf16[4,512,128]{2,1,0:T(8,128)(2,1)}, u32[]{:S(2)}) copy-start(bf16[4,512,128]{2,1,0:T(8,128)(2,1)} %param.22) | copy-start | bytes 1572868
  137.8 178.9 %all-reduce.4.cloned.1.call-start = ((), (), s32[]{:S(2)}) async-start(), calls=%async_computation.3 | async-start | bytes 14680064 | tf_op jit(solution)/shard_map/psum | solution.py:116
  189.5 6.9 %copy-start.8 = (bf16[8,4,1792]{2,1,0:T(4,128)(2,1)S(1)}, bf16[8,4,1792]{2,1,0:T(4,128)(2,1)}, u32[]{:S(2)}) copy-start(bf16[8,4,1792]{2,1,0:T(4,128)(2,1)} %param.21) | copy-start | bytes 344068
  198.1 0.7 copy-start.9
  198.1 257.2 %all-reduce.6.cloned.1.call-start = ((), (), s32[]{:S(2)}) async-start(), calls=%async_computation.5 | async-start | bytes 9437184 | tf_op jit(solution)/shard_map/psum | solution.py:125
  346.2 6.7 %copy-start.3 = (bf16[1024,1792]{1,0:T(8,128)(2,1)S(1)}, bf16[1024,1792]{1,0:T(8,128)(2,1)}, u32[]{:S(2)}) copy-start(bf16[1024,1792]{1,0:T(8,128)(2,1)} %reshape.99) | copy-start | bytes 11010052
  346.2 6.7 %copy-start.10 = (bf16[1792,576]{0,1:T(8,128)(2,1)S(1)}, bf16[1792,576]{0,1:T(8,128)(2,1)}, u32[]{:S(2)}) copy-start(bf16[1792,576]{0,1:T(8,128)(2,1)} %param.25) | copy-start | bytes 6193156
  356.6 212.1 %reduce-scatter.2.cloned.1.call-start = ((), (), s32[]{:S(2)}) async-start(), calls=%async_computation.4 | async-start | bytes 7569408 | tf_op jit(solution)/shard_map/reduce_scatter | solution.py:133
Sparse Core Ops, SparseCore 0:
  137.9 46.0 all-gather.1
  198.2 118.3 all-reduce.3
  356.8 98.5 all-reduce.5
  480.3 88.3 reduce-scatter.1
where the time goes:
time: 578 us; the launch traced here: 577 us
  waiting for transfers between devices  399 us (69%)
  local copies, waits for them, and re-layouts  63.3 us (11%)
  matrix products  37.1 us (6%)
  blocking collectives  35.5 us (6%)
  other arithmetic  22.1 us (4%)
  between operations  15.5 us (3%)
    psum x1, waiting for transfers between devices, on_device(): mixed_all = lax.psum(partial_sum + placed, 'dp')  118 us
    psum x1, waiting for transfers between devices, on_device(): gate_sum, up_sum = lax.psum((gate_part, up_part), 'grp')  98.4 us
    reduce_scatter x1, waiting for transfers between devices, on_device(): lax.psum_scatter(product.reshape(local_rows * lax.axis_size('dp'), hidden...  88.5 us
    ppermute x1, waiting for transfers between devices, swapped(): return lax.ppermute(block, axis, route)  47.9 us
    all_gather x1, waiting for transfers between devices, on_device(): lax.all_gather(grouped[:, None], 'grp', axis=1, tiled=True)  46 us
    all_to_all x1, blocking collectives, on_device(): lax.all_to_all(sectioned, 'dp', split_axis=3, concat_axis=0, tiled=True)  25 us
    reshape x2, local copies, waits for them, and re-layouts, on_device(): product.reshape(local_rows * lax.axis_size('dp'), hidden.shape[1], down_p...  16.7 us
  transfers between devices with their start and end apart: 5, of which 5 were waited for; matrix products, arithmetic and copies ran while one was open for 1% of the time, Pallas kernels for 0%

commit v1 on v0

v1 whole, which is shorter than its diff:
```python
import functools

import jax
import jax.numpy as jnp
from jax import lax
from jax.experimental import pallas as pl
from jax.experimental.pallas import tpu as pltpu
from jax.sharding import PartitionSpec as P

D = 7168
KV = 512
KW = 576
PAGE = 64
MAXP = 32
STEPS = 4
HEADS = 128
TOKENS = PAGE * MAXP
CHUNK = 512
KEYS = TOKENS + 128
QROWS = STEPS * HEADS
CHIPS = 16
DCOL = D // 4
HALF = DCOL // 2
FFW = 1152
GW = 2 * FFW + 128

score_scale = 0.07216878364870323
exp2_scale = score_scale * 1.4426950408889634
tiny_eps = 1e-06
neg_fill = -1e30

BF = jnp.bfloat16
F32 = jnp.float32
VMEM = pl.BlockSpec(memory_space=pltpu.VMEM)
SMEM = pl.BlockSpec(memory_space=pltpu.SMEM)
ANY = pl.BlockSpec(memory_space=pl.ANY)


def params(mb=48):
    return pltpu.CompilerParams(vmem_limit_bytes=mb * 1024 * 1024)


def shape(dims, kind=BF):
    return jax.ShapeDtypeStruct(dims, kind)


def dot(a, b):
    return jnp.dot(a, b, preferred_element_type=F32)


def dot_t(a, b):
    return lax.dot_general(a, b, (((1,), (1,)), ((), ())), preferred_element_type=F32)


def pack_body(ids, mig, q_ref, f_ref, o_ref):
    o_ref[0, 0:QROWS, :] = q_ref[0]
    o_ref[0, QROWS : QROWS + 16, :] = f_ref[0]


def pack(ids, migration, queries, fresh):
    return pl.pallas_call(
        pack_body,
        out_shape=shape((1, QROWS + 16, KW)),
        grid_spec=pltpu.PrefetchScalarGridSpec(
            num_scalar_prefetch=2,
            grid=(1,),
            in_specs=[
                pl.BlockSpec((1, QROWS, KW), lambda i, ids, mig: (mig[ids[4]], 0, 0)),
                pl.BlockSpec((1, 16, KW), lambda i, ids, mig: (mig[ids[4]], 0, 0)),
            ],
            out_specs=pl.BlockSpec((1, QROWS + 16, KW), lambda i, ids, mig: (0, 0, 0)),
        ),
        compiler_params=params(),
    )(ids, migration, queries, fresh)


def attend_body(moved, ids, mig, table, lengths, q_ref, f_ref, cache, o_ref, kbuf, s_ref, m_ref, l_ref, a_ref, sems):
    own = mig[ids[4]]
    row = own if moved else 1 - own
    length = lengths[ids[4] * 2 + row]
    copies = []
    for i in range(MAXP):
        copy = pltpu.make_async_copy(
            cache.at[table[row, i]], kbuf.at[pl.ds(i * PAGE, PAGE), :], sems.at[i]
        )
        copy.start()
        copies.append(copy)
    kbuf[TOKENS : TOKENS + 16, :] = f_ref[0]
    kbuf[TOKENS + 16 :, :] = jnp.zeros((KEYS - TOKENS - 16, KW), BF)
    q = q_ref[0]
    step = lax.broadcasted_iota(jnp.int32, (QROWS, 128), 0) // HEADS
    place = lax.broadcasted_iota(jnp.int32, (QROWS, 128), 1)
    fresh = jnp.where(place <= step, dot_t(q, kbuf[TOKENS:, :]), neg_fill)
    s_ref[:, TOKENS:] = fresh
    m_ref[...] = fresh
    for c in range(TOKENS // CHUNK):
        for i in range(c * CHUNK // PAGE, (c + 1) * CHUNK // PAGE):
            copies[i].wait()

        @pl.when(c * CHUNK < length)
        def _():
            scores = dot_t(q, kbuf[c * CHUNK : (c + 1) * CHUNK, :])
            key = lax.broadcasted_iota(jnp.int32, (QROWS, CHUNK), 1) + c * CHUNK
            scores = jnp.where(key < length, scores, neg_fill)
            s_ref[:, c * CHUNK : (c + 1) * CHUNK] = scores
            best = m_ref[...]
            for k in range(CHUNK // 128):
                best = jnp.maximum(best, scores[:, k * 128 : (k + 1) * 128])
            m_ref[...] = best

    top = jnp.max(m_ref[...], axis=1, keepdims=True)
    m_ref[...] = jnp.broadcast_to(top, (QROWS, 128))
    weight = jnp.exp2((s_ref[:, TOKENS:] - top) * exp2_scale)
    l_ref[...] = weight
    a_ref[...] = dot(weight.astype(BF), kbuf[TOKENS:, :KV])
    for c in range(TOKENS // CHUNK):

        @pl.when(c * CHUNK < length)
        def _():
            top = m_ref[:, 0:1]
            weight = jnp.exp2((s_ref[:, c * CHUNK : (c + 1) * CHUNK] - top) * exp2_scale)
            total = l_ref[...]
            for k in range(CHUNK // 128):
                total = total + weight[:, k * 128 : (k + 1) * 128]
            l_ref[...] = total
            a_ref[...] += dot(weight.astype(BF), kbuf[c * CHUNK : (c + 1) * CHUNK, :KV])

    out = a_ref[...] / jnp.sum(l_ref[...], axis=1, keepdims=True)
    for k in range(CHIPS):
        parts = [out[t * HEADS + k * 8 : t * HEADS + k * 8 + 8] for t in range(STEPS)]
        o_ref[k] = jnp.concatenate(parts, axis=0).astype(BF)


def attend(moved, ids, migration, table, lengths, queries, fresh, cache):
    if moved:
        q_map = lambda i, ids, mig, tab, lens: (0, 0, 0)
        f_map = lambda i, ids, mig, tab, lens: (0, QROWS // 16, 0)
    else:
        q_map = f_map = lambda i, ids, mig, tab, lens: (1 - mig[ids[4]], 0, 0)
    return pl.pallas_call(
        functools.partial(attend_body, moved),
        out_shape=shape((CHIPS, 32, KV)),
        grid_spec=pltpu.PrefetchScalarGridSpec(
            num_scalar_prefetch=4,
            grid=(1,),
            in_specs=[
                pl.BlockSpec((1, QROWS, KW), q_map),
                pl.BlockSpec((1, 16, KW), f_map),
                ANY,
            ],
            out_specs=pl.BlockSpec((CHIPS, 32, KV), lambda i, *_: (0, 0, 0)),
            scratch_shapes=[
                pltpu.VMEM((KEYS, KW), BF),
                pltpu.VMEM((QROWS, KEYS), F32),
                pltpu.VMEM((QROWS, 128), F32),
                pltpu.VMEM((QROWS, 128), F32),
                pltpu.VMEM((QROWS, KV), F32),
                pltpu.SemaphoreType.DMA((MAXP,)),
            ],
        ),
        compiler_params=params(),
    )(ids, migration, table, lengths, queries, fresh, cache)


def value_body(ids, mig, kept, moved, w_own, w_sib, o_ref, x_ref):
    grp, core = ids[0], ids[3]
    for k in range(CHIPS):
        first = mig[(2 * k + core) * 4 + grp] == 0
        a, b = kept[k], moved[(k + CHIPS // 2) % CHIPS]
        x_ref[k * 64 : k * 64 + 32, :] = jnp.where(first, b, a)
        x_ref[k * 64 + 32 : k * 64 + 64, :] = jnp.where(first, a, b)
    w = jnp.concatenate([w_own[h] for h in range(4)] + [w_sib[h] for h in range(4)], axis=1)
    head = lax.broadcasted_iota(jnp.int32, (256, 1024), 0) % 8
    place = lax.broadcasted_iota(jnp.int32, (256, 1024), 1) // 128
    meant = head == (place + 4 * core) % 8
    pick = lax.broadcasted_iota(jnp.int32, (32, 256), 1) // 8
    pick = (pick == lax.broadcasted_iota(jnp.int32, (32, 256), 0)).astype(BF)
    for n in range(4):
        y = dot(x_ref[n * 256 : (n + 1) * 256, :], w)
        y = jnp.where(meant, y, 0.0).astype(BF)
        o_ref[n * 32 : (n + 1) * 32, :] = dot(pick, y).astype(BF)


def value(ids, migration, kept, moved, w_own, w_sib):
    return pl.pallas_call(
        value_body,
        out_shape=shape((128, 1024)),
        in_specs=[SMEM, SMEM, VMEM, VMEM, VMEM, VMEM],
        out_specs=VMEM,
        scratch_shapes=[pltpu.VMEM((1024, KV), BF)],
        compiler_params=params(),
    )(ids, migration, kept, moved, w_own, w_sib)


def mix_body(ids, h0, h1, h2, h3, w_own, w_sib, o_ref, h_ref):
    @pl.when(pl.program_id(0) == 0)
    def _():
        for s, h in enumerate((h0, h1, h2, h3)):
            h_ref[(ids[0] - s) & 3] = h[...]

    h = h_ref[...].reshape(512, 1024)
    out = dot(h[:, :512], w_own[...]) + dot(h[:, 512:], w_sib[...])
    for k in range(CHIPS):
        parts = [out[y * 128 + k * 8 : y * 128 + k * 8 + 8] for y in range(4)]
        o_ref[k] = jnp.concatenate(parts, axis=0).astype(BF)


def mix(ids, hs, w_own, w_sib):
    col = 256
    h_spec = pl.BlockSpec((128, 1024), lambda i, ids: (0, 0))
    w_spec = pl.BlockSpec((512, col), lambda i, ids: (0, i))
    return pl.pallas_call(
        mix_body,
        out_shape=shape((CHIPS, 32, DCOL)),
        grid_spec=pltpu.PrefetchScalarGridSpec(
            num_scalar_prefetch=1,
            grid=(DCOL // col,),
            in_specs=[h_spec] * 4 + [w_spec] * 2,
            out_specs=pl.BlockSpec((CHIPS, 32, col), lambda i, ids: (0, 0, i)),
            scratch_shapes=[pltpu.VMEM((4, 128, 1024), BF)],
        ),
        compiler_params=params(),
    )(ids, *hs, w_own, w_sib)


def norm_body(r_ref, res, gain, m_ref, a_ref, b_ref):
    mixed = res[...].astype(F32)
    for k in range(CHIPS):
        mixed = mixed + r_ref[k].astype(F32)
    m_ref[...] = mixed
    scaled = (mixed * gain[...].astype(F32)).astype(BF)
    a_ref[...] = scaled[:, :HALF]
    b_ref[:, :HALF] = scaled[:, HALF:]
    square = jnp.sum(mixed * mixed, axis=1, keepdims=True)
    high = square.astype(BF)
    low = (square - high.astype(F32)).astype(BF)
    lane = lax.broadcasted_iota(jnp.int32, (32, 128), 1)
    b_ref[:, HALF:] = jnp.where(lane < 64, high.astype(F32), low.astype(F32)).astype(BF)


def norm(received, residual, gain):
    return pl.pallas_call(
        norm_body,
        out_shape=(shape((32, DCOL), F32), shape((32, HALF)), shape((32, HALF + 128))),
        in_specs=[VMEM] * 3,
        out_specs=(VMEM,) * 3,
        compiler_params=params(),
    )(received, residual, gain)


def lay_body(a0, a1, a2, a3, b0, b1, b2, b3, a_ref, b_ref):
    for s, a in enumerate((a0, a1, a2, a3)):
        a_ref[-s % 4] = a[...]
    for s, b in enumerate((b0, b1, b2, b3)):
        b_ref[-s % 4] = b[...]


def lay(a, b):
    return pl.pallas_call(
        lay_body,
        out_shape=(shape((4, 32, HALF)), shape((4, 32, HALF + 128))),
        in_specs=[VMEM] * 8,
        out_specs=(VMEM,) * 2,
        compiler_params=params(),
    )(*a, *b)


def gate_up_body(ids, a0, a1, a2, a3, b0, b1, b2, b3, g_own, g_sib, u_own, u_sib, o0, o1, o2, o3, x_ref, w_ref, sems):
    copies = []
    for n, w in enumerate((g_own, g_sib, u_own, u_sib)):
        copy = pltpu.make_async_copy(w, w_ref.at[n], sems.at[n])
        copy.start()
        copies.append(copy)
    grp = ids[0]
    outs = (o0, o1, o2, o3)
    for s, a in enumerate((a0, a1, a2, a3)):
        x_ref[(-s - grp) & 3, :, :HALF] = a[...].reshape(128, HALF)
    for dz in range(4):
        for s, b in enumerate((b0, b1, b2, b3)):
            dx = -s % 4
            x_ref[(dz - grp) & 3, dx * 32 : dx * 32 + 32, HALF:] = b[dz]
    x = x_ref[:, :, :DCOL].reshape(512, DCOL)
    for s in range(4):
        outs[s][:, 2 * FFW :] = x_ref[s, :, DCOL:]
    for n in range(2):
        copies[2 * n].wait()
        own = dot(x, w_ref[2 * n])
        copies[2 * n + 1].wait()
        sib = dot(x, w_ref[2 * n + 1])
        rest = jnp.concatenate([own[:, 512:], sib[:, 512:]], axis=1)
        for s in range(4):
            rows = slice(s * 128, s * 128 + 128)
            base = n * FFW
            outs[s][:, base : base + 512] = own[rows, :512].astype(BF)
            outs[s][:, base + 512 : base + 1024] = sib[rows, :512].astype(BF)
            outs[s][:, base + 1024 : base + FFW] = rest[rows].astype(BF)


def gate_up(ids, a, b, weights):
    return pl.pallas_call(
        gate_up_body,
        out_shape=(shape((128, GW)),) * 4,
        in_specs=[SMEM] + [VMEM] * 8 + [ANY] * 4,
        out_specs=(VMEM,) * 4,
        scratch_shapes=[
            pltpu.VMEM((4, 128, DCOL + 128), BF),
            pltpu.VMEM((4, DCOL, 576), BF),
            pltpu.SemaphoreType.DMA((4,)),
        ],
        compiler_params=params(),
    )(ids, *a, *b, *weights)


def hidden_body(g0, g1, g2, g3, o_ref):
    total = g0[...].astype(F32) + g1[...].astype(F32) + g2[...].astype(F32) + g3[...].astype(F32)
    square = jnp.sum(total[:, 2 * FFW :], axis=1, keepdims=True) * (1.0 / 64)
    scale = lax.rsqrt(square / D + tiny_eps)
    gate = total[:, :FFW] * scale
    up = total[:, FFW : 2 * FFW] * scale
    o_ref[...] = (gate / (1.0 + jnp.exp(-gate)) * up).astype(BF)


def hidden_of(parts):
    return pl.pallas_call(
        hidden_body,
        out_shape=shape((128, FFW)),
        in_specs=[VMEM] * 4,
        out_specs=VMEM,
        compiler_params=params(),
    )(*parts)


def down_body(ids, h0, h1, h2, h3, w_own, w_sib, o_ref, h_ref):
    @pl.when(pl.program_id(0) == 0)
    def _():
        for s, h in enumerate((h0, h1, h2, h3)):
            h_ref[(ids[0] - s) & 3] = h[...]

    h = h_ref[...].reshape(512, FFW)
    rest = jnp.concatenate([w_own[512:, :], w_sib[512:, :]], axis=0)
    out = dot(h[:, :512], w_own[:512, :]) + dot(h[:, 512:1024], w_sib[:512, :]) + dot(h[:, 1024:], rest)
    for dz in range(4):
        for dx in range(4):
            k = ((ids[1] + dz) & 3) * 4 + ((ids[2] + dx) & 3)
            first = (dz * 4 + dx) * 32
            o_ref[k] = out[first : first + 32].astype(BF)


def down(ids, hs, w_own, w_sib):
    col = 256
    h_spec = pl.BlockSpec((128, FFW), lambda i, ids: (0, 0))
    w_spec = pl.BlockSpec((576, col), lambda i, ids: (0, i))
    return pl.pallas_call(
        down_body,
        out_shape=shape((CHIPS, 32, DCOL)),
        grid_spec=pltpu.PrefetchScalarGridSpec(
            num_scalar_prefetch=1,
            grid=(DCOL // col,),
            in_specs=[h_spec] * 4 + [w_spec] * 2,
            out_specs=pl.BlockSpec((CHIPS, 32, col), lambda i, ids: (0, 0, i)),
            scratch_shapes=[pltpu.VMEM((4, 128, FFW), BF)],
        ),
        compiler_params=params(),
    )(ids, *hs, w_own, w_sib)


def finish_body(r_ref, m_ref, o_ref):
    total = m_ref[...]
    for k in range(CHIPS):
        total = total + r_ref[k].astype(F32)
    o_ref[...] = total.astype(BF)


def finish(received, mixed):
    return pl.pallas_call(
        finish_body,
        out_shape=shape((32, DCOL)),
        in_specs=[VMEM] * 2,
        out_specs=VMEM,
        compiler_params=params(),
    )(received, mixed)


def route(dz, dx, flip):
    pairs = []
    for z in range(4):
        for x in range(4):
            for core in range(2):
                to = (z + dz) % 4 * 8 + (x + dx) % 4 * 2 + (core ^ flip)
                pairs.append((z * 8 + x * 2 + core, to))
    return pairs


def sent(block, dz=0, dx=0, flip=0):
    return lax.ppermute(block, "dp", route(dz, dx, flip))


def turned(block, s):
    return lax.ppermute(block, "grp", [(i, (i + s) % 4) for i in range(4)])


def traded(blocks):
    same_core = [list(range(core, 32, 2)) for core in range(2)]
    return lax.all_to_all(blocks, "dp", 0, 0, tiled=True, axis_index_groups=same_core)


def on_device(
    queries,
    new_latent,
    latent_cache,
    block_table,
    lengths,
    migration,
    residual,
    value_projection_weight,
    output_proj,
    norm_gain,
    gate_proj,
    up_proj,
    down_projection_matrix,
):
    dp = lax.axis_index("dp")
    grp = lax.axis_index("grp")
    ids = jnp.stack([grp, dp // 8, dp // 2 % 4, dp % 2, dp * 4 + grp, grp, grp, grp]).astype(jnp.int32)
    queries = queries.reshape(2, QROWS, KW)
    fresh = jnp.pad(new_latent, ((0, 0), (0, 16 - STEPS), (0, 0)))
    residual_rows = residual.reshape(32, DCOL)
    gain = norm_gain.reshape(1, DCOL)

    outgoing = pack(ids, migration, queries, fresh)
    arrived = sent(outgoing, dz=2)
    value_sib = sent(value_projection_weight, flip=1)
    out_sib = sent(output_proj, flip=1)
    gate_sib = sent(gate_proj, flip=1)
    up_sib = sent(up_proj, flip=1)
    down_sib = sent(down_projection_matrix, flip=1)

    kept = attend(False, ids, migration, block_table, lengths, queries, fresh, latent_cache)
    moved = attend(True, ids, migration, block_table, lengths, arrived, arrived, latent_cache)
    kept = traded(kept)
    moved = traded(moved)
    heads = value(ids, migration, kept, moved, value_projection_weight, value_sib)
    heads = [heads] + [turned(heads, s) for s in (1, 2, 3)]
    partial = mix(ids, heads, output_proj, out_sib)
    mixed, a, b = norm(traded(partial), residual_rows, gain)
    a, b = lay(
        [a] + [sent(a, dx=s) for s in (1, 2, 3)],
        [b] + [sent(b, dz=s) for s in (1, 2, 3)],
    )
    parts = gate_up(
        ids,
        [a] + [sent(a, dz=s) for s in (1, 2, 3)],
        [b] + [sent(b, dx=s) for s in (1, 2, 3)],
        (gate_proj, gate_sib, up_proj, up_sib),
    )
    hid = hidden_of([parts[0]] + [turned(parts[s], s) for s in (1, 2, 3)])
    hid = [hid] + [turned(hid, s) for s in (1, 2, 3)]
    partial = down(ids, hid, down_projection_matrix, down_sib)
    out = finish(traded(partial), mixed)
    return out.reshape(8, 4, DCOL)


def solution(mesh):
    placed = (
        P(("dp", "grp"), None, None, None),
        P(("dp", "grp"), None, None),
        P(("dp", "grp"), None, None),
        P(("dp", "grp"), None),
        P(),
        P(),
        P("dp", None, "grp"),
        P("dp", None, None),
        P("dp", "grp"),
        P("grp"),
        P("grp", "dp"),
        P("grp", "dp"),
        P("dp", "grp"),
    )
    return jax.shard_map(
        on_device, mesh=mesh, in_specs=placed, out_specs=P("dp", None, "grp"), check_vma=False
    )
```

time: 578 us -> 244 us (0.42)
  waiting for transfers between devices: 399 us -> 105 us
  starting transfers between devices: 4.49 us -> 49.8 us
  Pallas kernels: 0 us -> 44.7 us
  local copies, waits for them, and re-layouts: 63.3 us -> 20.2 us
  matrix products: 37.1 us -> 0 us
  other arithmetic: 22.1 us -> 0 us
  between operations: 15.5 us -> 0.33 us
  blocking collectives: 35.5 us -> 25.5 us
    psum x2 -> x0, waiting for transfers between devices: 216 us -> none  [the longest x1 118 us: on_device(): mixed_all = lax.psum(partial_sum + placed, 'dp')]
    reduce_scatter x1 -> x0, waiting for transfers between devices: 88.5 us -> none  [on_device(): lax.psum_scatter(product.reshape(local_rows * lax.axis_size('dp'), hidden...]
    all_gather x1 -> x0, waiting for transfers between devices: 46 us -> none  [on_device(): lax.all_gather(grouped[:, None], 'grp', axis=1, tiled=True)]
    pallas_call x0 -> x11, Pallas kernels: none -> 44.7 us  [the longest x2 16 us: attend(): pl.pallas_call(functools.partial(attend_body, moved), out_shape=shape((CH...]
    all_to_all x0 -> x3, waiting for transfers between devices: none -> 37.8 us  [traded(): lax.all_to_all(blocks, 'dp', 0, 0, tiled=True, axis_index_groups=same_core)]
    dot_general x13 -> x0, matrix products: 37.1 us -> none  [the longest x1 8.09 us: on_device(): jnp.dot(hidden.reshape(-1, hidden.shape[2]), down_projection_matrix, pref...]
    ppermute x1 -> x27, starting transfers between devices: 3.96 us -> 33 us  [the longest x18 19 us: sent(): return lax.ppermute(block, 'dp', route(dz, dx, flip))]
    reshape x3, local copies, waits for them, and re-layouts: 23.6 us -> 0.72 us  [the longest x1 0.68 us: on_device(): return out.reshape(8, 4, DCOL)]
  transfers between devices with their start and end apart: 5 -> 30, of which waited for: 5 -> 14; matrix products, arithmetic and copies ran while one was open for 1% -> 7% of each run, Pallas kernels for 0% -> 13%
where the time goes in v1:
time: 244 us; the launch traced here: 245 us
  waiting for transfers between devices  105 us (43%)
  starting transfers between devices  49.8 us (20%)
  Pallas kernels  44.7 us (18%)
  blocking collectives  25.5 us (10%)
  local copies, waits for them, and re-layouts  20.2 us (8%)
    ppermute x9, waiting for transfers between devices, turned(): return lax.ppermute(block, 'grp', [(i, (i + s) % 4) for i in range(4)])  40.1 us
    all_to_all x3, waiting for transfers between devices, traded(): lax.all_to_all(blocks, 'dp', 0, 0, tiled=True, axis_index_groups=same_core)  37.8 us
    ppermute x18, waiting for transfers between devices, sent(): return lax.ppermute(block, 'dp', route(dz, dx, flip))  27 us
    all_to_all x1, blocking collectives, traded(): lax.all_to_all(blocks, 'dp', 0, 0, tiled=True, axis_index_groups=same_core)  25.5 us
    ppermute x18, starting transfers between devices, sent(): return lax.ppermute(block, 'dp', route(dz, dx, flip))  19 us
    all_to_all x3, starting transfers between devices, traded(): lax.all_to_all(blocks, 'dp', 0, 0, tiled=True, axis_index_groups=same_core)  16.7 us
    pallas_call x2, Pallas kernels, attend(): pl.pallas_call(functools.partial(attend_body, moved), out_shape=shape((CH...  16 us
    ppermute x9, starting transfers between devices, turned(): return lax.ppermute(block, 'grp', [(i, (i + s) % 4) for i in range(4)])  14 us
  transfers between devices with their start and end apart: 30, of which 14 were waited for; matrix products, arithmetic and copies ran while one was open for 7% of the time, Pallas kernels for 13%

profile of v1, /device:TPU:0, one launch (start us, length us, event | category | flops | bytes accessed | tf_op | source)
XLA Modules:
  0.0 245.3 jit_solution(8250179148228041970)
XLA Ops:
  0.0 1.7 copy.19
  1.8 0.1 stack.26.ids
  1.9 0.6 shard_map.128
  2.5 0.0 copy-start.3
  2.5 4.1 %collective-permute-start = (bf16[1,528,576]{2,1,0:T(8,128)(2,1)S(1)}, bf16[1,528,576]{2,1,0:T(8,128)(2,1)S(1)}, u32[]{:S(2)}, u32[]{:S(2)}) collective-permute-start(bf16[1,528,576]{2,1,0:T(8,128)(2,1)S(1)} %shard_map.128), channel_id=1, source_target_pairs={{0,64},{4,68},{8,72},{12,76},{16,80},{20,84},{24,88},{28,92},{32,9... | collective-permute-start | bytes 1824776 | tf_op jit(solution)/shard_map/ppermute | solution.py:395
  6.6 8.0 %shard_map.127 = bf16[16,32,512]{2,1,0:T(8,128)(2,1)} custom-call(s32[8]{0:T(128)S(1)} %stack.26.ids, s32[128]{0:T(128)S(1)} %copy-done.4, s32[2,32]{1,0:T(2,128)S(1)} %copy-done.5, s32[256]{0:T(256)S(1)} %copy-done.6, bf16[2,512,576]{2,1,0:T(8,128)(2,1)S(1)} %bitcast.7, bf16[2,16,576]{2,1,0:T(8,128)(2,1)S(1)} %pad.4.f_ref, bf16[64,64,576]{2,1,0:T(8,128)(2,1)} %cache.3), custom_call_target="tpu_custom_call" | custom-call | tf_op jit(solution)/shard_map/pallas_call | solution.py:140
  14.6 4.3 %all-to-all-start = ((bf16[16,32,512]{2,1,0:T(8,128)(2,1)}), bf16[16,32,512]{2,1,0:T(8,128)(2,1)S(1)}, u32[]{:S(2)}, u32[]{:S(2)}) async-start(bf16[16,32,512]{2,1,0:T(8,128)(2,1)} %shard_map.127), calls=%async_computation | async-start | bytes 1048576 | tf_op jit(solution)/shard_map/all_to_all | solution.py:404
  18.9 0.1 collective-permute-start.1
  19.0 6.8 %collective-permute-done.q_ref.f_ref = bf16[1,528,576]{2,1,0:T(8,128)(2,1)S(1)} collective-permute-done((bf16[1,528,576]{2,1,0:T(8,128)(2,1)S(1)}, bf16[1,528,576]{2,1,0:T(8,128)(2,1)S(1)}, u32[]{:S(2)}, u32[]{:S(2)}) %collective-permute-start) | collective-permute-done | bytes 608288 | tf_op jit(solution)/shard_map/ppermute | solution.py:395
  25.8 8.0 %shard_map.129 = bf16[16,32,512]{2,1,0:T(8,128)(2,1)} custom-call(s32[8]{0:T(128)S(1)} %stack.26.ids, s32[128]{0:T(128)S(1)} %copy-done.4, s32[2,32]{1,0:T(2,128)S(1)} %copy-done.5, s32[256]{0:T(256)S(1)} %copy-done.6, bf16[1,528,576]{2,1,0:T(8,128)(2,1)S(1)} %collective-permute-done.q_ref.f_ref, bf16[1,528,576]{2,1,0:T(8,128)(2,1)S(1)} %collective-permute-done.q_ref.f_ref, ...), custom_call_target="tpu_custom_call" | custom-call | tf_op jit(solution)/shard_map/pallas_call | solution.py:140
  33.8 0.0 copy-start.2
  33.9 0.0 all-to-all-done.kept
  33.9 8.6 %all-to-all-start.1 = ((bf16[16,32,512]{2,1,0:T(8,128)(2,1)}), bf16[16,32,512]{2,1,0:T(8,128)(2,1)S(1)}, u32[]{:S(2)}, u32[]{:S(2)}) async-start(bf16[16,32,512]{2,1,0:T(8,128)(2,1)} %shard_map.129), calls=%async_computation.1 | async-start | bytes 1048576 | tf_op jit(solution)/shard_map/all_to_all | solution.py:404
  42.4 11.0 %all-to-all-done.1.moved = bf16[16,32,512]{2,1,0:T(8,128)(2,1)S(1)} async-done(((bf16[16,32,512]{2,1,0:T(8,128)(2,1)}), bf16[16,32,512]{2,1,0:T(8,128)(2,1)S(1)}, u32[]{:S(2)}, u32[]{:S(2)}) %all-to-all-start.1) | async-done | bytes 524320 | tf_op jit(solution)/shard_map/all_to_all | solution.py:404
  53.5 3.0 %shard_map.130.h0 = bf16[128,1024]{1,0:T(8,128)(2,1)S(1)} custom-call(s32[8]{0:T(128)S(1)} %stack.26.ids, s32[128]{0:T(128)S(1)} %copy-done.4, bf16[16,32,512]{2,1,0:T(8,128)(2,1)S(1)} %all-to-all-done.kept, bf16[16,32,512]{2,1,0:T(8,128)(2,1)S(1)} %all-to-all-done.1.moved, bf16[4,512,128]{2,1,0:T(8,128)(2,1)S(1)} %copy-done.3, ...), custom_call_target="tpu_custom_call" | custom-call | tf_op jit(solution)/shard_map/pallas_call | solution.py:185
  56.4 1.1 collective-permute-start.2
  57.5 2.6 %collective-permute-start.3 = (bf16[128,1024]{1,0:T(8,128)(2,1)S(1)}, bf16[128,1024]{1,0:T(8,128)(2,1)S(1)}, u32[]{:S(2)}, u32[]{:S(2)}) collective-permute-start(bf16[128,1024]{1,0:T(8,128)(2,1)S(1)} %shard_map.130.h0), channel_id=1, source_target_pairs={{0,2},{1,3},{2,0},{3,1},{4,6},{5,7},{6,4},{7,5},{8,10},{9,11},{10,... | collective-permute-start | bytes 786440 | tf_op jit(solution)/shard_map/ppermute | solution.py:399
  60.2 1.8 collective-permute-start.4
  61.9 3.5 %collective-permute-done.2.h1 = bf16[128,1024]{1,0:T(8,128)(2,1)S(1)} collective-permute-done((bf16[128,1024]{1,0:T(8,128)(2,1)S(1)}, bf16[128,1024]{1,0:T(8,128)(2,1)S(1)}, u32[]{:S(2)}, u32[]{:S(2)}) %collective-permute-start.2) | collective-permute-done | bytes 262176 | tf_op jit(solution)/shard_map/ppermute | solution.py:399
  65.4 6.8 %collective-permute-done.3.h2 = bf16[128,1024]{1,0:T(8,128)(2,1)S(1)} collective-permute-done((bf16[128,1024]{1,0:T(8,128)(2,1)S(1)}, bf16[128,1024]{1,0:T(8,128)(2,1)S(1)}, u32[]{:S(2)}, u32[]{:S(2)}) %collective-permute-start.3) | collective-permute-done | bytes 262176 | tf_op jit(solution)/shard_map/ppermute | solution.py:399
  72.2 6.3 %shard_map.131 = bf16[16,32,1792]{2,1,0:T(8,128)(2,1)S(1)} custom-call(s32[8]{0:T(128)S(1)} %stack.26.ids, bf16[128,1024]{1,0:T(8,128)(2,1)S(1)} %shard_map.130.h0, bf16[128,1024]{1,0:T(8,128)(2,1)S(1)} %collective-permute-done.2.h1, bf16[128,1024]{1,0:T(8,128)(2,1)S(1)} %collective-permute-done.3.h2, bf16[128,1024]{1,0:T(8,128)(2,1)S(1)} %collective-permute-done.4.h3, ...), custom_call_target="tpu_custom_call" | custom-call | tf_op jit(solution)/shard_map/pallas_call | solution.py:212
  78.5 1.3 copy-done
  79.8 3.8 %all-to-all-start.2 = ((bf16[16,32,1792]{2,1,0:T(8,128)(2,1)}), bf16[16,32,1792]{2,1,0:T(8,128)(2,1)S(1)}, u32[]{:S(2)}, u32[]{:S(2)}) async-start(bf16[16,32,1792]{2,1,0:T(8,128)(2,1)} %copy-done), calls=%async_computation.2 | async-start | bytes 3670016 | tf_op jit(solution)/shard_map/all_to_all | solution.py:404
  83.7 0.1 collective-permute-start.18
  83.8 0.5 collective-permute-start.19
  84.2 0.1 collective-permute-start.26
  84.4 26.8 %all-to-all-done.2.r_ref = bf16[16,32,1792]{2,1,0:T(8,128)(2,1)S(1)} async-done(((bf16[16,32,1792]{2,1,0:T(8,128)(2,1)}), bf16[16,32,1792]{2,1,0:T(8,128)(2,1)S(1)}, u32[]{:S(2)}, u32[]{:S(2)}) %all-to-all-start.2) | async-done | bytes 1835040 | tf_op jit(solution)/shard_map/all_to_all | solution.py:404
  111.2 0.3 shard_map.132
  111.5 0.0 collective-permute-start.6
  111.5 0.1 collective-permute-start.7
  111.6 5.9 %collective-permute-done.6.a1 = bf16[32,896]{1,0:T(8,128)(2,1)S(1)} collective-permute-done((bf16[32,896]{1,0:T(8,128)(2,1)S(1)}, bf16[32,896]{1,0:T(8,128)(2,1)S(1)}, u32[]{:S(2)}, u32[]{:S(2)}) %collective-permute-start.6) | collective-permute-done | bytes 57376 | tf_op jit(solution)/shard_map/ppermute | solution.py:395
  117.5 0.8 collective-permute-start.10
  118.3 2.6 %collective-permute-start.8 = (bf16[32,896]{1,0:T(8,128)(2,1)S(1)}, bf16[32,896]{1,0:T(8,128)(2,1)S(1)}, u32[]{:S(2)}, u32[]{:S(2)}) collective-permute-start(bf16[32,896]{1,0:T(8,128)(2,1)S(1)} %get-tuple-element.14.a0), channel_id=1, source_target_pairs={{0,24},{4,28},{8,0},{12,4},{16,8},{20,12},{24,16},{28,20},{32,56},... | collective-permute-start | bytes 172040 | tf_op jit(solution)/shard_map/ppermute | solution.py:395
  121.0 1.8 collective-permute-done.8.a3
  122.8 1.6 collective-permute-start.11
  124.4 0.4 collective-permute-start.9
  124.8 2.2 collective-permute-done.11.b3
  127.1 6.0 %collective-permute-done.9.b1 = bf16[32,1024]{1,0:T(8,128)(2,1)S(1)} collective-permute-done((bf16[32,1024]{1,0:T(8,128)(2,1)S(1)}, bf16[32,1024]{1,0:T(8,128)(2,1)S(1)}, u32[]{:S(2)}, u32[]{:S(2)}) %collective-permute-start.9) | collective-permute-done | bytes 65568 | tf_op jit(solution)/shard_map/ppermute | solution.py:395
  133.2 0.1 collective-permute-start.12
  133.2 0.8 collective-permute-start.13
  134.1 4.7 %collective-permute-start.16 = (bf16[4,32,1024]{2,1,0:T(8,128)(2,1)S(1)}, bf16[4,32,1024]{2,1,0:T(8,128)(2,1)S(1)}, u32[]{:S(2)}, u32[]{:S(2)}) collective-permute-start(bf16[4,32,1024]{2,1,0:T(8,128)(2,1)S(1)} %get-tuple-element.17.b0), channel_id=1, source_target_pairs={{0,16},{4,20},{8,24},{12,28},{16,0},{20,4},{24,8},{28,12},{32,48},... | collective-permute-start | bytes 786440 | tf_op jit(solution)/shard_map/ppermute | solution.py:395
  138.8 4.2 %collective-permute-done.12.a1 = bf16[4,32,896]{2,1,0:T(8,128)(2,1)S(1)} collective-permute-done((bf16[4,32,896]{2,1,0:T(8,128)(2,1)S(1)}, bf16[4,32,896]{2,1,0:T(8,128)(2,1)S(1)}, u32[]{:S(2)}, u32[]{:S(2)}) %collective-permute-start.12) | collective-permute-done | bytes 229408 | tf_op jit(solution)/shard_map/ppermute | solution.py:395
  142.9 3.0 %collective-permute-start.17 = (bf16[4,32,1024]{2,1,0:T(8,128)(2,1)S(1)}, bf16[4,32,1024]{2,1,0:T(8,128)(2,1)S(1)}, u32[]{:S(2)}, u32[]{:S(2)}) collective-permute-start(bf16[4,32,1024]{2,1,0:T(8,128)(2,1)S(1)} %get-tuple-element.17.b0), channel_id=1, source_target_pairs={{0,24},{4,28},{8,0},{12,4},{16,8},{20,12},{24,16},{28,20},{32,56},... | collective-permute-start | bytes 786440 | tf_op jit(solution)/shard_map/ppermute | solution.py:395
  145.9 0.0 collective-permute-start.14
  146.0 4.1 %copy.20.g_own = bf16[1792,576]{1,0:T(8,128)(2,1)} copy(bf16[1792,576]{0,1:T(8,128)(2,1)} %param.23) | data formatting | bytes 4128768 | tf_op args[10]
  150.1 4.1 %copy.22.u_own = bf16[1792,576]{1,0:T(8,128)(2,1)} copy(bf16[1792,576]{0,1:T(8,128)(2,1)} %param.24) | data formatting | bytes 4128768 | tf_op args[11]
  154.1 4.1 %copy.21.g_sib = bf16[1792,576]{1,0:T(8,128)(2,1)} copy(bf16[1792,576]{0,1:T(8,128)(2,1)} %collective-permute-done.18) | data formatting | bytes 4128768 | tf_op jit(solution)/shard_map/ppermute | solution.py:395
  158.2 4.1 %copy.23.u_sib = bf16[1792,576]{1,0:T(8,128)(2,1)} copy(bf16[1792,576]{0,1:T(8,128)(2,1)} %collective-permute-done.19) | data formatting | bytes 4128768 | tf_op jit(solution)/shard_map/ppermute | solution.py:395
  162.4 10.6 %shard_map.134 = (bf16[128,2432]{1,0:T(8,128)(2,1)S(1)}, bf16[128,2432]{1,0:T(8,128)(2,1)S(1)}, bf16[128,2432]{1,0:T(8,128)(2,1)S(1)}, bf16[128,2432]{1,0:T(8,128)(2,1)S(1)}) custom-call(s32[8]{0:T(128)S(1)} %stack.26.ids, bf16[4,32,896]{2,1,0:T(8,128)(2,1)S(1)} %get-tuple-element.16.a0, bf16[4,32,896]{2,1,0:T(8,128)(2,1)S(1)} %collective-permute-done.12.a1, ...), custom_call_target="tpu_custom_call" | custom-call | tf_op jit(solution)/shard_map/pallas_call | solution.py:300
  173.0 0.0 copy-start.1
  173.0 0.7 collective-permute-start.20
  173.7 2.5 %collective-permute-start.21 = (bf16[128,2432]{1,0:T(8,128)(2,1)S(1)}, bf16[128,2432]{1,0:T(8,128)(2,1)S(1)}, u32[]{:S(2)}, u32[]{:S(2)}) collective-permute-start(bf16[128,2432]{1,0:T(8,128)(2,1)S(1)} %get-tuple-element.20), channel_id=1, source_target_pairs={{0,2},{1,3},{2,0},{3,1},{4,6},{5,7},{6,4},{7,5},{8,10},{9,11},{10,... | collective-permute-start | bytes 1867784 | tf_op jit(solution)/shard_map/ppermute | solution.py:399
  176.1 1.8 collective-permute-start.22
  177.9 12.7 %collective-permute-done.20.g1 = bf16[128,2432]{1,0:T(8,128)(2,1)S(1)} collective-permute-done((bf16[128,2432]{1,0:T(8,128)(2,1)S(1)}, bf16[128,2432]{1,0:T(8,128)(2,1)S(1)}, u32[]{:S(2)}, u32[]{:S(2)}) %collective-permute-start.20) | collective-permute-done | bytes 622624 | tf_op jit(solution)/shard_map/ppermute | solution.py:399
  190.6 6.7 %collective-permute-done.21.g2 = bf16[128,2432]{1,0:T(8,128)(2,1)S(1)} collective-permute-done((bf16[128,2432]{1,0:T(8,128)(2,1)S(1)}, bf16[128,2432]{1,0:T(8,128)(2,1)S(1)}, u32[]{:S(2)}, u32[]{:S(2)}) %collective-permute-start.21) | collective-permute-done | bytes 622624 | tf_op jit(solution)/shard_map/ppermute | solution.py:399
  197.2 0.8 shard_map.135.h0
  198.0 0.1 collective-permute-start.23
  198.1 3.6 %collective-permute-start.24 = (bf16[128,1152]{1,0:T(8,128)(2,1)S(1)}, bf16[128,1152]{1,0:T(8,128)(2,1)S(1)}, u32[]{:S(2)}, u32[]{:S(2)}) collective-permute-start(bf16[128,1152]{1,0:T(8,128)(2,1)S(1)} %shard_map.135.h0), channel_id=1, source_target_pairs={{0,2},{1,3},{2,0},{3,1},{4,6},{5,7},{6,4},{7,5},{8,10},{9,11},{10,... | collective-permute-start | bytes 884744 | tf_op jit(solution)/shard_map/ppermute | solution.py:399
  201.6 7.3 %collective-permute-done.23.h1 = bf16[128,1152]{1,0:T(8,128)(2,1)S(1)} collective-permute-done((bf16[128,1152]{1,0:T(8,128)(2,1)S(1)}, bf16[128,1152]{1,0:T(8,128)(2,1)S(1)}, u32[]{:S(2)}, u32[]{:S(2)}) %collective-permute-start.23) | collective-permute-done | bytes 294944 | tf_op jit(solution)/shard_map/ppermute | solution.py:399
  209.0 3.2 %collective-permute-done.24.h2 = bf16[128,1152]{1,0:T(8,128)(2,1)S(1)} collective-permute-done((bf16[128,1152]{1,0:T(8,128)(2,1)S(1)}, bf16[128,1152]{1,0:T(8,128)(2,1)S(1)}, u32[]{:S(2)}, u32[]{:S(2)}) %collective-permute-start.24) | collective-permute-done | bytes 294944 | tf_op jit(solution)/shard_map/ppermute | solution.py:399
  212.1 6.7 %shard_map.136 = bf16[16,32,1792]{2,1,0:T(8,128)(2,1)S(1)} custom-call(s32[8]{0:T(128)S(1)} %stack.26.ids, bf16[128,1152]{1,0:T(8,128)(2,1)S(1)} %shard_map.135.h0, bf16[128,1152]{1,0:T(8,128)(2,1)S(1)} %collective-permute-done.23.h1, bf16[128,1152]{1,0:T(8,128)(2,1)S(1)} %collective-permute-done.24.h2, bf16[128,1152]{1,0:T(8,128)(2,1)S(1)} %collective-permute-done.25.h3, ...), custom_call_target="tpu_custom_call" | custom-call | tf_op jit(solution)/shard_map/pallas_call | solution.py:353
  218.9 25.5 %all_to_all.20.r_ref = bf16[16,32,1792]{2,1,0:T(8,128)(2,1)S(1)} all-to-all(bf16[16,32,1792]{2,1,0:T(8,128)(2,1)S(1)} %shard_map.136), channel_id=1, replica_groups={{0,8,16,24,32,40,48,56,64,72,80,88,96,104,112,120},{4,12,20,28,36,44,52..., dimensions={0} | all-to-all | bytes 3670016 | tf_op jit(solution)/shard_map/all_to_all | solution.py:404
  244.4 0.2 shard_map.137
  244.6 0.7 reshape.15
  (38 shorter events, 0.2 us)
Async XLA Ops:
  0.0 1.8 copy-start.8
  0.0 1.9 copy-start.4
  0.0 72.2 %collective-permute-start.5 = (bf16[512,1792]{1,0:T(8,128)(2,1)}, bf16[512,1792]{1,0:T(8,128)(2,1)}, u32[]{:S(2)}, u32[]{:S(2)}) collective-permute-start(bf16[512,1792]{1,0:T(8,128)(2,1)} %w_own.4), channel_id=1, source_target_pairs={{0,4},{4,0},{8,12},{12,8},{16,20},{20,16},{24,28},{28,24},{32,36},... | collective-permute-start | bytes 5505032 | tf_op jit(solution)/shard_map/ppermute | solution.py:395
  0.0 6.6 %copy-start.5 = (s32[2,32]{1,0:T(2,128)S(1)}, s32[2,32]{1,0:T(2,128)}, u32[]{:S(2)}) copy-start(s32[2,32]{1,0:T(2,128)} %table.3) | copy-start | bytes 772
  0.0 6.6 %copy-start.6 = (s32[256]{0:T(256)S(1)}, s32[256]{0:T(256)}, u32[]{:S(2)}) copy-start(s32[256]{0:T(256)} %lengths.3) | copy-start | bytes 3076
  2.5 16.4 %copy-start.3 = (bf16[4,512,128]{2,1,0:T(8,128)(2,1)S(1)}, bf16[4,512,128]{2,1,0:T(8,128)(2,1)}, u32[]{:S(2)}) copy-start(bf16[4,512,128]{2,1,0:T(8,128)(2,1)} %w_own.3) | copy-start | bytes 1572868
  2.5 23.3 %collective-permute-start = (bf16[1,528,576]{2,1,0:T(8,128)(2,1)S(1)}, bf16[1,528,576]{2,1,0:T(8,128)(2,1)S(1)}, u32[]{:S(2)}, u32[]{:S(2)}) collective-permute-start(bf16[1,528,576]{2,1,0:T(8,128)(2,1)S(1)} %shard_map.128), channel_id=1, source_target_pairs={{0,64},{4,68},{8,72},{12,76},{16,80},{20,84},{24,88},{28,92},{32,9... | collective-permute-start | bytes 1824776 | tf_op jit(solution)/shard_map/ppermute | solution.py:395
  14.6 19.3 %all-to-all-start = ((bf16[16,32,512]{2,1,0:T(8,128)(2,1)}), bf16[16,32,512]{2,1,0:T(8,128)(2,1)S(1)}, u32[]{:S(2)}, u32[]{:S(2)}) async-start(bf16[16,32,512]{2,1,0:T(8,128)(2,1)} %shard_map.127), calls=%async_computation | async-start | bytes 1048576 | tf_op jit(solution)/shard_map/all_to_all | solution.py:404
  18.9 23.5 %collective-permute-start.1 = (bf16[4,512,128]{2,1,0:T(8,128)(2,1)S(1)}, bf16[4,512,128]{2,1,0:T(8,128)(2,1)}, u32[]{:S(2)}, u32[]{:S(2)}) collective-permute-start(bf16[4,512,128]{2,1,0:T(8,128)(2,1)S(1)} %copy-done.3), channel_id=1, source_target_pairs={{0,4},{4,0},{8,12},{12,8},{16,20},{20,16},{24,28},{28,24},{32,36},... | collective-permute-start | bytes 1572872 | tf_op jit(solution)/shard_map/ppermute | solution.py:395
  33.8 38.4 %copy-start.2 = (bf16[512,1792]{1,0:T(8,128)(2,1)S(1)}, bf16[512,1792]{1,0:T(8,128)(2,1)}, u32[]{:S(2)}) copy-start(bf16[512,1792]{1,0:T(8,128)(2,1)} %w_own.4) | copy-start | bytes 5505028
  33.9 19.6 %all-to-all-start.1 = ((bf16[16,32,512]{2,1,0:T(8,128)(2,1)}), bf16[16,32,512]{2,1,0:T(8,128)(2,1)S(1)}, u32[]{:S(2)}, u32[]{:S(2)}) async-start(bf16[16,32,512]{2,1,0:T(8,128)(2,1)} %shard_map.129), calls=%async_computation.1 | async-start | bytes 1048576 | tf_op jit(solution)/shard_map/all_to_all | solution.py:404
  56.4 9.0 %collective-permute-start.2 = (bf16[128,1024]{1,0:T(8,128)(2,1)S(1)}, bf16[128,1024]{1,0:T(8,128)(2,1)S(1)}, u32[]{:S(2)}, u32[]{:S(2)}) collective-permute-start(bf16[128,1024]{1,0:T(8,128)(2,1)S(1)} %shard_map.130.h0), channel_id=1, source_target_pairs={{0,1},{1,2},{2,3},{3,0},{4,5},{5,6},{6,7},{7,4},{8,9},{9,10},{10,1... | collective-permute-start | bytes 786440 | tf_op jit(solution)/shard_map/ppermute | solution.py:399
  57.5 14.7 %collective-permute-start.3 = (bf16[128,1024]{1,0:T(8,128)(2,1)S(1)}, bf16[128,1024]{1,0:T(8,128)(2,1)S(1)}, u32[]{:S(2)}, u32[]{:S(2)}) collective-permute-start(bf16[128,1024]{1,0:T(8,128)(2,1)S(1)} %shard_map.130.h0), channel_id=1, source_target_pairs={{0,2},{1,3},{2,0},{3,1},{4,6},{5,7},{6,4},{7,5},{8,10},{9,11},{10,... | collective-permute-start | bytes 786440 | tf_op jit(solution)/shard_map/ppermute | solution.py:399
  60.2 12.0 %collective-permute-start.4 = (bf16[128,1024]{1,0:T(8,128)(2,1)S(1)}, bf16[128,1024]{1,0:T(8,128)(2,1)S(1)}, u32[]{:S(2)}, u32[]{:S(2)}) collective-permute-start(bf16[128,1024]{1,0:T(8,128)(2,1)S(1)} %shard_map.130.h0), channel_id=1, source_target_pairs={{0,3},{1,0},{2,1},{3,2},{4,7},{5,4},{6,5},{7,6},{8,11},{9,8},{10,9... | collective-permute-start | bytes 786440 | tf_op jit(solution)/shard_map/ppermute | solution.py:399
  78.5 1.3 copy-start
  79.8 4.5 %copy-start.7 = (bf16[8,4,1792]{2,1,0:T(4,128)(2,1)S(1)}, bf16[8,4,1792]{2,1,0:T(4,128)(2,1)}, u32[]{:S(2)}) copy-start(bf16[8,4,1792]{2,1,0:T(4,128)(2,1)} %param.19) | copy-start | bytes 344068
  79.8 4.6 %copy-start.9 = (bf16[1792]{0:T(1024)(128)(2,1)S(1)}, bf16[1792]{0:T(1024)(128)(2,1)}, u32[]{:S(2)}) copy-start(bf16[1792]{0:T(1024)(128)(2,1)} %param.22) | copy-start | bytes 10756
  79.8 31.4 %all-to-all-start.2 = ((bf16[16,32,1792]{2,1,0:T(8,128)(2,1)}), bf16[16,32,1792]{2,1,0:T(8,128)(2,1)S(1)}, u32[]{:S(2)}, u32[]{:S(2)}) async-start(bf16[16,32,1792]{2,1,0:T(8,128)(2,1)} %copy-done), calls=%async_computation.2 | async-start | bytes 3670016 | tf_op jit(solution)/shard_map/all_to_all | solution.py:404
  83.7 50.4 %collective-permute-start.18 = (bf16[1792,576]{0,1:T(8,128)(2,1)}, bf16[1792,576]{0,1:T(8,128)(2,1)}, u32[]{:S(2)}, u32[]{:S(2)}) collective-permute-start(bf16[1792,576]{0,1:T(8,128)(2,1)} %param.23), channel_id=1, source_target_pairs={{0,4},{4,0},{8,12},{12,8},{16,20},{20,16},{24,28},{28,24},{32,36},... | collective-permute-start | bytes 6193160 | tf_op jit(solution)/shard_map/ppermute | solution.py:395
  83.8 50.3 %collective-permute-start.19 = (bf16[1792,576]{0,1:T(8,128)(2,1)}, bf16[1792,576]{0,1:T(8,128)(2,1)}, u32[]{:S(2)}, u32[]{:S(2)}) collective-permute-start(bf16[1792,576]{0,1:T(8,128)(2,1)} %param.24), channel_id=1, source_target_pairs={{0,4},{4,0},{8,12},{12,8},{16,20},{20,16},{24,28},{28,24},{32,36},... | collective-permute-start | bytes 6193160 | tf_op jit(solution)/shard_map/ppermute | solution.py:395
  84.2 117.4 %collective-permute-start.26 = (bf16[576,1792]{1,0:T(8,128)(2,1)}, bf16[576,1792]{1,0:T(8,128)(2,1)}, u32[]{:S(2)}, u32[]{:S(2)}) collective-permute-start(bf16[576,1792]{1,0:T(8,128)(2,1)} %w_own.5), channel_id=1, source_target_pairs={{0,4},{4,0},{8,12},{12,8},{16,20},{20,16},{24,28},{28,24},{32,36},... | collective-permute-start | bytes 6193160 | tf_op jit(solution)/shard_map/ppermute | solution.py:395
  111.5 6.0 %collective-permute-start.6 = (bf16[32,896]{1,0:T(8,128)(2,1)S(1)}, bf16[32,896]{1,0:T(8,128)(2,1)S(1)}, u32[]{:S(2)}, u32[]{:S(2)}) collective-permute-start(bf16[32,896]{1,0:T(8,128)(2,1)S(1)} %get-tuple-element.14.a0), channel_id=1, source_target_pairs={{0,8},{4,12},{8,16},{12,20},{16,24},{20,28},{24,0},{28,4},{32,40},... | collective-permute-start | bytes 172040 | tf_op jit(solution)/shard_map/ppermute | solution.py:395
  111.5 6.8 %collective-permute-start.7 = (bf16[32,896]{1,0:T(8,128)(2,1)S(1)}, bf16[32,896]{1,0:T(8,128)(2,1)S(1)}, u32[]{:S(2)}, u32[]{:S(2)}) collective-permute-start(bf16[32,896]{1,0:T(8,128)(2,1)S(1)} %get-tuple-element.14.a0), channel_id=1, source_target_pairs={{0,16},{4,20},{8,24},{12,28},{16,0},{20,4},{24,8},{28,12},{32,48},... | collective-permute-start | bytes 172040 | tf_op jit(solution)/shard_map/ppermute | solution.py:395
  117.5 6.9 %collective-permute-start.10 = (bf16[32,1024]{1,0:T(8,128)(2,1)S(1)}, bf16[32,1024]{1,0:T(8,128)(2,1)S(1)}, u32[]{:S(2)}, u32[]{:S(2)}) collective-permute-start(bf16[32,1024]{1,0:T(8,128)(2,1)S(1)} %get-tuple-element.15.b0), channel_id=1, source_target_pairs={{0,64},{4,68},{8,72},{12,76},{16,80},{20,84},{24,88},{28,92},{32,9... | collective-permute-start | bytes 196616 | tf_op jit(solution)/shard_map/ppermute | solution.py:395
  118.3 4.5 %collective-permute-start.8 = (bf16[32,896]{1,0:T(8,128)(2,1)S(1)}, bf16[32,896]{1,0:T(8,128)(2,1)S(1)}, u32[]{:S(2)}, u32[]{:S(2)}) collective-permute-start(bf16[32,896]{1,0:T(8,128)(2,1)S(1)} %get-tuple-element.14.a0), channel_id=1, source_target_pairs={{0,24},{4,28},{8,0},{12,4},{16,8},{20,12},{24,16},{28,20},{32,56},... | collective-permute-start | bytes 172040 | tf_op jit(solution)/shard_map/ppermute | solution.py:395
  122.8 4.3 %collective-permute-start.11 = (bf16[32,1024]{1,0:T(8,128)(2,1)S(1)}, bf16[32,1024]{1,0:T(8,128)(2,1)S(1)}, u32[]{:S(2)}, u32[]{:S(2)}) collective-permute-start(bf16[32,1024]{1,0:T(8,128)(2,1)S(1)} %get-tuple-element.15.b0), channel_id=1, source_target_pairs={{0,96},{4,100},{8,104},{12,108},{16,112},{20,116},{24,120},{28,124... | collective-permute-start | bytes 196616 | tf_op jit(solution)/shard_map/ppermute | solution.py:395
  124.4 8.7 %collective-permute-start.9 = (bf16[32,1024]{1,0:T(8,128)(2,1)S(1)}, bf16[32,1024]{1,0:T(8,128)(2,1)S(1)}, u32[]{:S(2)}, u32[]{:S(2)}) collective-permute-start(bf16[32,1024]{1,0:T(8,128)(2,1)S(1)} %get-tuple-element.15.b0), channel_id=1, source_target_pairs={{0,32},{4,36},{8,40},{12,44},{16,48},{20,52},{24,56},{28,60},{32,6... | collective-permute-start | bytes 196616 | tf_op jit(solution)/shard_map/ppermute | solution.py:395
  133.2 9.8 %collective-permute-start.12 = (bf16[4,32,896]{2,1,0:T(8,128)(2,1)S(1)}, bf16[4,32,896]{2,1,0:T(8,128)(2,1)S(1)}, u32[]{:S(2)}, u32[]{:S(2)}) collective-permute-start(bf16[4,32,896]{2,1,0:T(8,128)(2,1)S(1)} %get-tuple-element.16.a0), channel_id=1, source_target_pairs={{0,32},{4,36},{8,40},{12,44},{16,48},{20,52},{24,56},{28,60},{32,6... | collective-permute-start | bytes 688136 | tf_op jit(solution)/shard_map/ppermute | solution.py:395
  133.2 12.7 %collective-permute-start.13 = (bf16[4,32,896]{2,1,0:T(8,128)(2,1)S(1)}, bf16[4,32,896]{2,1,0:T(8,128)(2,1)S(1)}, u32[]{:S(2)}, u32[]{:S(2)}) collective-permute-start(bf16[4,32,896]{2,1,0:T(8,128)(2,1)S(1)} %get-tuple-element.16.a0), channel_id=1, source_target_pairs={{0,64},{4,68},{8,72},{12,76},{16,80},{20,84},{24,88},{28,92},{32,9... | collective-permute-start | bytes 688136 | tf_op jit(solution)/shard_map/ppermute | solution.py:395
  134.1 28.3 %collective-permute-start.15 = (bf16[4,32,1024]{2,1,0:T(8,128)(2,1)S(1)}, bf16[4,32,1024]{2,1,0:T(8,128)(2,1)S(1)}, u32[]{:S(2)}, u32[]{:S(2)}) collective-permute-start(bf16[4,32,1024]{2,1,0:T(8,128)(2,1)S(1)} %get-tuple-element.17.b0), channel_id=1, source_target_pairs={{0,8},{4,12},{8,16},{12,20},{16,24},{20,28},{24,0},{28,4},{32,40},... | collective-permute-start | bytes 786440 | tf_op jit(solution)/shard_map/ppermute | solution.py:395
  134.1 28.3 %collective-permute-start.16 = (bf16[4,32,1024]{2,1,0:T(8,128)(2,1)S(1)}, bf16[4,32,1024]{2,1,0:T(8,128)(2,1)S(1)}, u32[]{:S(2)}, u32[]{:S(2)}) collective-permute-start(bf16[4,32,1024]{2,1,0:T(8,128)(2,1)S(1)} %get-tuple-element.17.b0), channel_id=1, source_target_pairs={{0,16},{4,20},{8,24},{12,28},{16,0},{20,4},{24,8},{28,12},{32,48},... | collective-permute-start | bytes 786440 | tf_op jit(solution)/shard_map/ppermute | solution.py:395
  142.9 19.4 %collective-permute-start.17 = (bf16[4,32,1024]{2,1,0:T(8,128)(2,1)S(1)}, bf16[4,32,1024]{2,1,0:T(8,128)(2,1)S(1)}, u32[]{:S(2)}, u32[]{:S(2)}) collective-permute-start(bf16[4,32,1024]{2,1,0:T(8,128)(2,1)S(1)} %get-tuple-element.17.b0), channel_id=1, source_target_pairs={{0,24},{4,28},{8,0},{12,4},{16,8},{20,12},{24,16},{28,20},{32,56},... | collective-permute-start | bytes 786440 | tf_op jit(solution)/shard_map/ppermute | solution.py:395
  145.9 16.4 %collective-permute-start.14 = (bf16[4,32,896]{2,1,0:T(8,128)(2,1)S(1)}, bf16[4,32,896]{2,1,0:T(8,128)(2,1)S(1)}, u32[]{:S(2)}, u32[]{:S(2)}) collective-permute-start(bf16[4,32,896]{2,1,0:T(8,128)(2,1)S(1)} %get-tuple-element.16.a0), channel_id=1, source_target_pairs={{0,96},{4,100},{8,104},{12,108},{16,112},{20,116},{24,120},{28,124... | collective-permute-start | bytes 688136 | tf_op jit(solution)/shard_map/ppermute | solution.py:395
  173.0 39.1 %copy-start.1 = (bf16[576,1792]{1,0:T(8,128)(2,1)S(1)}, bf16[576,1792]{1,0:T(8,128)(2,1)}, u32[]{:S(2)}) copy-start(bf16[576,1792]{1,0:T(8,128)(2,1)} %w_own.5) | copy-start | bytes 6193156
  173.0 17.6 %collective-permute-start.20 = (bf16[128,2432]{1,0:T(8,128)(2,1)S(1)}, bf16[128,2432]{1,0:T(8,128)(2,1)S(1)}, u32[]{:S(2)}, u32[]{:S(2)}) collective-permute-start(bf16[128,2432]{1,0:T(8,128)(2,1)S(1)} %get-tuple-element.19), channel_id=1, source_target_pairs={{0,1},{1,2},{2,3},{3,0},{4,5},{5,6},{6,7},{7,4},{8,9},{9,10},{10,1... | collective-permute-start | bytes 1867784 | tf_op jit(solution)/shard_map/ppermute | solution.py:399
  173.7 23.6 %collective-permute-start.21 = (bf16[128,2432]{1,0:T(8,128)(2,1)S(1)}, bf16[128,2432]{1,0:T(8,128)(2,1)S(1)}, u32[]{:S(2)}, u32[]{:S(2)}) collective-permute-start(bf16[128,2432]{1,0:T(8,128)(2,1)S(1)} %get-tuple-element.20), channel_id=1, source_target_pairs={{0,2},{1,3},{2,0},{3,1},{4,6},{5,7},{6,4},{7,5},{8,10},{9,11},{10,... | collective-permute-start | bytes 1867784 | tf_op jit(solution)/shard_map/ppermute | solution.py:399
  176.1 21.1 %collective-permute-start.22 = (bf16[128,2432]{1,0:T(8,128)(2,1)S(1)}, bf16[128,2432]{1,0:T(8,128)(2,1)S(1)}, u32[]{:S(2)}, u32[]{:S(2)}) collective-permute-start(bf16[128,2432]{1,0:T(8,128)(2,1)S(1)} %get-tuple-element.21), channel_id=1, source_target_pairs={{0,3},{1,0},{2,1},{3,2},{4,7},{5,4},{6,5},{7,6},{8,11},{9,8},{10,9... | collective-permute-start | bytes 1867784 | tf_op jit(solution)/shard_map/ppermute | solution.py:399
  198.0 11.0 %collective-permute-start.23 = (bf16[128,1152]{1,0:T(8,128)(2,1)S(1)}, bf16[128,1152]{1,0:T(8,128)(2,1)S(1)}, u32[]{:S(2)}, u32[]{:S(2)}) collective-permute-start(bf16[128,1152]{1,0:T(8,128)(2,1)S(1)} %shard_map.135.h0), channel_id=1, source_target_pairs={{0,1},{1,2},{2,3},{3,0},{4,5},{5,6},{6,7},{7,4},{8,9},{9,10},{10,1... | collective-permute-start | bytes 884744 | tf_op jit(solution)/shard_map/ppermute | solution.py:399
  198.1 14.1 %collective-permute-start.24 = (bf16[128,1152]{1,0:T(8,128)(2,1)S(1)}, bf16[128,1152]{1,0:T(8,128)(2,1)S(1)}, u32[]{:S(2)}, u32[]{:S(2)}) collective-permute-start(bf16[128,1152]{1,0:T(8,128)(2,1)S(1)} %shard_map.135.h0), channel_id=1, source_target_pairs={{0,2},{1,3},{2,0},{3,1},{4,6},{5,7},{6,4},{7,5},{8,10},{9,11},{10,... | collective-permute-start | bytes 884744 | tf_op jit(solution)/shard_map/ppermute | solution.py:399
  201.6 10.5 %collective-permute-start.25 = (bf16[128,1152]{1,0:T(8,128)(2,1)S(1)}, bf16[128,1152]{1,0:T(8,128)(2,1)S(1)}, u32[]{:S(2)}, u32[]{:S(2)}) collective-permute-start(bf16[128,1152]{1,0:T(8,128)(2,1)S(1)} %shard_map.135.h0), channel_id=1, source_target_pairs={{0,3},{1,0},{2,1},{3,2},{4,7},{5,4},{6,5},{7,6},{8,11},{9,8},{10,9... | collective-permute-start | bytes 884744 | tf_op jit(solution)/shard_map/ppermute | solution.py:399

commit v2 on v1

v2 whole, which is shorter than its diff:
```python
import functools

import jax
import jax.numpy as jnp
from jax import lax
from jax.experimental import pallas as pl
from jax.experimental.pallas import tpu as pltpu
from jax.sharding import PartitionSpec as P

D = 7168
KV = 512
KW = 576
PAGE = 64
MAXP = 32
STEPS = 4
HEADS = 128
TOKENS = PAGE * MAXP
BLOCK = 256
CHUNK = 512
KEYS = TOKENS + 128
QROWS = STEPS * HEADS
CHIPS = 16
DCOL = D // 4
FFW = 1152
GW = 2 * FFW + 128

score_scale = 0.07216878364870323
exp2_scale = score_scale * 1.4426950408889634
tiny_eps = 1e-06
neg_fill = -1e30

BF = jnp.bfloat16
F32 = jnp.float32
VMEM = pl.BlockSpec(memory_space=pltpu.VMEM)
SMEM = pl.BlockSpec(memory_space=pltpu.SMEM)
ANY = pl.BlockSpec(memory_space=pl.ANY)
HBM = pl.BlockSpec(memory_space=pltpu.HBM)


def params(mb=48):
    return pltpu.CompilerParams(vmem_limit_bytes=mb * 1024 * 1024)


def shape(dims, kind=BF):
    return jax.ShapeDtypeStruct(dims, kind)


def dot(a, b):
    return jnp.dot(a, b, preferred_element_type=F32)


def dot_t(a, b):
    return lax.dot_general(a, b, (((1,), (1,)), ((), ())), preferred_element_type=F32)


def pack_body(ids, mig, q_ref, f_ref, qo_ref, fo_ref, sems):
    one = pl.ds(mig[ids[4]], 1)
    copies = [copy_of(q_ref.at[one], qo_ref, sems.at[0]), copy_of(f_ref.at[one], fo_ref, sems.at[1])]
    start(copies)
    finished(copies)


def pack(ids, migration, queries, fresh):
    return pl.pallas_call(
        pack_body,
        out_shape=(shape((1, STEPS, KW, HEADS)), shape((1, STEPS, KW))),
        in_specs=[SMEM, SMEM, HBM, HBM],
        out_specs=(HBM, HBM),
        scratch_shapes=[pltpu.SemaphoreType.DMA((2,))],
        compiler_params=params(),
    )(ids, migration, queries, fresh)


def copy_of(source, target, sem):
    return pltpu.make_async_copy(source, target, sem)


def start(copies):
    for copy in copies:
        copy.start()


def finished(copies):
    for copy in copies:
        copy.wait()


def attend_body(moved, ids, mig, table, lengths, q_ref, f_ref, cache, *refs):
    o_ref, kbuf, q_buf, sems = refs[-4:]
    own = mig[ids[4]]
    row = own if moved else 1 - own
    length = lengths[ids[4] * 2 + row]
    per = CHUNK // PAGE
    groups = [
        [
            copy_of(cache.at[table[row, i]], kbuf.at[pl.ds(i * PAGE, PAGE), :], sems.at[i])
            for i in range(c * per, (c + 1) * per)
        ]
        for c in range(TOKENS // CHUNK)
    ]
    start(groups[0])
    start(groups[1])
    eye = lax.broadcasted_iota(jnp.int32, (HEADS, HEADS), 0)
    eye = (eye == lax.broadcasted_iota(jnp.int32, (HEADS, HEADS), 1)).astype(BF)
    for t in range(STEPS):
        q_buf[t * HEADS : (t + 1) * HEADS, :] = dot_t(eye, q_ref[0, t]).astype(BF)
    kbuf[TOKENS : TOKENS + 16, :] = f_ref[0]
    kbuf[TOKENS + 16 :, :] = jnp.zeros((KEYS - TOKENS - 16, KW), BF)
    key = lax.broadcasted_iota(jnp.int32, (8, TOKENS), 1)
    past = jnp.where(key < length, 0.0, neg_fill)[0:1]
    place = lax.broadcasted_iota(jnp.int32, (BLOCK, 128), 1)
    step = lax.broadcasted_iota(jnp.int32, (BLOCK, 128), 0) // HEADS
    blocks = []
    for n in range(QROWS // BLOCK):
        q = q_buf[n * BLOCK : (n + 1) * BLOCK, :]
        fresh = dot_t(q, kbuf[TOKENS:, :])
        scores = [jnp.where(place <= step + n * (BLOCK // HEADS), fresh, neg_fill)]
        for c, group in enumerate(groups):
            if n == 0:
                finished(group)
                if c + 2 < len(groups):
                    start(groups[c + 2])
            keys = slice(c * CHUNK, (c + 1) * CHUNK)
            scores.append(dot_t(q, kbuf[keys, :]) + past[:, keys])
        blocks.append(scores)
    for n, scores in enumerate(blocks):
        top = functools.reduce(jnp.maximum, [jnp.max(s, axis=1, keepdims=True) for s in scores])
        weights = [jnp.exp2((s - top) * exp2_scale) for s in scores]
        total = functools.reduce(jnp.add, [jnp.sum(w, axis=1, keepdims=True) for w in weights])
        weight = jnp.concatenate([w.astype(BF) for w in weights[1:] + weights[:1]], axis=1)
        out = dot(weight, kbuf[:, :KV]) / total
        for k in range(CHIPS):
            parts = [out[t * HEADS + k * 8 : t * HEADS + k * 8 + 8] for t in range(BLOCK // HEADS)]
            o_ref[k, n * 16 : n * 16 + 16, :] = jnp.concatenate(parts, axis=0).astype(BF)


def attend(moved, ids, migration, table, lengths, queries, fresh, cache, after):
    if moved:
        q_map = lambda i, ids, mig, tab, lens: (0, 0, 0, 0)
        f_map = lambda i, ids, mig, tab, lens: (0, 0, 0)
    else:
        q_map = lambda i, ids, mig, tab, lens: (1 - mig[ids[4]], 0, 0, 0)
        f_map = lambda i, ids, mig, tab, lens: (1 - mig[ids[4]], 0, 0)
    return pl.pallas_call(
        functools.partial(attend_body, moved),
        out_shape=shape((CHIPS, 32, KV)),
        grid_spec=pltpu.PrefetchScalarGridSpec(
            num_scalar_prefetch=4,
            grid=(1,),
            in_specs=[
                pl.BlockSpec((1, STEPS, KW, HEADS), q_map),
                pl.BlockSpec((1, 16, KW), f_map),
                HBM,
            ]
            + [ANY] * len(after),
            out_specs=pl.BlockSpec((CHIPS, 32, KV), lambda i, *_: (0, 0, 0)),
            scratch_shapes=[
                pltpu.VMEM((KEYS, KW), BF),
                pltpu.VMEM((QROWS, KW), BF),
                pltpu.SemaphoreType.DMA((MAXP,)),
            ],
        ),
        compiler_params=params(),
    )(ids, migration, table, lengths, queries, fresh, cache, *after)


def value_body(moved, ids, r_ref, w_own, w_sib, _, o_ref):
    core = ids[3]
    half = CHIPS // 2
    w = jnp.concatenate([w_own[h] for h in range(4)] + [w_sib[h] for h in range(4)], axis=1)
    head = lax.broadcasted_iota(jnp.int32, (256, 1024), 0) % 8
    place = lax.broadcasted_iota(jnp.int32, (256, 1024), 1) // 128
    meant = head == (place + 4 * core) % 8
    pick = lax.broadcasted_iota(jnp.int32, (32, 256), 1) // 8
    pick = (pick == lax.broadcasted_iota(jnp.int32, (32, 256), 0)).astype(BF)
    for n in range(2):
        at = (1 - n if moved else n) * half
        y = dot(r_ref[at : at + half].reshape(256, KV), w)
        y = jnp.where(meant, y, 0.0).astype(BF)
        o_ref[n * 32 : (n + 1) * 32, :] = dot(pick, y).astype(BF)


def value(moved, ids, received, w_own, w_sib, after):
    return pl.pallas_call(
        functools.partial(value_body, moved),
        out_shape=shape((64, 1024)),
        in_specs=[SMEM, VMEM, VMEM, VMEM, ANY],
        out_specs=VMEM,
        compiler_params=params(),
    )(ids, received, w_own, w_sib, after)


SPANS = ((0, 768), (768, 1792))


def column_copies(w_own, w_sib, w_ref, sems, depth):
    groups = []
    for n, (at, end) in enumerate(SPANS):
        cols = pl.ds(at, end - at)
        groups.append(
            [
                copy_of(w.at[:, cols], w_ref.at[pl.ds(i * depth, depth), cols], sems.at[n, i])
                for i, w in enumerate((w_own, w_sib))
            ]
        )
        start(groups[-1])
    return groups


def mix_body(ids, k0, k1, k2, k3, m0, m1, m2, m3, w_own, w_sib, o_ref, h_ref, p_ref, w_ref, sems):
    groups = column_copies(w_own, w_sib, w_ref, sems, 512)
    to = lax.broadcasted_iota(jnp.int32, (256, 256), 0)
    of = lax.broadcasted_iota(jnp.int32, (256, 256), 1)
    order = ((to // 4 % 4) * 64 + (to // 16) * 4 + to % 4 == of).astype(BF)
    for n, hs in enumerate(((k0, k1, k2, k3), (m0, m1, m2, m3))):
        for s, h in enumerate(hs):
            h_ref[(ids[0] - s) & 3] = h[...]
        p_ref[n * 256 : (n + 1) * 256, :] = dot(order, h_ref[...].reshape(256, 1024)).astype(BF)
    for n, (at, end) in enumerate(SPANS):
        finished(groups[n])
        out = dot(p_ref[...], w_ref[:, at:end]).astype(BF)
        o_ref[:, :16, at:end] = out[:256].reshape(CHIPS, 16, end - at)
        o_ref[:, 16:, at:end] = out[256:].reshape(CHIPS, 16, end - at)


def mix(ids, kept, moved, w_own, w_sib):
    return pl.pallas_call(
        mix_body,
        out_shape=shape((CHIPS, 32, DCOL)),
        in_specs=[SMEM] + [VMEM] * 8 + [HBM] * 2,
        out_specs=VMEM,
        scratch_shapes=[
            pltpu.VMEM((4, 64, 1024), BF),
            pltpu.VMEM((512, 1024), BF),
            pltpu.VMEM((1024, DCOL), BF),
            pltpu.SemaphoreType.DMA((2, 2)),
        ],
        compiler_params=params(),
    )(ids, *kept, *moved, w_own, w_sib)


def norm_body(r_ref, res, gain, m_ref, o_ref):
    mixed = res[...].astype(F32)
    for k in range(CHIPS):
        mixed = mixed + r_ref[k].astype(F32)
    m_ref[...] = mixed
    scaled = (mixed * gain[...].astype(F32)).astype(BF)
    square = jnp.sum(mixed * mixed, axis=1, keepdims=True)
    high = square.astype(BF).astype(F32)
    lane = lax.broadcasted_iota(jnp.int32, (32, 128), 1)
    square = jnp.where(lane < 64, high, square - high).astype(BF)
    for k in range(CHIPS):
        o_ref[k, :, :DCOL] = scaled
        o_ref[k, :, DCOL:] = square


def norm(received, residual, gain):
    return pl.pallas_call(
        norm_body,
        out_shape=(shape((32, DCOL), F32), shape((CHIPS, 32, DCOL + 128))),
        in_specs=[VMEM] * 3,
        out_specs=(VMEM,) * 2,
        compiler_params=params(),
    )(received, residual, gain)


PIECES = ((0, 0, 128), (1, 0, 64), (1, 64, 128), (2, 0, 64), (2, 64, 128), (3, 0, 64), (3, 64, 128))


def gate_up_body(ids, x_in, g_own, g_sib, u_own, u_sib, *refs):
    outs, (x_ref, w_ref, sems) = refs[: len(PIECES)], refs[len(PIECES) :]
    groups = []
    for n in range(2 * FFW // 768):
        group = []
        at, end = n * 768, (n + 1) * 768
        while at < end:
            which, row = divmod(at, 576)
            count = min(end - at, 576 - row)
            source = (g_own, g_sib, u_own, u_sib)[which].at[pl.ds(row, count), :]
            group.append(copy_of(source, w_ref.at[pl.ds(at, count), :], sems.at[n, len(group)]))
            at += count
        start(group)
        groups.append(group)
    for s in range(4):
        first = ((ids[0] + s) & 3) * 4
        for i in range(4):
            x_ref[s * 128 + i * 32 : s * 128 + i * 32 + 32, :] = x_in[first + i]
    for n in range(2 * FFW // 768):
        finished(groups[n])
        cols = slice(n * 768, (n + 1) * 768)
        out = dot_t(x_ref[:, :DCOL], w_ref[cols, :]).astype(BF)
        for piece, (s, top, end) in zip(outs, PIECES):
            piece[:, cols] = out[s * 128 + top : s * 128 + end]
    for piece, (s, top, end) in zip(outs, PIECES):
        piece[:, 2 * FFW :] = x_ref[s * 128 + top : s * 128 + end, DCOL:]


def gate_up(ids, x, weights):
    return pl.pallas_call(
        gate_up_body,
        out_shape=tuple(shape((end - top, GW)) for _, top, end in PIECES),
        in_specs=[SMEM, VMEM] + [HBM] * 4,
        out_specs=(VMEM,) * len(PIECES),
        scratch_shapes=[
            pltpu.VMEM((512, DCOL + 128), BF),
            pltpu.VMEM((2 * FFW, DCOL), BF),
            pltpu.SemaphoreType.DMA((2 * FFW // 768, 2)),
        ],
        compiler_params=params(),
    )(ids, x, *weights)


def pass_body(a, b, c, d, o_ref, p_ref):
    o_ref[...] = (a[...].astype(F32) + b[...].astype(F32)).astype(BF)
    p_ref[...] = (c[...].astype(F32) + d[...].astype(F32)).astype(BF)


def pass_on(a, b, c, d):
    return pl.pallas_call(
        pass_body,
        out_shape=(shape((64, GW)),) * 2,
        in_specs=[VMEM] * 4,
        out_specs=(VMEM,) * 2,
        compiler_params=params(),
    )(a, b, c, d)


def hidden_body(own, a_low, a_high, b_low, b_high, o_ref):
    for n, (a, b) in enumerate(((a_low, b_low), (a_high, b_high))):
        rows = slice(n * 64, n * 64 + 64)
        total = own[rows, :].astype(F32) + a[...].astype(F32) + b[...].astype(F32)
        square = jnp.sum(total[:, 2 * FFW :], axis=1, keepdims=True) * (1.0 / 64)
        scale = lax.rsqrt(square / D + tiny_eps)
        gate = total[:, :FFW] * scale
        up = total[:, FFW : 2 * FFW] * scale
        o_ref[rows, :] = (gate / (1.0 + jnp.exp(-gate)) * up).astype(BF)


def hidden_of(*parts):
    return pl.pallas_call(
        hidden_body,
        out_shape=shape((128, FFW)),
        in_specs=[VMEM] * 5,
        out_specs=VMEM,
        compiler_params=params(),
    )(*parts)


def down_body(ids, h0, h1, h2, h3, w_own, w_sib, o_ref, h_ref, w_ref, sems):
    groups = column_copies(w_own, w_sib, w_ref, sems, 576)
    for s, h in enumerate((h0, h1, h2, h3)):
        h_ref[(ids[0] - s) & 3] = h[...]
    for n, (at, end) in enumerate(SPANS):
        finished(groups[n])
        out = dot(h_ref[...].reshape(512, FFW), w_ref[:, at:end]).astype(BF)
        o_ref[:, :, at:end] = out.reshape(CHIPS, 32, end - at)


def down(ids, hs, w_own, w_sib):
    return pl.pallas_call(
        down_body,
        out_shape=shape((CHIPS, 32, DCOL)),
        in_specs=[SMEM] + [VMEM] * 4 + [HBM] * 2,
        out_specs=VMEM,
        scratch_shapes=[
            pltpu.VMEM((4, 128, FFW), BF),
            pltpu.VMEM((FFW, DCOL), BF),
            pltpu.SemaphoreType.DMA((2, 2)),
        ],
        compiler_params=params(),
    )(ids, *hs, w_own, w_sib)


def finish_body(r_ref, m_ref, o_ref):
    total = m_ref[...]
    for k in range(CHIPS):
        total = total + r_ref[k].astype(F32)
    o_ref[...] = total.astype(BF)


def finish(received, mixed):
    return pl.pallas_call(
        finish_body,
        out_shape=shape((32, DCOL)),
        in_specs=[VMEM] * 2,
        out_specs=VMEM,
        compiler_params=params(),
    )(received, mixed)


def route(dz, dx, flip):
    pairs = []
    for z in range(4):
        for x in range(4):
            for core in range(2):
                to = (z + dz) % 4 * 8 + (x + dx) % 4 * 2 + (core ^ flip)
                pairs.append((z * 8 + x * 2 + core, to))
    return pairs


def sent(block, dz=0, dx=0, flip=0):
    return lax.ppermute(block, "dp", route(dz, dx, flip))


def turned(block, s):
    return lax.ppermute(block, "grp", [(i, (i + s) % 4) for i in range(4)])


def traded(blocks):
    same_core = [list(range(core, 32, 2)) for core in range(2)]
    return lax.all_to_all(blocks, "dp", 0, 0, tiled=True, axis_index_groups=same_core)


def padded(fresh):
    return jnp.pad(fresh, ((0, 0), (0, 16 - STEPS), (0, 0)))


def on_device(
    queries,
    new_latent,
    latent_cache,
    block_table,
    lengths,
    migration,
    residual,
    value_projection_weight,
    output_proj,
    norm_gain,
    gate_proj,
    up_proj,
    down_projection_matrix,
):
    dp = lax.axis_index("dp")
    grp = lax.axis_index("grp")
    ids = jnp.stack([grp, dp // 8, dp // 2 % 4, dp % 2, dp * 4 + grp, grp, grp, grp]).astype(jnp.int32)
    queries = queries.reshape(2, STEPS, HEADS, KW).transpose(0, 1, 3, 2)
    fresh = padded(new_latent)
    gain = norm_gain.reshape(1, DCOL)
    places = lax.dynamic_slice_in_dim(migration, dp * 4, 4)
    places = places.reshape(4, 1, 1)
    rows = residual.reshape(4, 2, STEPS, DCOL)
    low, high = rows[:, 0], rows[:, 1]
    rows = jnp.stack([jnp.where(places == 0, high, low), jnp.where(places == 0, low, high)])
    rows = rows.reshape(32, DCOL)

    q_out, f_out = pack(ids, migration, queries, new_latent)
    q_in, f_in = sent(q_out, dz=2), padded(sent(f_out, dz=2))
    value_sib = sent(value_projection_weight, flip=1)
    out_sib = sent(output_proj, flip=1)
    gate, up = gate_proj.T, up_proj.T
    gate_sib = sent(gate, flip=1)
    up_sib = sent(up, flip=1)
    down_sib = sent(down_projection_matrix, flip=1)

    def attention(moved, queries, fresh, after):
        return attend(moved, ids, migration, block_table, lengths, queries, fresh, latent_cache, after)

    def project(moved, latent, after):
        return value(moved, ids, latent, value_projection_weight, value_sib, after)

    def spread(block):
        return [block] + [turned(block, s) for s in (1, 2, 3)]

    k_lat = attention(False, queries, fresh, [])
    k_lat_in = traded(k_lat)
    m_lat = attention(True, q_in, f_in, [k_lat, value_sib, out_sib, gate_sib, up_sib, down_sib])
    m_lat_in = traded(m_lat)
    k_heads = project(False, k_lat_in, m_lat)
    m_heads = project(True, m_lat_in, k_heads)
    partial = mix(ids, spread(k_heads), spread(m_heads), output_proj, out_sib)
    mixed, scaled = norm(traded(partial), rows, gain)
    own, a_low, a_high, c_low, c_high, b_low, b_high = gate_up(
        ids, traded(scaled), (gate, gate_sib, up, up_sib)
    )
    c_low, c_high = turned(c_low, 1), turned(c_high, 3)
    a_high, b_low = turned(a_high, 1), turned(b_low, 3)
    a_low, b_high = pass_on(a_low, c_low, b_high, c_high)
    a_low, b_high = turned(a_low, 1), turned(b_high, 3)
    hid = spread(hidden_of(own, a_low, a_high, b_low, b_high))
    partial = down(ids, hid, down_projection_matrix, down_sib)
    out = finish(traded(partial), mixed).reshape(2, 4, STEPS, DCOL)
    out = jnp.stack([jnp.where(places == j, out[1], out[0]) for j in range(2)], axis=1)
    return out.reshape(8, STEPS, DCOL)


def solution(mesh):
    placed = (
        P(("dp", "grp"), None, None, None),
        P(("dp", "grp"), None, None),
        P(("dp", "grp"), None, None),
        P(("dp", "grp"), None),
        P(),
        P(),
        P("dp", None, "grp"),
        P("dp", None, None),
        P("dp", "grp"),
        P("grp"),
        P("grp", "dp"),
        P("grp", "dp"),
        P("dp", "grp"),
    )
    return jax.shard_map(
        on_device, mesh=mesh, in_specs=placed, out_specs=P("dp", None, "grp"), check_vma=False
    )
```

time: 244 us -> 212 us (0.87); the launches traced: 245 us -> 211 us
  waiting for transfers between devices: 105 us -> 60 us
  blocking collectives: 25.5 us -> 55.5 us
  local copies, waits for them, and re-layouts: 20.2 us -> 7.9 us
  Pallas kernels: 44.7 us -> 38.1 us
    all_to_all x1 -> x2, blocking collectives: 25.5 us -> 55.5 us  [traded(): lax.all_to_all(blocks, 'dp', 0, 0, tiled=True, axis_index_groups=same_core)]
    ppermute x18 -> x7, waiting for transfers between devices: 27 us -> 4.44 us  [sent(): return lax.ppermute(block, 'dp', route(dz, dx, flip))]
    ppermute x9 -> x15, waiting for transfers between devices: 40.1 us -> 25.7 us  [turned(): return lax.ppermute(block, 'grp', [(i, (i + s) % 4) for i in range(4)])]
    ppermute x9 -> x15, starting transfers between devices: 14 us -> 26.2 us  [turned(): return lax.ppermute(block, 'grp', [(i, (i + s) % 4) for i in range(4)])]
    ppermute x18 -> x7, starting transfers between devices: 19 us -> 9.02 us  [sent(): return lax.ppermute(block, 'dp', route(dz, dx, flip))]
    ppermute x2 -> x0, local copies, waits for them, and re-layouts: 8.19 us -> none  [sent(): return lax.ppermute(block, 'dp', route(dz, dx, flip))]
    all_to_all x3, waiting for transfers between devices: 37.8 us -> 29.9 us  [traded(): lax.all_to_all(blocks, 'dp', 0, 0, tiled=True, axis_index_groups=same_core)]
    pallas_call x7 -> x8, Pallas kernels: 27.6 us -> 21.7 us  [the longest x1 8.11 us: gate_up(): pl.pallas_call(gate_up_body, out_shape=tuple((shape((end - top, GW)) for...]
  transfers between devices with their start and end apart: 30 -> 25, of which waited for: 14 -> 13; matrix products, arithmetic and copies ran while one was open for 7% -> 0% of each run, Pallas kernels for 13% -> 10%
where the time goes in v2:
time: 212 us; the launch traced here: 211 us
  waiting for transfers between devices  60 us (28%)
  blocking collectives  55.5 us (26%)
  starting transfers between devices  48.2 us (23%)
  Pallas kernels  38.1 us (18%)
  local copies, waits for them, and re-layouts  7.9 us (4%)
    all_to_all x2, blocking collectives, traded(): lax.all_to_all(blocks, 'dp', 0, 0, tiled=True, axis_index_groups=same_core)  55.5 us
    all_to_all x3, waiting for transfers between devices, traded(): lax.all_to_all(blocks, 'dp', 0, 0, tiled=True, axis_index_groups=same_core)  29.9 us
    ppermute x15, starting transfers between devices, turned(): return lax.ppermute(block, 'grp', [(i, (i + s) % 4) for i in range(4)])  26.2 us
    ppermute x15, waiting for transfers between devices, turned(): return lax.ppermute(block, 'grp', [(i, (i + s) % 4) for i in range(4)])  25.7 us
    pallas_call x2, Pallas kernels, attend(): pl.pallas_call(functools.partial(attend_body, moved), out_shape=shape((CH...  15.6 us
    all_to_all x3, starting transfers between devices, traded(): lax.all_to_all(blocks, 'dp', 0, 0, tiled=True, axis_index_groups=same_core)  13 us
    ppermute x7, starting transfers between devices, sent(): return lax.ppermute(block, 'dp', route(dz, dx, flip))  9.02 us
    pallas_call x1, Pallas kernels, gate_up(): pl.pallas_call(gate_up_body, out_shape=tuple((shape((end - top, GW)) for...  8.11 us
  transfers between devices with their start and end apart: 25, of which 13 were waited for; matrix products, arithmetic and copies ran while one was open for 0% of the time, Pallas kernels for 10%

profile of v2, /device:TPU:0, one launch (start us, length us, event | category | flops | bytes accessed | tf_op | source)
XLA Modules:
  0.0 210.5 jit_solution(13715839503706554199)
XLA Ops:
  0.0 0.5 collective-permute-start.5
  0.5 0.5 collective-permute-start.3
  1.0 0.1 stack.36.ids
  1.1 1.3 copy-done.2
  2.4 0.7 copy-done.7
  3.1 0.7 copy-done.8
  3.7 1.4 shard_map.128
  5.1 4.0 %collective-permute-start.2 = (bf16[1,4,576]{2,1,0:T(4,128)(2,1)S(1)}, bf16[1,4,576]{2,1,0:T(4,128)(2,1)S(1)}, u32[]{:S(2)}, u32[]{:S(2)}) collective-permute-start(bf16[1,4,576]{2,1,0:T(4,128)(2,1)S(1)} %get-tuple-element.19), channel_id=1, source_target_pairs={{0,64},{4,68},{8,72},{12,76},{16,80},{20,84},{24,88},{28,92},{32,9... | collective-permute-start | bytes 13832 | tf_op jit(solution)/shard_map/ppermute | solution.py:402
  9.2 1.6 collective-permute-done.2
  10.8 2.8 %collective-permute-done.refs_1_.w_sib = bf16[4,512,128]{2,1,0:T(8,128)(2,1)S(1)} collective-permute-done((bf16[4,512,128]{2,1,0:T(8,128)(2,1)}, bf16[4,512,128]{2,1,0:T(8,128)(2,1)S(1)}, u32[]{:S(2)}, u32[]{:S(2)}) %collective-permute-start) | collective-permute-done | bytes 524320 | tf_op jit(solution)/shard_map/ppermute | solution.py:402
  13.6 4.0 %collective-permute-start.1 = (bf16[1,4,576,128]{3,2,1,0:T(8,128)(2,1)}, bf16[1,4,576,128]{3,2,1,0:T(8,128)(2,1)}, u32[]{:S(2)}, u32[]{:S(2)}) collective-permute-start(bf16[1,4,576,128]{3,2,1,0:T(8,128)(2,1)} %get-tuple-element.18), channel_id=1, source_target_pairs={{0,64},{4,68},{8,72},{12,76},{16,80},{20,84},{24,88},{28,92},{32,9... | collective-permute-start | bytes 1769480 | tf_op jit(solution)/shard_map/ppermute | solution.py:402
  17.6 0.0 copy-start.9
  17.6 0.6 copy-done.9
  18.2 0.7 copy-done.11
  18.9 0.7 copy-done.13
  19.6 7.2 %shard_map.127.refs_0_ = bf16[16,32,512]{2,1,0:T(8,128)(2,1)} custom-call(s32[8]{0:T(128)S(1)} %stack.36.ids, s32[128]{0:T(128)S(1)} %copy-done.9, s32[2,32]{1,0:T(2,128)S(1)} %copy-done.11, s32[256]{0:T(256)S(1)} %copy-done.13, bf16[2,4,576,128]{3,2,1,0:T(8,128)(2,1)S(1)} %bitcast.27, bf16[2,16,576]{2,1,0:T(8,128)(2,1)S(1)} %pad.8.f_ref, ...), custom_call_target="tpu_custom_call" | custom-call | tf_op jit(solution)/shard_map/pallas_call | solution.py:144
  26.8 4.9 %all-to-all-start = ((bf16[16,32,512]{2,1,0:T(8,128)(2,1)}), bf16[16,32,512]{2,1,0:T(8,128)(2,1)S(1)}, u32[]{:S(2)}, u32[]{:S(2)}) async-start(bf16[16,32,512]{2,1,0:T(8,128)(2,1)} %shard_map.127.refs_0_), calls=%async_computation | async-start | bytes 1048576 | tf_op jit(solution)/shard_map/all_to_all | solution.py:411
  31.8 8.4 %shard_map.129._ = bf16[16,32,512]{2,1,0:T(8,128)(2,1)} custom-call(s32[8]{0:T(128)S(1)} %stack.36.ids, s32[128]{0:T(128)S(1)} %copy-done.10, s32[2,32]{1,0:T(2,128)S(1)} %copy-done.12, s32[256]{0:T(256)S(1)} %copy-done.14, bf16[1,4,576,128]{3,2,1,0:T(8,128)(2,1)} %collective-permute-done.1.q_ref, bf16[1,16,576]{2,1,0:T(8,128)(2,1)S(1)} %pad.9.f_ref, ...), custom_call_target="tpu_custom_call" | custom-call | tf_op jit(solution)/shard_map/pallas_call | solution.py:144
  40.2 3.1 %all-to-all-done.r_ref = bf16[16,32,512]{2,1,0:T(8,128)(2,1)S(1)} async-done(((bf16[16,32,512]{2,1,0:T(8,128)(2,1)}), bf16[16,32,512]{2,1,0:T(8,128)(2,1)S(1)}, u32[]{:S(2)}, u32[]{:S(2)}) %all-to-all-start) | async-done | bytes 524320 | tf_op jit(solution)/shard_map/all_to_all | solution.py:411
  43.3 4.3 %all-to-all-start.1 = ((bf16[16,32,512]{2,1,0:T(8,128)(2,1)}), bf16[16,32,512]{2,1,0:T(8,128)(2,1)S(1)}, u32[]{:S(2)}, u32[]{:S(2)}) async-start(bf16[16,32,512]{2,1,0:T(8,128)(2,1)} %shard_map.129._), calls=%async_computation.1 | async-start | bytes 1048576 | tf_op jit(solution)/shard_map/all_to_all | solution.py:411
  47.6 0.0 copy-start.3
  47.6 1.0 copy-done.3
  48.6 1.6 shard_map.130._.k0
  50.2 1.6 collective-permute-start.7
  51.8 2.9 %collective-permute-start.8 = (bf16[64,1024]{1,0:T(8,128)(2,1)S(1)}, bf16[64,1024]{1,0:T(8,128)(2,1)S(1)}, u32[]{:S(2)}, u32[]{:S(2)}) collective-permute-start(bf16[64,1024]{1,0:T(8,128)(2,1)S(1)} %shard_map.130._.k0), channel_id=1, source_target_pairs={{0,2},{1,3},{2,0},{3,1},{4,6},{5,7},{6,4},{7,5},{8,10},{9,11},{10,... | collective-permute-start | bytes 393224 | tf_op jit(solution)/shard_map/ppermute | solution.py:406
  54.7 1.3 collective-permute-start.9
  56.1 2.5 %all-to-all-done.1.r_ref = bf16[16,32,512]{2,1,0:T(8,128)(2,1)S(1)} async-done(((bf16[16,32,512]{2,1,0:T(8,128)(2,1)}), bf16[16,32,512]{2,1,0:T(8,128)(2,1)S(1)}, u32[]{:S(2)}, u32[]{:S(2)}) %all-to-all-start.1) | async-done | bytes 524320 | tf_op jit(solution)/shard_map/all_to_all | solution.py:411
  58.6 1.6 shard_map.131.m0
  60.1 1.6 collective-permute-start.10
  61.8 2.9 %collective-permute-start.11 = (bf16[64,1024]{1,0:T(8,128)(2,1)S(1)}, bf16[64,1024]{1,0:T(8,128)(2,1)S(1)}, u32[]{:S(2)}, u32[]{:S(2)}) collective-permute-start(bf16[64,1024]{1,0:T(8,128)(2,1)S(1)} %shard_map.131.m0), channel_id=1, source_target_pairs={{0,2},{1,3},{2,0},{3,1},{4,6},{5,7},{6,4},{7,5},{8,10},{9,11},{10,... | collective-permute-start | bytes 393224 | tf_op jit(solution)/shard_map/ppermute | solution.py:406
  64.7 1.3 collective-permute-start.12
  66.0 1.6 collective-permute-done.10.m1
  67.6 1.4 collective-permute-done.11.m2
  69.0 0.6 collective-permute-done.12.m3
  69.6 4.0 %shard_map.132 = bf16[16,32,1792]{2,1,0:T(8,128)(2,1)S(1)} custom-call(s32[8]{0:T(128)S(1)} %stack.36.ids, bf16[64,1024]{1,0:T(8,128)(2,1)S(1)} %shard_map.130._.k0, bf16[64,1024]{1,0:T(8,128)(2,1)S(1)} %collective-permute-done.7.k1, bf16[64,1024]{1,0:T(8,128)(2,1)S(1)} %collective-permute-done.8.k2, bf16[64,1024]{1,0:T(8,128)(2,1)S(1)} %collective-permute-done.9.k3, ...), custom_call_target="tpu_custom_call" | custom-call | tf_op jit(solution)/shard_map/pallas_call | solution.py:227
  73.7 1.3 copy-done.1
  75.0 3.8 %all-to-all-start.2 = ((bf16[16,32,1792]{2,1,0:T(8,128)(2,1)}), bf16[16,32,1792]{2,1,0:T(8,128)(2,1)S(1)}, u32[]{:S(2)}, u32[]{:S(2)}) async-start(bf16[16,32,1792]{2,1,0:T(8,128)(2,1)} %copy-done.1), calls=%async_computation.2 | async-start | bytes 3670016 | tf_op jit(solution)/shard_map/all_to_all | solution.py:411
  78.8 0.1 broadcast_compare_fusion
  78.9 0.1 broadcast_select_fusion.2
  79.0 0.1 pad_maximum_fusion
  79.2 24.3 %all-to-all-done.2.r_ref = bf16[16,32,1792]{2,1,0:T(8,128)(2,1)S(1)} async-done(((bf16[16,32,1792]{2,1,0:T(8,128)(2,1)}), bf16[16,32,1792]{2,1,0:T(8,128)(2,1)S(1)}, u32[]{:S(2)}, u32[]{:S(2)}) %all-to-all-start.2) | async-done | bytes 1835040 | tf_op jit(solution)/shard_map/all_to_all | solution.py:411
  103.5 0.4 shard_map.133
  103.9 29.2 %all_to_all.25.x_in = bf16[16,32,1920]{2,1,0:T(8,128)(2,1)S(1)} all-to-all(bf16[16,32,1920]{2,1,0:T(8,128)(2,1)S(1)} %get-tuple-element.20), channel_id=1, replica_groups={{0,8,16,24,32,40,48,56,64,72,80,88,96,104,112,120},{4,12,20,28,36,44,52..., dimensions={0} | all-to-all | bytes 3932160 | tf_op jit(solution)/shard_map/all_to_all | solution.py:411
  133.0 8.1 %shard_map.134 = (bf16[128,2432]{1,0:T(8,128)(2,1)S(1)}, bf16[64,2432]{1,0:T(8,128)(2,1)S(1)}, bf16[64,2432]{1,0:T(8,128)(2,1)S(1)}, bf16[64,2432]{1,0:T(8,128)(...) custom-call(s32[8]{0:T(128)S(1)} %stack.36.ids, ...), custom_call_target="tpu_custom_call" | custom-call | tf_op jit(solution)/shard_map/pallas_call | solution.py:299
  141.2 1.2 collective-permute-start.13
  142.4 2.1 collective-permute-start.14
  144.5 3.2 %collective-permute-start.17 = (bf16[64,2432]{1,0:T(8,128)(2,1)S(1)}, bf16[64,2432]{1,0:T(8,128)(2,1)S(1)}, u32[]{:S(2)}, u32[]{:S(2)}) collective-permute-start(bf16[64,2432]{1,0:T(8,128)(2,1)S(1)} %get-tuple-element.28), channel_id=1, source_target_pairs={{0,3},{1,0},{2,1},{3,2},{4,7},{5,4},{6,5},{7,6},{8,11},{9,8},{10,9... | collective-permute-start | bytes 933896 | tf_op jit(solution)/shard_map/ppermute | solution.py:406
  147.7 5.0 %collective-permute-done.13.b = bf16[64,2432]{1,0:T(8,128)(2,1)S(1)} collective-permute-done((bf16[64,2432]{1,0:T(8,128)(2,1)S(1)}, bf16[64,2432]{1,0:T(8,128)(2,1)S(1)}, u32[]{:S(2)}, u32[]{:S(2)}) %collective-permute-start.13) | collective-permute-done | bytes 311328 | tf_op jit(solution)/shard_map/ppermute | solution.py:406
  152.8 0.1 shard_map.135
  152.9 1.0 collective-permute-start.15
  153.9 2.4 %collective-permute-start.18 = (bf16[64,2432]{1,0:T(8,128)(2,1)S(1)}, bf16[64,2432]{1,0:T(8,128)(2,1)S(1)}, u32[]{:S(2)}, u32[]{:S(2)}) collective-permute-start(bf16[64,2432]{1,0:T(8,128)(2,1)S(1)} %get-tuple-element.29), channel_id=1, source_target_pairs={{0,3},{1,0},{2,1},{3,2},{4,7},{5,4},{6,5},{7,6},{8,11},{9,8},{10,9... | collective-permute-start | bytes 933896 | tf_op jit(solution)/shard_map/ppermute | solution.py:406
  156.3 3.1 %collective-permute-done.16.a_high = bf16[64,2432]{1,0:T(8,128)(2,1)S(1)} collective-permute-done((bf16[64,2432]{1,0:T(8,128)(2,1)S(1)}, bf16[64,2432]{1,0:T(8,128)(2,1)S(1)}, u32[]{:S(2)}, u32[]{:S(2)}) %collective-permute-start.16) | collective-permute-done | bytes 311328 | tf_op jit(solution)/shard_map/ppermute | solution.py:406
  159.4 3.8 %collective-permute-done.15.a_low = bf16[64,2432]{1,0:T(8,128)(2,1)S(1)} collective-permute-done((bf16[64,2432]{1,0:T(8,128)(2,1)S(1)}, bf16[64,2432]{1,0:T(8,128)(2,1)S(1)}, u32[]{:S(2)}, u32[]{:S(2)}) %collective-permute-start.15) | collective-permute-done | bytes 311328 | tf_op jit(solution)/shard_map/ppermute | solution.py:406
  163.2 0.5 shard_map.136.h0
  163.8 0.8 collective-permute-start.19
  164.5 3.7 %collective-permute-start.20 = (bf16[128,1152]{1,0:T(8,128)(2,1)S(1)}, bf16[128,1152]{1,0:T(8,128)(2,1)S(1)}, u32[]{:S(2)}, u32[]{:S(2)}) collective-permute-start(bf16[128,1152]{1,0:T(8,128)(2,1)S(1)} %shard_map.136.h0), channel_id=1, source_target_pairs={{0,2},{1,3},{2,0},{3,1},{4,6},{5,7},{6,4},{7,5},{8,10},{9,11},{10,... | collective-permute-start | bytes 884744 | tf_op jit(solution)/shard_map/ppermute | solution.py:406
  168.3 6.7 %collective-permute-done.19.h1 = bf16[128,1152]{1,0:T(8,128)(2,1)S(1)} collective-permute-done((bf16[128,1152]{1,0:T(8,128)(2,1)S(1)}, bf16[128,1152]{1,0:T(8,128)(2,1)S(1)}, u32[]{:S(2)}, u32[]{:S(2)}) %collective-permute-start.19) | collective-permute-done | bytes 294944 | tf_op jit(solution)/shard_map/ppermute | solution.py:406
  174.9 3.5 %collective-permute-done.20.h2 = bf16[128,1152]{1,0:T(8,128)(2,1)S(1)} collective-permute-done((bf16[128,1152]{1,0:T(8,128)(2,1)S(1)}, bf16[128,1152]{1,0:T(8,128)(2,1)S(1)}, u32[]{:S(2)}, u32[]{:S(2)}) %collective-permute-start.20) | collective-permute-done | bytes 294944 | tf_op jit(solution)/shard_map/ppermute | solution.py:406
  178.4 4.5 %shard_map.137 = bf16[16,32,1792]{2,1,0:T(8,128)(2,1)S(1)} custom-call(s32[8]{0:T(128)S(1)} %stack.36.ids, bf16[128,1152]{1,0:T(8,128)(2,1)S(1)} %shard_map.136.h0, bf16[128,1152]{1,0:T(8,128)(2,1)S(1)} %collective-permute-done.19.h1, bf16[128,1152]{1,0:T(8,128)(2,1)S(1)} %collective-permute-done.20.h2, bf16[128,1152]{1,0:T(8,128)(2,1)S(1)} %collective-permute-done.21.h3, ...), custom_call_target="tpu_custom_call" | custom-call | tf_op jit(solution)/shard_map/pallas_call | solution.py:360
  182.9 26.3 %all_to_all.26.r_ref = bf16[16,32,1792]{2,1,0:T(8,128)(2,1)S(1)} all-to-all(bf16[16,32,1792]{2,1,0:T(8,128)(2,1)S(1)} %shard_map.137), channel_id=1, replica_groups={{0,8,16,24,32,40,48,56,64,72,80,88,96,104,112,120},{4,12,20,28,36,44,52..., dimensions={0} | all-to-all | bytes 3670016 | tf_op jit(solution)/shard_map/all_to_all | solution.py:411
  209.3 0.2 shard_map.138
  209.6 0.1 broadcast_select_fusion.3
  209.7 0.1 pad_maximum_fusion.1
  209.8 0.7 copy.16
  (48 shorter events, 0.2 us)
Async XLA Ops:
  0.0 31.8 %collective-permute-start.4 = (bf16[576,1792]{1,0:T(8,128)(2,1)}, bf16[576,1792]{1,0:T(8,128)(2,1)S(1)}, u32[]{:S(2)}, u32[]{:S(2)}) collective-permute-start(bf16[576,1792]{1,0:T(8,128)(2,1)} %bitcast.28), channel_id=1, source_target_pairs={{0,4},{4,0},{8,12},{12,8},{16,20},{20,16},{24,28},{28,24},{32,36},... | collective-permute-start | bytes 6193160 | tf_op jit(solution)/shard_map/ppermute | solution.py:402
  0.0 31.8 %collective-permute-start.5 = (bf16[576,1792]{1,0:T(8,128)(2,1)}, bf16[576,1792]{1,0:T(8,128)(2,1)}, u32[]{:S(2)}, u32[]{:S(2)}) collective-permute-start(bf16[576,1792]{1,0:T(8,128)(2,1)} %bitcast.30), channel_id=1, source_target_pairs={{0,4},{4,0},{8,12},{12,8},{16,20},{20,16},{24,28},{28,24},{32,36},... | collective-permute-start | bytes 6193160 | tf_op jit(solution)/shard_map/ppermute | solution.py:402
  0.5 31.3 %collective-permute-start.6 = (bf16[576,1792]{1,0:T(8,128)(2,1)}, bf16[576,1792]{1,0:T(8,128)(2,1)}, u32[]{:S(2)}, u32[]{:S(2)}) collective-permute-start(bf16[576,1792]{1,0:T(8,128)(2,1)} %w_own.7), channel_id=1, source_target_pairs={{0,4},{4,0},{8,12},{12,8},{16,20},{20,16},{24,28},{28,24},{32,36},... | collective-permute-start | bytes 6193160 | tf_op jit(solution)/shard_map/ppermute | solution.py:402
  0.5 31.2 %collective-permute-start.3 = (bf16[512,1792]{1,0:T(8,128)(2,1)}, bf16[512,1792]{1,0:T(8,128)(2,1)}, u32[]{:S(2)}, u32[]{:S(2)}) collective-permute-start(bf16[512,1792]{1,0:T(8,128)(2,1)} %w_own.6), channel_id=1, source_target_pairs={{0,4},{4,0},{8,12},{12,8},{16,20},{20,16},{24,28},{28,24},{32,36},... | collective-permute-start | bytes 5505032 | tf_op jit(solution)/shard_map/ppermute | solution.py:402
  1.1 1.3 copy-start.2
  2.4 0.7 copy-start.7
  3.1 0.7 copy-start.8
  5.1 5.6 %collective-permute-start.2 = (bf16[1,4,576]{2,1,0:T(4,128)(2,1)S(1)}, bf16[1,4,576]{2,1,0:T(4,128)(2,1)S(1)}, u32[]{:S(2)}, u32[]{:S(2)}) collective-permute-start(bf16[1,4,576]{2,1,0:T(4,128)(2,1)S(1)} %get-tuple-element.19), channel_id=1, source_target_pairs={{0,64},{4,68},{8,72},{12,76},{16,80},{20,84},{24,88},{28,92},{32,9... | collective-permute-start | bytes 13832 | tf_op jit(solution)/shard_map/ppermute | solution.py:402
  10.8 2.8 %collective-permute-start = (bf16[4,512,128]{2,1,0:T(8,128)(2,1)}, bf16[4,512,128]{2,1,0:T(8,128)(2,1)S(1)}, u32[]{:S(2)}, u32[]{:S(2)}) collective-permute-start(bf16[4,512,128]{2,1,0:T(8,128)(2,1)} %w_own.5), channel_id=1, source_target_pairs={{0,4},{4,0},{8,12},{12,8},{16,20},{20,16},{24,28},{28,24},{32,36},... | collective-permute-start | bytes 1572872 | tf_op jit(solution)/shard_map/ppermute | solution.py:402
  13.6 18.1 %collective-permute-start.1 = (bf16[1,4,576,128]{3,2,1,0:T(8,128)(2,1)}, bf16[1,4,576,128]{3,2,1,0:T(8,128)(2,1)}, u32[]{:S(2)}, u32[]{:S(2)}) collective-permute-start(bf16[1,4,576,128]{3,2,1,0:T(8,128)(2,1)} %get-tuple-element.18), channel_id=1, source_target_pairs={{0,64},{4,68},{8,72},{12,76},{16,80},{20,84},{24,88},{28,92},{32,9... | collective-permute-start | bytes 1769480 | tf_op jit(solution)/shard_map/ppermute | solution.py:402
  17.6 0.7 copy-start.9
  18.2 0.7 copy-start.11
  18.9 0.7 copy-start.13
  19.6 12.2 %copy-start.10 = (s32[128]{0:T(128)S(1)}, s32[128]{0:T(128)}, u32[]{:S(2)}) copy-start(s32[128]{0:T(128)} %mig.5) | copy-start | bytes 1540
  19.6 12.2 %copy-start.12 = (s32[2,32]{1,0:T(2,128)S(1)}, s32[2,32]{1,0:T(2,128)}, u32[]{:S(2)}) copy-start(s32[2,32]{1,0:T(2,128)} %table.3) | copy-start | bytes 772
  19.6 12.2 %copy-start.14 = (s32[256]{0:T(256)S(1)}, s32[256]{0:T(256)}, u32[]{:S(2)}) copy-start(s32[256]{0:T(256)} %lengths.3) | copy-start | bytes 3076
  26.8 16.4 %all-to-all-start = ((bf16[16,32,512]{2,1,0:T(8,128)(2,1)}), bf16[16,32,512]{2,1,0:T(8,128)(2,1)S(1)}, u32[]{:S(2)}, u32[]{:S(2)}) async-start(bf16[16,32,512]{2,1,0:T(8,128)(2,1)} %shard_map.127.refs_0_), calls=%async_computation | async-start | bytes 1048576 | tf_op jit(solution)/shard_map/all_to_all | solution.py:411
  31.8 8.4 %copy-start = (bf16[576,1792]{1,0:T(8,128)(2,1)}, bf16[576,1792]{1,0:T(8,128)(2,1)S(1)}, u32[]{:S(2)}) copy-start(bf16[576,1792]{1,0:T(8,128)(2,1)S(1)} %collective-permute-done.4.refs_3_.g_sib) | copy-start | bytes 6193156
  43.3 15.3 %copy-start.4 = (bf16[4,512,128]{2,1,0:T(8,128)(2,1)S(1)}, bf16[4,512,128]{2,1,0:T(8,128)(2,1)}, u32[]{:S(2)}) copy-start(bf16[4,512,128]{2,1,0:T(8,128)(2,1)} %w_own.5) | copy-start | bytes 1572868
  43.3 15.3 %all-to-all-start.1 = ((bf16[16,32,512]{2,1,0:T(8,128)(2,1)}), bf16[16,32,512]{2,1,0:T(8,128)(2,1)S(1)}, u32[]{:S(2)}, u32[]{:S(2)}) async-start(bf16[16,32,512]{2,1,0:T(8,128)(2,1)} %shard_map.129._), calls=%async_computation.1 | async-start | bytes 1048576 | tf_op jit(solution)/shard_map/all_to_all | solution.py:411
  47.6 1.0 copy-start.3
  50.2 14.5 %collective-permute-start.7 = (bf16[64,1024]{1,0:T(8,128)(2,1)S(1)}, bf16[64,1024]{1,0:T(8,128)(2,1)S(1)}, u32[]{:S(2)}, u32[]{:S(2)}) collective-permute-start(bf16[64,1024]{1,0:T(8,128)(2,1)S(1)} %shard_map.130._.k0), channel_id=1, source_target_pairs={{0,1},{1,2},{2,3},{3,0},{4,5},{5,6},{6,7},{7,4},{8,9},{9,10},{10,1... | collective-permute-start | bytes 393224 | tf_op jit(solution)/shard_map/ppermute | solution.py:406
  51.8 14.2 %collective-permute-start.8 = (bf16[64,1024]{1,0:T(8,128)(2,1)S(1)}, bf16[64,1024]{1,0:T(8,128)(2,1)S(1)}, u32[]{:S(2)}, u32[]{:S(2)}) collective-permute-start(bf16[64,1024]{1,0:T(8,128)(2,1)S(1)} %shard_map.130._.k0), channel_id=1, source_target_pairs={{0,2},{1,3},{2,0},{3,1},{4,6},{5,7},{6,4},{7,5},{8,10},{9,11},{10,... | collective-permute-start | bytes 393224 | tf_op jit(solution)/shard_map/ppermute | solution.py:406
  54.7 11.3 %collective-permute-start.9 = (bf16[64,1024]{1,0:T(8,128)(2,1)S(1)}, bf16[64,1024]{1,0:T(8,128)(2,1)S(1)}, u32[]{:S(2)}, u32[]{:S(2)}) collective-permute-start(bf16[64,1024]{1,0:T(8,128)(2,1)S(1)} %shard_map.130._.k0), channel_id=1, source_target_pairs={{0,3},{1,0},{2,1},{3,2},{4,7},{5,4},{6,5},{7,6},{8,11},{9,8},{10,9... | collective-permute-start | bytes 393224 | tf_op jit(solution)/shard_map/ppermute | solution.py:406
  58.6 11.1 %copy-start.6 = (bf16[512,1792]{1,0:T(8,128)(2,1)S(1)}, bf16[512,1792]{1,0:T(8,128)(2,1)}, u32[]{:S(2)}) copy-start(bf16[512,1792]{1,0:T(8,128)(2,1)} %w_own.6) | copy-start | bytes 5505028
  60.1 7.5 %collective-permute-start.10 = (bf16[64,1024]{1,0:T(8,128)(2,1)S(1)}, bf16[64,1024]{1,0:T(8,128)(2,1)S(1)}, u32[]{:S(2)}, u32[]{:S(2)}) collective-permute-start(bf16[64,1024]{1,0:T(8,128)(2,1)S(1)} %shard_map.131.m0), channel_id=1, source_target_pairs={{0,1},{1,2},{2,3},{3,0},{4,5},{5,6},{6,7},{7,4},{8,9},{9,10},{10,1... | collective-permute-start | bytes 393224 | tf_op jit(solution)/shard_map/ppermute | solution.py:406
  61.8 7.3 %collective-permute-start.11 = (bf16[64,1024]{1,0:T(8,128)(2,1)S(1)}, bf16[64,1024]{1,0:T(8,128)(2,1)S(1)}, u32[]{:S(2)}, u32[]{:S(2)}) collective-permute-start(bf16[64,1024]{1,0:T(8,128)(2,1)S(1)} %shard_map.131.m0), channel_id=1, source_target_pairs={{0,2},{1,3},{2,0},{3,1},{4,6},{5,7},{6,4},{7,5},{8,10},{9,11},{10,... | collective-permute-start | bytes 393224 | tf_op jit(solution)/shard_map/ppermute | solution.py:406
  64.7 5.0 %collective-permute-start.12 = (bf16[64,1024]{1,0:T(8,128)(2,1)S(1)}, bf16[64,1024]{1,0:T(8,128)(2,1)S(1)}, u32[]{:S(2)}, u32[]{:S(2)}) collective-permute-start(bf16[64,1024]{1,0:T(8,128)(2,1)S(1)} %shard_map.131.m0), channel_id=1, source_target_pairs={{0,3},{1,0},{2,1},{3,2},{4,7},{5,4},{6,5},{7,6},{8,11},{9,8},{10,9... | collective-permute-start | bytes 393224 | tf_op jit(solution)/shard_map/ppermute | solution.py:406
  73.7 1.3 copy-start.1
  75.0 3.9 %copy-start.15 = (bf16[8,4,1792]{2,1,0:T(4,128)(2,1)S(1)}, bf16[8,4,1792]{2,1,0:T(4,128)(2,1)}, u32[]{:S(2)}) copy-start(bf16[8,4,1792]{2,1,0:T(4,128)(2,1)} %param.19) | copy-start | bytes 344068
  75.0 4.2 %copy-start.16 = (bf16[1792]{0:T(1024)(128)(2,1)S(1)}, bf16[1792]{0:T(1024)(128)(2,1)}, u32[]{:S(2)}) copy-start(bf16[1792]{0:T(1024)(128)(2,1)} %param.22) | copy-start | bytes 10756
  75.0 28.5 %all-to-all-start.2 = ((bf16[16,32,1792]{2,1,0:T(8,128)(2,1)}), bf16[16,32,1792]{2,1,0:T(8,128)(2,1)S(1)}, u32[]{:S(2)}, u32[]{:S(2)}) async-start(bf16[16,32,1792]{2,1,0:T(8,128)(2,1)} %copy-done.1), calls=%async_computation.2 | async-start | bytes 3670016 | tf_op jit(solution)/shard_map/all_to_all | solution.py:411
  141.2 37.3 %copy-start.5 = (bf16[576,1792]{1,0:T(8,128)(2,1)S(1)}, bf16[576,1792]{1,0:T(8,128)(2,1)}, u32[]{:S(2)}) copy-start(bf16[576,1792]{1,0:T(8,128)(2,1)} %w_own.7) | copy-start | bytes 6193156
  141.2 11.6 %collective-permute-start.13 = (bf16[64,2432]{1,0:T(8,128)(2,1)S(1)}, bf16[64,2432]{1,0:T(8,128)(2,1)S(1)}, u32[]{:S(2)}, u32[]{:S(2)}) collective-permute-start(bf16[64,2432]{1,0:T(8,128)(2,1)S(1)} %get-tuple-element.23), channel_id=1, source_target_pairs={{0,1},{1,2},{2,3},{3,0},{4,5},{5,6},{6,7},{7,4},{8,9},{9,10},{10,1... | collective-permute-start | bytes 933896 | tf_op jit(solution)/shard_map/ppermute | solution.py:406
  142.4 10.3 %collective-permute-start.14 = (bf16[64,2432]{1,0:T(8,128)(2,1)S(1)}, bf16[64,2432]{1,0:T(8,128)(2,1)S(1)}, u32[]{:S(2)}, u32[]{:S(2)}) collective-permute-start(bf16[64,2432]{1,0:T(8,128)(2,1)S(1)} %get-tuple-element.25), channel_id=1, source_target_pairs={{0,3},{1,0},{2,1},{3,2},{4,7},{5,4},{6,5},{7,6},{8,11},{9,8},{10,9... | collective-permute-start | bytes 933896 | tf_op jit(solution)/shard_map/ppermute | solution.py:406
  144.5 14.9 %collective-permute-start.16 = (bf16[64,2432]{1,0:T(8,128)(2,1)S(1)}, bf16[64,2432]{1,0:T(8,128)(2,1)S(1)}, u32[]{:S(2)}, u32[]{:S(2)}) collective-permute-start(bf16[64,2432]{1,0:T(8,128)(2,1)S(1)} %get-tuple-element.27), channel_id=1, source_target_pairs={{0,1},{1,2},{2,3},{3,0},{4,5},{5,6},{6,7},{7,4},{8,9},{9,10},{10,1... | collective-permute-start | bytes 933896 | tf_op jit(solution)/shard_map/ppermute | solution.py:406
  144.5 14.9 %collective-permute-start.17 = (bf16[64,2432]{1,0:T(8,128)(2,1)S(1)}, bf16[64,2432]{1,0:T(8,128)(2,1)S(1)}, u32[]{:S(2)}, u32[]{:S(2)}) collective-permute-start(bf16[64,2432]{1,0:T(8,128)(2,1)S(1)} %get-tuple-element.28), channel_id=1, source_target_pairs={{0,3},{1,0},{2,1},{3,2},{4,7},{5,4},{6,5},{7,6},{8,11},{9,8},{10,9... | collective-permute-start | bytes 933896 | tf_op jit(solution)/shard_map/ppermute | solution.py:406
  152.9 10.3 %collective-permute-start.15 = (bf16[64,2432]{1,0:T(8,128)(2,1)S(1)}, bf16[64,2432]{1,0:T(8,128)(2,1)S(1)}, u32[]{:S(2)}, u32[]{:S(2)}) collective-permute-start(bf16[64,2432]{1,0:T(8,128)(2,1)S(1)} %get-tuple-element.26), channel_id=1, source_target_pairs={{0,1},{1,2},{2,3},{3,0},{4,5},{5,6},{6,7},{7,4},{8,9},{9,10},{10,1... | collective-permute-start | bytes 933896 | tf_op jit(solution)/shard_map/ppermute | solution.py:406
  153.9 9.3 %collective-permute-start.18 = (bf16[64,2432]{1,0:T(8,128)(2,1)S(1)}, bf16[64,2432]{1,0:T(8,128)(2,1)S(1)}, u32[]{:S(2)}, u32[]{:S(2)}) collective-permute-start(bf16[64,2432]{1,0:T(8,128)(2,1)S(1)} %get-tuple-element.29), channel_id=1, source_target_pairs={{0,3},{1,0},{2,1},{3,2},{4,7},{5,4},{6,5},{7,6},{8,11},{9,8},{10,9... | collective-permute-start | bytes 933896 | tf_op jit(solution)/shard_map/ppermute | solution.py:406
  163.8 11.2 %collective-permute-start.19 = (bf16[128,1152]{1,0:T(8,128)(2,1)S(1)}, bf16[128,1152]{1,0:T(8,128)(2,1)S(1)}, u32[]{:S(2)}, u32[]{:S(2)}) collective-permute-start(bf16[128,1152]{1,0:T(8,128)(2,1)S(1)} %shard_map.136.h0), channel_id=1, source_target_pairs={{0,1},{1,2},{2,3},{3,0},{4,5},{5,6},{6,7},{7,4},{8,9},{9,10},{10,1... | collective-permute-start | bytes 884744 | tf_op jit(solution)/shard_map/ppermute | solution.py:406
  164.5 13.9 %collective-permute-start.20 = (bf16[128,1152]{1,0:T(8,128)(2,1)S(1)}, bf16[128,1152]{1,0:T(8,128)(2,1)S(1)}, u32[]{:S(2)}, u32[]{:S(2)}) collective-permute-start(bf16[128,1152]{1,0:T(8,128)(2,1)S(1)} %shard_map.136.h0), channel_id=1, source_target_pairs={{0,2},{1,3},{2,0},{3,1},{4,6},{5,7},{6,4},{7,5},{8,10},{9,11},{10,... | collective-permute-start | bytes 884744 | tf_op jit(solution)/shard_map/ppermute | solution.py:406
  168.3 10.2 %collective-permute-start.21 = (bf16[128,1152]{1,0:T(8,128)(2,1)S(1)}, bf16[128,1152]{1,0:T(8,128)(2,1)S(1)}, u32[]{:S(2)}, u32[]{:S(2)}) collective-permute-start(bf16[128,1152]{1,0:T(8,128)(2,1)S(1)} %shard_map.136.h0), channel_id=1, source_target_pairs={{0,3},{1,0},{2,1},{3,2},{4,7},{5,4},{6,5},{7,6},{8,11},{9,8},{10,9... | collective-permute-start | bytes 884744 | tf_op jit(solution)/shard_map/ppermute | solution.py:406

commit v3 on v2

--- a/solution.py
+++ b/solution.py
@@ -19,6 +19,8 @@
 CHUNK = 512
 KEYS = TOKENS + 128
 QROWS = STEPS * HEADS
+TROWS = STEPS * KW
+FROWS = 5 * 16
 CHIPS = 16
 DCOL = D // 4
 FFW = 1152
@@ -53,20 +55,24 @@
     return lax.dot_general(a, b, (((1,), (1,)), ((), ())), preferred_element_type=F32)
 
 
-def pack_body(ids, mig, q_ref, f_ref, qo_ref, fo_ref, sems):
-    one = pl.ds(mig[ids[4]], 1)
-    copies = [copy_of(q_ref.at[one], qo_ref, sems.at[0]), copy_of(f_ref.at[one], fo_ref, sems.at[1])]
-    start(copies)
-    finished(copies)
+def pack_body(ids, mig, q_ref, f_ref, o_ref):
+    o_ref[0, :TROWS, :] = q_ref[0]
+    o_ref[0, TROWS:, :] = f_ref[0]
 
 
 def pack(ids, migration, queries, fresh):
     return pl.pallas_call(
         pack_body,
-        out_shape=(shape((1, STEPS, KW, HEADS)), shape((1, STEPS, KW))),
-        in_specs=[SMEM, SMEM, HBM, HBM],
-        out_specs=(HBM, HBM),
-        scratch_shapes=[pltpu.SemaphoreType.DMA((2,))],
+        out_shape=shape((1, TROWS + FROWS, HEADS)),
+        grid_spec=pltpu.PrefetchScalarGridSpec(
+            num_scalar_prefetch=2,
+            grid=(1,),
+            in_specs=[
+                pl.BlockSpec((1, TROWS, HEADS), lambda i, ids, mig: (mig[ids[4]], 0, 0)),
+                pl.BlockSpec((1, FROWS, HEADS), lambda i, ids, mig: (mig[ids[4]], 0, 0)),
+            ],
+            out_specs=pl.BlockSpec((1, TROWS + FROWS, HEADS), lambda i, ids, mig: (0, 0, 0)),
+        ),
         compiler_params=params(),
     )(ids, migration, queries, fresh)
 
@@ -86,9 +92,15 @@
 
 
 def attend_body(moved, ids, mig, table, lengths, q_ref, f_ref, cache, *refs):
-    o_ref, kbuf, q_buf, sems = refs[-4:]
+    o_ref, kbuf, t_buf, f_buf, q_buf, sems, i_sems = refs[-7:]
     own = mig[ids[4]]
     row = own if moved else 1 - own
+    slot = 0 if moved else row
+    inputs = [
+        copy_of(q_ref.at[slot, pl.ds(0, TROWS), :], t_buf, i_sems.at[0]),
+        copy_of(f_ref.at[slot, pl.ds(TROWS if moved else 0, FROWS), :], f_buf, i_sems.at[1]),
+    ]
+    start(inputs)
     length = lengths[ids[4] * 2 + row]
     per = CHUNK // PAGE
     groups = [
@@ -102,10 +114,13 @@
     start(groups[1])
     eye = lax.broadcasted_iota(jnp.int32, (HEADS, HEADS), 0)
     eye = (eye == lax.broadcasted_iota(jnp.int32, (HEADS, HEADS), 1)).astype(BF)
+    kbuf[TOKENS + 16 :, :] = jnp.zeros((KEYS - TOKENS - 16, KW), BF)
+    finished(inputs)
+    for i in range(5):
+        width = min(HEADS, KW - i * HEADS)
+        kbuf[TOKENS : TOKENS + 16, i * HEADS : i * HEADS + width] = f_buf[i * 16 : i * 16 + 16, :width]
     for t in range(STEPS):
-        q_buf[t * HEADS : (t + 1) * HEADS, :] = dot_t(eye, q_ref[0, t]).astype(BF)
-    kbuf[TOKENS : TOKENS + 16, :] = f_ref[0]
-    kbuf[TOKENS + 16 :, :] = jnp.zeros((KEYS - TOKENS - 16, KW), BF)
+        q_buf[t * HEADS : (t + 1) * HEADS, :] = dot_t(eye, t_buf[t * KW : (t + 1) * KW, :]).astype(BF)
     key = lax.broadcasted_iota(jnp.int32, (8, TOKENS), 1)
     past = jnp.where(key < length, 0.0, neg_fill)[0:1]
     place = lax.broadcasted_iota(jnp.int32, (BLOCK, 128), 1)
@@ -135,36 +150,25 @@
 
 
 def attend(moved, ids, migration, table, lengths, queries, fresh, cache, after):
-    if moved:
-        q_map = lambda i, ids, mig, tab, lens: (0, 0, 0, 0)
-        f_map = lambda i, ids, mig, tab, lens: (0, 0, 0)
-    else:
-        q_map = lambda i, ids, mig, tab, lens: (1 - mig[ids[4]], 0, 0, 0)
-        f_map = lambda i, ids, mig, tab, lens: (1 - mig[ids[4]], 0, 0)
     return pl.pallas_call(
         functools.partial(attend_body, moved),
         out_shape=shape((CHIPS, 32, KV)),
-        grid_spec=pltpu.PrefetchScalarGridSpec(
-            num_scalar_prefetch=4,
-            grid=(1,),
-            in_specs=[
-                pl.BlockSpec((1, STEPS, KW, HEADS), q_map),
-                pl.BlockSpec((1, 16, KW), f_map),
-                HBM,
-            ]
-            + [ANY] * len(after),
-            out_specs=pl.BlockSpec((CHIPS, 32, KV), lambda i, *_: (0, 0, 0)),
-            scratch_shapes=[
-                pltpu.VMEM((KEYS, KW), BF),
-                pltpu.VMEM((QROWS, KW), BF),
-                pltpu.SemaphoreType.DMA((MAXP,)),
-            ],
-        ),
+        in_specs=[SMEM] * 4 + [HBM] * 3 + [ANY] * len(after),
+        out_specs=VMEM,
+        scratch_shapes=[
+            pltpu.VMEM((KEYS, KW), BF),
+            pltpu.VMEM((TROWS, HEADS), BF),
+            pltpu.VMEM((FROWS, HEADS), BF),
+            pltpu.VMEM((QROWS, KW), BF),
+            pltpu.SemaphoreType.DMA((MAXP,)),
+            pltpu.SemaphoreType.DMA((2,)),
+        ],
         compiler_params=params(),
     )(ids, migration, table, lengths, queries, fresh, cache, *after)
 
 
-def value_body(moved, ids, r_ref, w_own, w_sib, _, o_ref):
+def value_body(moved, ids, r_ref, w_own, w_sib, *refs):
+    o_ref = refs[-1]
     core = ids[3]
     half = CHIPS // 2
     w = jnp.concatenate([w_own[h] for h in range(4)] + [w_sib[h] for h in range(4)], axis=1)
@@ -184,10 +188,10 @@
     return pl.pallas_call(
         functools.partial(value_body, moved),
         out_shape=shape((64, 1024)),
-        in_specs=[SMEM, VMEM, VMEM, VMEM, ANY],
+        in_specs=[SMEM, VMEM, VMEM, VMEM] + [ANY] * len(after),
         out_specs=VMEM,
         compiler_params=params(),
-    )(ids, received, w_own, w_sib, after)
+    )(ids, received, w_own, w_sib, *after)
 
 
 SPANS = ((0, 768), (768, 1792))
@@ -411,8 +415,9 @@
     return lax.all_to_all(blocks, "dp", 0, 0, tiled=True, axis_index_groups=same_core)
 
 
-def padded(fresh):
-    return jnp.pad(fresh, ((0, 0), (0, 16 - STEPS), (0, 0)))
+def blocked(fresh):
+    fresh = jnp.pad(fresh, ((0, 0), (0, 16 - STEPS), (0, 5 * HEADS - KW)))
+    return fresh.reshape(2, 16, 5, HEADS).transpose(0, 2, 1, 3).reshape(2, FROWS, HEADS)
 
 
 def on_device(
@@ -433,8 +438,8 @@
     dp = lax.axis_index("dp")
     grp = lax.axis_index("grp")
     ids = jnp.stack([grp, dp // 8, dp // 2 % 4, dp % 2, dp * 4 + grp, grp, grp, grp]).astype(jnp.int32)
-    queries = queries.reshape(2, STEPS, HEADS, KW).transpose(0, 1, 3, 2)
-    fresh = padded(new_latent)
+    queries = queries.transpose(0, 1, 3, 2).reshape(2, TROWS, HEADS)
+    fresh = blocked(new_latent)
     gain = norm_gain.reshape(1, DCOL)
     places = lax.dynamic_slice_in_dim(migration, dp * 4, 4)
     places = places.reshape(4, 1, 1)
@@ -443,8 +448,7 @@
     rows = jnp.stack([jnp.where(places == 0, high, low), jnp.where(places == 0, low, high)])
     rows = rows.reshape(32, DCOL)
 
-    q_out, f_out = pack(ids, migration, queries, new_latent)
-    q_in, f_in = sent(q_out, dz=2), padded(sent(f_out, dz=2))
+    arrived = sent(pack(ids, migration, queries, fresh), dz=2)
     value_sib = sent(value_projection_weight, flip=1)
     out_sib = sent(output_proj, flip=1)
     gate, up = gate_proj.T, up_proj.T
@@ -463,10 +467,10 @@
 
     k_lat = attention(False, queries, fresh, [])
     k_lat_in = traded(k_lat)
-    m_lat = attention(True, q_in, f_in, [k_lat, value_sib, out_sib, gate_sib, up_sib, down_sib])
+    m_lat = attention(True, arrived, arrived, [k_lat])
     m_lat_in = traded(m_lat)
-    k_heads = project(False, k_lat_in, m_lat)
-    m_heads = project(True, m_lat_in, k_heads)
+    k_heads = project(False, k_lat_in, [m_lat])
+    m_heads = project(True, m_lat_in, [k_heads])
     partial = mix(ids, spread(k_heads), spread(m_heads), output_proj, out_sib)
     mixed, scaled = norm(traded(partial), rows, gain)
     own, a_low, a_high, c_low, c_high, b_low, b_high = gate_up(

time: 212 us -> 202 us (0.953)
  blocking collectives: 55.5 us -> 21.5 us
  waiting for transfers between devices: 60 us -> 85.6 us
    all_to_all x2 -> x1, blocking collectives: 55.5 us -> 21.5 us  [traded(): lax.all_to_all(blocks, 'dp', 0, 0, tiled=True, axis_index_groups=same_core)]
    all_to_all x3 -> x4, waiting for transfers between devices: 29.9 us -> 53.6 us  [traded(): lax.all_to_all(blocks, 'dp', 0, 0, tiled=True, axis_index_groups=same_core)]
    all_to_all x3 -> x4, starting transfers between devices: 13 us -> 21.8 us  [traded(): lax.all_to_all(blocks, 'dp', 0, 0, tiled=True, axis_index_groups=same_core)]
    ppermute x15, waiting for transfers between devices: 25.7 us -> 30 us  [turned(): return lax.ppermute(block, 'grp', [(i, (i + s) % 4) for i in range(4)])]
    ppermute x7 -> x6, starting transfers between devices: 9.02 us -> 4.83 us  [sent(): return lax.ppermute(block, 'dp', route(dz, dx, flip))]
    ppermute x15, starting transfers between devices: 26.2 us -> 23.7 us  [turned(): return lax.ppermute(block, 'grp', [(i, (i + s) % 4) for i in range(4)])]
    unnamed x34 -> x24, local copies, waits for them, and re-layouts: 7.02 us -> 4.59 us
    ppermute x7 -> x6, waiting for transfers between devices: 4.44 us -> 2.08 us  [sent(): return lax.ppermute(block, 'dp', route(dz, dx, flip))]
  transfers between devices with their start and end apart: 25 -> 25, of which waited for: 13 -> 13; matrix products, arithmetic and copies ran while one was open for 0% -> 1% of each run, Pallas kernels for 10% -> 14%
where the time goes in v3:
time: 202 us; the launch traced here: 201 us
  waiting for transfers between devices  85.6 us (42%)
  starting transfers between devices  50.3 us (25%)
  Pallas kernels  36.3 us (18%)
  blocking collectives  21.5 us (11%)
  local copies, waits for them, and re-layouts  6.26 us (3%)
    all_to_all x4, waiting for transfers between devices, traded(): lax.all_to_all(blocks, 'dp', 0, 0, tiled=True, axis_index_groups=same_core)  53.6 us
    ppermute x15, waiting for transfers between devices, turned(): return lax.ppermute(block, 'grp', [(i, (i + s) % 4) for i in range(4)])  30 us
    ppermute x15, starting transfers between devices, turned(): return lax.ppermute(block, 'grp', [(i, (i + s) % 4) for i in range(4)])  23.7 us
    all_to_all x4, starting transfers between devices, traded(): lax.all_to_all(blocks, 'dp', 0, 0, tiled=True, axis_index_groups=same_core)  21.8 us
    all_to_all x1, blocking collectives, traded(): lax.all_to_all(blocks, 'dp', 0, 0, tiled=True, axis_index_groups=same_core)  21.5 us
    pallas_call x2, Pallas kernels, attend(): pl.pallas_call(functools.partial(attend_body, moved), out_shape=shape((CH...  14.6 us
    pallas_call x1, Pallas kernels, gate_up(): pl.pallas_call(gate_up_body, out_shape=tuple((shape((end - top, GW)) for...  8.11 us
    ppermute x6, starting transfers between devices, sent(): return lax.ppermute(block, 'dp', route(dz, dx, flip))  4.83 us
  transfers between devices with their start and end apart: 25, of which 13 were waited for; matrix products, arithmetic and copies ran while one was open for 1% of the time, Pallas kernels for 14%

profile of v3, /device:TPU:0, one launch (start us, length us, event | category | flops | bytes accessed | tf_op | source)
XLA Modules:
  0.0 200.8 jit_solution(15043009988408025206)
XLA Ops:
  0.0 0.7 pad.4
  0.7 0.1 reshape.100
  0.9 0.1 stack.36.ids
  0.9 1.3 copy-done.1
  2.2 0.7 copy-done.6
  2.9 0.6 shard_map.128
  3.5 0.0 copy-start.2
  3.5 0.0 copy-start.7
  3.5 4.1 %collective-permute-start.1 = (bf16[1,2384,128]{2,1,0:T(8,128)(2,1)S(1)}, bf16[1,2384,128]{2,1,0:T(8,128)(2,1)S(1)}, u32[]{:S(2)}, u32[]{:S(2)}) collective-permute-start(bf16[1,2384,128]{2,1,0:T(8,128)(2,1)S(1)} %shard_map.128), channel_id=1, source_target_pairs={{0,64},{4,68},{8,72},{12,76},{16,80},{20,84},{24,88},{28,92},{32,9... | collective-permute-start | bytes 1830920 | tf_op jit(solution)/shard_map/ppermute | solution.py:406
  7.6 7.3 %shard_map.127.refs_0_ = bf16[16,32,512]{2,1,0:T(8,128)(2,1)} custom-call(s32[8]{0:T(128)S(1)} %stack.36.ids, s32[128]{0:T(128)S(1)} %copy-done.6, s32[2,32]{1,0:T(2,128)S(1)} %copy-done.8, s32[256]{0:T(256)S(1)} %copy-done.9, bf16[2,2304,128]{2,1,0:T(8,128)(2,1)S(1)} %bitcast.31, bf16[2,80,128]{2,1,0:T(8,128)(2,1)S(1)} %bitcast.33, bf16[64,64,576]{2,1,0:T(8,128)(2,1)} %cache.3), custom_call_target="tpu_custom_call" | custom-call | tf_op jit(solution)/shard_map/pallas_call | solution.py:153
  14.9 4.9 %all-to-all-start = ((bf16[16,32,512]{2,1,0:T(8,128)(2,1)}), bf16[16,32,512]{2,1,0:T(8,128)(2,1)S(1)}, u32[]{:S(2)}, u32[]{:S(2)}) async-start(bf16[16,32,512]{2,1,0:T(8,128)(2,1)} %shard_map.127.refs_0_), calls=%async_computation | async-start | bytes 1048576 | tf_op jit(solution)/shard_map/all_to_all | solution.py:415
  19.8 0.1 collective-permute-start
  19.9 2.1 %collective-permute-done.1.q_ref.f_ref = bf16[1,2384,128]{2,1,0:T(8,128)(2,1)S(1)} collective-permute-done((bf16[1,2384,128]{2,1,0:T(8,128)(2,1)S(1)}, bf16[1,2384,128]{2,1,0:T(8,128)(2,1)S(1)}, u32[]{:S(2)}, u32[]{:S(2)}) %collective-permute-start.1) | collective-permute-done | bytes 610336 | tf_op jit(solution)/shard_map/ppermute | solution.py:406
  21.9 7.3 %shard_map.129.refs_0_ = bf16[16,32,512]{2,1,0:T(8,128)(2,1)} custom-call(s32[8]{0:T(128)S(1)} %stack.36.ids, s32[128]{0:T(128)S(1)} %copy-done.7, s32[2,32]{1,0:T(2,128)S(1)} %copy-done.8, s32[256]{0:T(256)S(1)} %copy-done.9, bf16[1,2384,128]{2,1,0:T(8,128)(2,1)S(1)} %collective-permute-done.1.q_ref.f_ref, ...), custom_call_target="tpu_custom_call" | custom-call | tf_op jit(solution)/shard_map/pallas_call | solution.py:153
  29.3 2.4 %all-to-all-done.r_ref = bf16[16,32,512]{2,1,0:T(8,128)(2,1)S(1)} async-done(((bf16[16,32,512]{2,1,0:T(8,128)(2,1)}), bf16[16,32,512]{2,1,0:T(8,128)(2,1)S(1)}, u32[]{:S(2)}, u32[]{:S(2)}) %all-to-all-start) | async-done | bytes 524320 | tf_op jit(solution)/shard_map/all_to_all | solution.py:415
  31.7 9.4 %all-to-all-start.1 = ((bf16[16,32,512]{2,1,0:T(8,128)(2,1)}), bf16[16,32,512]{2,1,0:T(8,128)(2,1)S(1)}, u32[]{:S(2)}, u32[]{:S(2)}) async-start(bf16[16,32,512]{2,1,0:T(8,128)(2,1)} %shard_map.129.refs_0_), calls=%async_computation.1 | async-start | bytes 1048576 | tf_op jit(solution)/shard_map/all_to_all | solution.py:415
  41.1 1.6 shard_map.130.refs_0_.k0
  42.6 3.1 %collective-permute-start.4 = (bf16[64,1024]{1,0:T(8,128)(2,1)S(1)}, bf16[64,1024]{1,0:T(8,128)(2,1)S(1)}, u32[]{:S(2)}, u32[]{:S(2)}) collective-permute-start(bf16[64,1024]{1,0:T(8,128)(2,1)S(1)} %shard_map.130.refs_0_.k0), channel_id=1, source_target_pairs={{0,3},{1,0},{2,1},{3,2},{4,7},{5,4},{6,5},{7,6},{8,11},{9,8},{10,9... | collective-permute-start | bytes 393224 | tf_op jit(solution)/shard_map/ppermute | solution.py:410
  45.7 0.6 collective-permute-start.3
  46.3 1.0 collective-permute-start.2
  47.3 3.9 %all-to-all-done.1.r_ref = bf16[16,32,512]{2,1,0:T(8,128)(2,1)S(1)} async-done(((bf16[16,32,512]{2,1,0:T(8,128)(2,1)}), bf16[16,32,512]{2,1,0:T(8,128)(2,1)S(1)}, u32[]{:S(2)}, u32[]{:S(2)}) %all-to-all-start.1) | async-done | bytes 524320 | tf_op jit(solution)/shard_map/all_to_all | solution.py:415
  51.2 1.6 shard_map.131.m0
  52.7 3.2 %collective-permute-start.7 = (bf16[64,1024]{1,0:T(8,128)(2,1)S(1)}, bf16[64,1024]{1,0:T(8,128)(2,1)S(1)}, u32[]{:S(2)}, u32[]{:S(2)}) collective-permute-start(bf16[64,1024]{1,0:T(8,128)(2,1)S(1)} %shard_map.131.m0), channel_id=1, source_target_pairs={{0,3},{1,0},{2,1},{3,2},{4,7},{5,4},{6,5},{7,6},{8,11},{9,8},{10,9... | collective-permute-start | bytes 393224 | tf_op jit(solution)/shard_map/ppermute | solution.py:410
  56.0 0.6 collective-permute-start.6
  56.6 1.0 collective-permute-start.5
  57.6 2.3 %collective-permute-done.7.m3 = bf16[64,1024]{1,0:T(8,128)(2,1)S(1)} collective-permute-done((bf16[64,1024]{1,0:T(8,128)(2,1)S(1)}, bf16[64,1024]{1,0:T(8,128)(2,1)S(1)}, u32[]{:S(2)}, u32[]{:S(2)}) %collective-permute-start.7) | collective-permute-done | bytes 131104 | tf_op jit(solution)/shard_map/ppermute | solution.py:410
  59.9 2.7 %collective-permute-done.6.m2 = bf16[64,1024]{1,0:T(8,128)(2,1)S(1)} collective-permute-done((bf16[64,1024]{1,0:T(8,128)(2,1)S(1)}, bf16[64,1024]{1,0:T(8,128)(2,1)S(1)}, u32[]{:S(2)}, u32[]{:S(2)}) %collective-permute-start.6) | collective-permute-done | bytes 131104 | tf_op jit(solution)/shard_map/ppermute | solution.py:410
  62.6 1.3 collective-permute-done.5.m1
  63.9 4.0 %shard_map.132 = bf16[16,32,1792]{2,1,0:T(8,128)(2,1)S(1)} custom-call(s32[8]{0:T(128)S(1)} %stack.36.ids, bf16[64,1024]{1,0:T(8,128)(2,1)S(1)} %shard_map.130.refs_0_.k0, bf16[64,1024]{1,0:T(8,128)(2,1)S(1)} %collective-permute-done.2.k1, bf16[64,1024]{1,0:T(8,128)(2,1)S(1)} %collective-permute-done.3.k2, bf16[64,1024]{1,0:T(8,128)(2,1)S(1)} %collective-permute-done.4.k3, ...), custom_call_target="tpu_custom_call" | custom-call | tf_op jit(solution)/shard_map/pallas_call | solution.py:231
  67.9 1.3 copy-done
  69.2 3.8 %all-to-all-start.2 = ((bf16[16,32,1792]{2,1,0:T(8,128)(2,1)}), bf16[16,32,1792]{2,1,0:T(8,128)(2,1)S(1)}, u32[]{:S(2)}, u32[]{:S(2)}) async-start(bf16[16,32,1792]{2,1,0:T(8,128)(2,1)} %copy-done), calls=%async_computation.2 | async-start | bytes 3670016 | tf_op jit(solution)/shard_map/all_to_all | solution.py:415
  73.0 0.1 collective-permute-start.9
  73.1 0.5 collective-permute-start.10
  73.6 0.1 broadcast_compare_fusion
  73.7 0.1 broadcast_select_fusion.2
  73.8 0.1 pad_maximum_fusion
  73.9 22.8 %all-to-all-done.2.r_ref = bf16[16,32,1792]{2,1,0:T(8,128)(2,1)S(1)} async-done(((bf16[16,32,1792]{2,1,0:T(8,128)(2,1)}), bf16[16,32,1792]{2,1,0:T(8,128)(2,1)S(1)}, u32[]{:S(2)}, u32[]{:S(2)}) %all-to-all-start.2) | async-done | bytes 1835040 | tf_op jit(solution)/shard_map/all_to_all | solution.py:415
  96.8 0.4 shard_map.133
  97.2 1.4 copy-done.4
  98.5 3.7 %all-to-all-start.3 = ((bf16[16,32,1920]{2,1,0:T(8,128)(2,1)}), bf16[16,32,1920]{2,1,0:T(8,128)(2,1)S(1)}, u32[]{:S(2)}, u32[]{:S(2)}) async-start(bf16[16,32,1920]{2,1,0:T(8,128)(2,1)} %copy-done.4), calls=%async_computation.3 | async-start | bytes 3932160 | tf_op jit(solution)/shard_map/all_to_all | solution.py:415
  102.3 0.1 collective-permute-start.20
  102.4 24.5 %all-to-all-done.3.x_in = bf16[16,32,1920]{2,1,0:T(8,128)(2,1)S(1)} async-done(((bf16[16,32,1920]{2,1,0:T(8,128)(2,1)}), bf16[16,32,1920]{2,1,0:T(8,128)(2,1)S(1)}, u32[]{:S(2)}, u32[]{:S(2)}) %all-to-all-start.3) | async-done | bytes 1966112 | tf_op jit(solution)/shard_map/all_to_all | solution.py:415
  126.9 8.1 %shard_map.134 = (bf16[128,2432]{1,0:T(8,128)(2,1)S(1)}, bf16[64,2432]{1,0:T(8,128)(2,1)S(1)}, bf16[64,2432]{1,0:T(8,128)(2,1)S(1)}, bf16[64,2432]{1,0:T(8,128)(...) custom-call(s32[8]{0:T(128)S(1)} %stack.36.ids, ...), custom_call_target="tpu_custom_call" | custom-call | tf_op jit(solution)/shard_map/pallas_call | solution.py:303
  135.0 0.0 copy-start.3
  135.0 0.1 collective-permute-start.11
  135.1 3.2 %collective-permute-start.12 = (bf16[64,2432]{1,0:T(8,128)(2,1)S(1)}, bf16[64,2432]{1,0:T(8,128)(2,1)S(1)}, u32[]{:S(2)}, u32[]{:S(2)}) collective-permute-start(bf16[64,2432]{1,0:T(8,128)(2,1)S(1)} %get-tuple-element.21), channel_id=1, source_target_pairs={{0,3},{1,0},{2,1},{3,2},{4,7},{5,4},{6,5},{7,6},{8,11},{9,8},{10,9... | collective-permute-start | bytes 933896 | tf_op jit(solution)/shard_map/ppermute | solution.py:410
  138.3 3.2 %collective-permute-start.15 = (bf16[64,2432]{1,0:T(8,128)(2,1)S(1)}, bf16[64,2432]{1,0:T(8,128)(2,1)S(1)}, u32[]{:S(2)}, u32[]{:S(2)}) collective-permute-start(bf16[64,2432]{1,0:T(8,128)(2,1)S(1)} %get-tuple-element.24), channel_id=1, source_target_pairs={{0,3},{1,0},{2,1},{3,2},{4,7},{5,4},{6,5},{7,6},{8,11},{9,8},{10,9... | collective-permute-start | bytes 933896 | tf_op jit(solution)/shard_map/ppermute | solution.py:410
  141.5 4.1 %collective-permute-done.11.b = bf16[64,2432]{1,0:T(8,128)(2,1)S(1)} collective-permute-done((bf16[64,2432]{1,0:T(8,128)(2,1)S(1)}, bf16[64,2432]{1,0:T(8,128)(2,1)S(1)}, u32[]{:S(2)}, u32[]{:S(2)}) %collective-permute-start.11) | collective-permute-done | bytes 311328 | tf_op jit(solution)/shard_map/ppermute | solution.py:410
  145.7 0.1 shard_map.135
  145.8 0.1 collective-permute-start.13
  145.9 3.2 %collective-permute-start.16 = (bf16[64,2432]{1,0:T(8,128)(2,1)S(1)}, bf16[64,2432]{1,0:T(8,128)(2,1)S(1)}, u32[]{:S(2)}, u32[]{:S(2)}) collective-permute-start(bf16[64,2432]{1,0:T(8,128)(2,1)S(1)} %get-tuple-element.25), channel_id=1, source_target_pairs={{0,3},{1,0},{2,1},{3,2},{4,7},{5,4},{6,5},{7,6},{8,11},{9,8},{10,9... | collective-permute-start | bytes 933896 | tf_op jit(solution)/shard_map/ppermute | solution.py:410
  149.1 9.4 %collective-permute-done.13.a_low = bf16[64,2432]{1,0:T(8,128)(2,1)S(1)} collective-permute-done((bf16[64,2432]{1,0:T(8,128)(2,1)S(1)}, bf16[64,2432]{1,0:T(8,128)(2,1)S(1)}, u32[]{:S(2)}, u32[]{:S(2)}) %collective-permute-start.13) | collective-permute-done | bytes 311328 | tf_op jit(solution)/shard_map/ppermute | solution.py:410
  158.5 0.5 shard_map.136.h0
  159.1 3.4 %collective-permute-start.19 = (bf16[128,1152]{1,0:T(8,128)(2,1)S(1)}, bf16[128,1152]{1,0:T(8,128)(2,1)S(1)}, u32[]{:S(2)}, u32[]{:S(2)}) collective-permute-start(bf16[128,1152]{1,0:T(8,128)(2,1)S(1)} %shard_map.136.h0), channel_id=1, source_target_pairs={{0,3},{1,0},{2,1},{3,2},{4,7},{5,4},{6,5},{7,6},{8,11},{9,8},{10,9... | collective-permute-start | bytes 884744 | tf_op jit(solution)/shard_map/ppermute | solution.py:410
  162.5 0.9 collective-permute-start.17
  163.4 6.4 %collective-permute-done.19.h3 = bf16[128,1152]{1,0:T(8,128)(2,1)S(1)} collective-permute-done((bf16[128,1152]{1,0:T(8,128)(2,1)S(1)}, bf16[128,1152]{1,0:T(8,128)(2,1)S(1)}, u32[]{:S(2)}, u32[]{:S(2)}) %collective-permute-start.19) | collective-permute-done | bytes 294944 | tf_op jit(solution)/shard_map/ppermute | solution.py:410
  169.9 0.9 collective-permute-done.18.h2
  170.8 2.8 %collective-permute-done.17.h1 = bf16[128,1152]{1,0:T(8,128)(2,1)S(1)} collective-permute-done((bf16[128,1152]{1,0:T(8,128)(2,1)S(1)}, bf16[128,1152]{1,0:T(8,128)(2,1)S(1)}, u32[]{:S(2)}, u32[]{:S(2)}) %collective-permute-start.17) | collective-permute-done | bytes 294944 | tf_op jit(solution)/shard_map/ppermute | solution.py:410
  173.6 4.5 %shard_map.137 = bf16[16,32,1792]{2,1,0:T(8,128)(2,1)S(1)} custom-call(s32[8]{0:T(128)S(1)} %stack.36.ids, bf16[128,1152]{1,0:T(8,128)(2,1)S(1)} %shard_map.136.h0, bf16[128,1152]{1,0:T(8,128)(2,1)S(1)} %collective-permute-done.17.h1, bf16[128,1152]{1,0:T(8,128)(2,1)S(1)} %collective-permute-done.18.h2, bf16[128,1152]{1,0:T(8,128)(2,1)S(1)} %collective-permute-done.19.h3, ...), custom_call_target="tpu_custom_call" | custom-call | tf_op jit(solution)/shard_map/pallas_call | solution.py:364
  178.1 21.5 %all_to_all.25.r_ref = bf16[16,32,1792]{2,1,0:T(8,128)(2,1)S(1)} all-to-all(bf16[16,32,1792]{2,1,0:T(8,128)(2,1)S(1)} %shard_map.137), channel_id=1, replica_groups={{0,8,16,24,32,40,48,56,64,72,80,88,96,104,112,120},{4,12,20,28,36,44,52..., dimensions={0} | all-to-all | bytes 3670016 | tf_op jit(solution)/shard_map/all_to_all | solution.py:415
  199.6 0.3 shard_map.138
  199.9 0.1 broadcast_select_fusion.3
  200.1 0.1 pad_maximum_fusion.1
  200.2 0.7 copy.21
  (38 shorter events, 0.2 us)
Async XLA Ops:
  0.0 7.6 %copy-start.9 = (s32[256]{0:T(256)S(1)}, s32[256]{0:T(256)}, u32[]{:S(2)}) copy-start(s32[256]{0:T(256)} %lengths.3) | copy-start | bytes 3076
  0.0 7.6 %copy-start.8 = (s32[2,32]{1,0:T(2,128)S(1)}, s32[2,32]{1,0:T(2,128)}, u32[]{:S(2)}) copy-start(s32[2,32]{1,0:T(2,128)} %table.3) | copy-start | bytes 772
  0.0 63.9 %collective-permute-start.8 = (bf16[512,1792]{1,0:T(8,128)(2,1)}, bf16[512,1792]{1,0:T(8,128)(2,1)}, u32[]{:S(2)}, u32[]{:S(2)}) collective-permute-start(bf16[512,1792]{1,0:T(8,128)(2,1)} %w_own.6), channel_id=1, source_target_pairs={{0,4},{4,0},{8,12},{12,8},{16,20},{20,16},{24,28},{28,24},{32,36},... | collective-permute-start | bytes 5505032 | tf_op jit(solution)/shard_map/ppermute | solution.py:406
  0.9 1.3 copy-start.1
  2.2 0.7 copy-start.6
  3.5 16.3 %copy-start.2 = (bf16[4,512,128]{2,1,0:T(8,128)(2,1)S(1)}, bf16[4,512,128]{2,1,0:T(8,128)(2,1)}, u32[]{:S(2)}) copy-start(bf16[4,512,128]{2,1,0:T(8,128)(2,1)} %w_own.5) | copy-start | bytes 1572868
  3.5 18.5 %copy-start.7 = (s32[128]{0:T(128)S(1)}, s32[128]{0:T(128)}, u32[]{:S(2)}) copy-start(s32[128]{0:T(128)} %mig.5) | copy-start | bytes 1540
  3.5 18.5 %collective-permute-start.1 = (bf16[1,2384,128]{2,1,0:T(8,128)(2,1)S(1)}, bf16[1,2384,128]{2,1,0:T(8,128)(2,1)S(1)}, u32[]{:S(2)}, u32[]{:S(2)}) collective-permute-start(bf16[1,2384,128]{2,1,0:T(8,128)(2,1)S(1)} %shard_map.128), channel_id=1, source_target_pairs={{0,64},{4,68},{8,72},{12,76},{16,80},{20,84},{24,88},{28,92},{32,9... | collective-permute-start | bytes 1830920 | tf_op jit(solution)/shard_map/ppermute | solution.py:406
  14.9 16.8 %all-to-all-start = ((bf16[16,32,512]{2,1,0:T(8,128)(2,1)}), bf16[16,32,512]{2,1,0:T(8,128)(2,1)S(1)}, u32[]{:S(2)}, u32[]{:S(2)}) async-start(bf16[16,32,512]{2,1,0:T(8,128)(2,1)} %shard_map.127.refs_0_), calls=%async_computation | async-start | bytes 1048576 | tf_op jit(solution)/shard_map/all_to_all | solution.py:415
  19.8 21.3 %collective-permute-start = (bf16[4,512,128]{2,1,0:T(8,128)(2,1)S(1)}, bf16[4,512,128]{2,1,0:T(8,128)(2,1)S(1)}, u32[]{:S(2)}, u32[]{:S(2)}) collective-permute-start(bf16[4,512,128]{2,1,0:T(8,128)(2,1)S(1)} %copy-done.2), channel_id=1, source_target_pairs={{0,4},{4,0},{8,12},{12,8},{16,20},{20,16},{24,28},{28,24},{32,36},... | collective-permute-start | bytes 1572872 | tf_op jit(solution)/shard_map/ppermute | solution.py:406
  31.7 19.5 %all-to-all-start.1 = ((bf16[16,32,512]{2,1,0:T(8,128)(2,1)}), bf16[16,32,512]{2,1,0:T(8,128)(2,1)S(1)}, u32[]{:S(2)}, u32[]{:S(2)}) async-start(bf16[16,32,512]{2,1,0:T(8,128)(2,1)} %shard_map.129.refs_0_), calls=%async_computation.1 | async-start | bytes 1048576 | tf_op jit(solution)/shard_map/all_to_all | solution.py:415
  42.6 13.4 %collective-permute-start.4 = (bf16[64,1024]{1,0:T(8,128)(2,1)S(1)}, bf16[64,1024]{1,0:T(8,128)(2,1)S(1)}, u32[]{:S(2)}, u32[]{:S(2)}) collective-permute-start(bf16[64,1024]{1,0:T(8,128)(2,1)S(1)} %shard_map.130.refs_0_.k0), channel_id=1, source_target_pairs={{0,3},{1,0},{2,1},{3,2},{4,7},{5,4},{6,5},{7,6},{8,11},{9,8},{10,9... | collective-permute-start | bytes 393224 | tf_op jit(solution)/shard_map/ppermute | solution.py:410
  45.7 10.9 %collective-permute-start.3 = (bf16[64,1024]{1,0:T(8,128)(2,1)S(1)}, bf16[64,1024]{1,0:T(8,128)(2,1)S(1)}, u32[]{:S(2)}, u32[]{:S(2)}) collective-permute-start(bf16[64,1024]{1,0:T(8,128)(2,1)S(1)} %shard_map.130.refs_0_.k0), channel_id=1, source_target_pairs={{0,2},{1,3},{2,0},{3,1},{4,6},{5,7},{6,4},{7,5},{8,10},{9,11},{10,... | collective-permute-start | bytes 393224 | tf_op jit(solution)/shard_map/ppermute | solution.py:410
  46.3 11.3 %collective-permute-start.2 = (bf16[64,1024]{1,0:T(8,128)(2,1)S(1)}, bf16[64,1024]{1,0:T(8,128)(2,1)S(1)}, u32[]{:S(2)}, u32[]{:S(2)}) collective-permute-start(bf16[64,1024]{1,0:T(8,128)(2,1)S(1)} %shard_map.130.refs_0_.k0), channel_id=1, source_target_pairs={{0,1},{1,2},{2,3},{3,0},{4,5},{5,6},{6,7},{7,4},{8,9},{9,10},{10,1... | collective-permute-start | bytes 393224 | tf_op jit(solution)/shard_map/ppermute | solution.py:410
  51.2 12.7 %copy-start.5 = (bf16[512,1792]{1,0:T(8,128)(2,1)S(1)}, bf16[512,1792]{1,0:T(8,128)(2,1)}, u32[]{:S(2)}) copy-start(bf16[512,1792]{1,0:T(8,128)(2,1)} %w_own.6) | copy-start | bytes 5505028
  52.7 7.2 %collective-permute-start.7 = (bf16[64,1024]{1,0:T(8,128)(2,1)S(1)}, bf16[64,1024]{1,0:T(8,128)(2,1)S(1)}, u32[]{:S(2)}, u32[]{:S(2)}) collective-permute-start(bf16[64,1024]{1,0:T(8,128)(2,1)S(1)} %shard_map.131.m0), channel_id=1, source_target_pairs={{0,3},{1,0},{2,1},{3,2},{4,7},{5,4},{6,5},{7,6},{8,11},{9,8},{10,9... | collective-permute-start | bytes 393224 | tf_op jit(solution)/shard_map/ppermute | solution.py:410
  56.0 6.6 %collective-permute-start.6 = (bf16[64,1024]{1,0:T(8,128)(2,1)S(1)}, bf16[64,1024]{1,0:T(8,128)(2,1)S(1)}, u32[]{:S(2)}, u32[]{:S(2)}) collective-permute-start(bf16[64,1024]{1,0:T(8,128)(2,1)S(1)} %shard_map.131.m0), channel_id=1, source_target_pairs={{0,2},{1,3},{2,0},{3,1},{4,6},{5,7},{6,4},{7,5},{8,10},{9,11},{10,... | collective-permute-start | bytes 393224 | tf_op jit(solution)/shard_map/ppermute | solution.py:410
  56.6 7.2 %collective-permute-start.5 = (bf16[64,1024]{1,0:T(8,128)(2,1)S(1)}, bf16[64,1024]{1,0:T(8,128)(2,1)S(1)}, u32[]{:S(2)}, u32[]{:S(2)}) collective-permute-start(bf16[64,1024]{1,0:T(8,128)(2,1)S(1)} %shard_map.131.m0), channel_id=1, source_target_pairs={{0,1},{1,2},{2,3},{3,0},{4,5},{5,6},{6,7},{7,4},{8,9},{9,10},{10,1... | collective-permute-start | bytes 393224 | tf_op jit(solution)/shard_map/ppermute | solution.py:410
  67.9 1.3 copy-start
  69.2 4.4 %copy-start.11 = (bf16[1792]{0:T(1024)(128)(2,1)S(1)}, bf16[1792]{0:T(1024)(128)(2,1)}, u32[]{:S(2)}) copy-start(bf16[1792]{0:T(1024)(128)(2,1)} %param.22) | copy-start | bytes 10756
  69.2 4.5 %copy-start.10 = (bf16[8,4,1792]{2,1,0:T(4,128)(2,1)S(1)}, bf16[8,4,1792]{2,1,0:T(4,128)(2,1)}, u32[]{:S(2)}) copy-start(bf16[8,4,1792]{2,1,0:T(4,128)(2,1)} %param.19) | copy-start | bytes 344068
  69.2 27.6 %all-to-all-start.2 = ((bf16[16,32,1792]{2,1,0:T(8,128)(2,1)}), bf16[16,32,1792]{2,1,0:T(8,128)(2,1)S(1)}, u32[]{:S(2)}, u32[]{:S(2)}) async-start(bf16[16,32,1792]{2,1,0:T(8,128)(2,1)} %copy-done), calls=%async_computation.2 | async-start | bytes 3670016 | tf_op jit(solution)/shard_map/all_to_all | solution.py:415
  73.0 29.4 %collective-permute-start.9 = (bf16[576,1792]{1,0:T(8,128)(2,1)}, bf16[576,1792]{1,0:T(8,128)(2,1)}, u32[]{:S(2)}, u32[]{:S(2)}) collective-permute-start(bf16[576,1792]{1,0:T(8,128)(2,1)} %bitcast.34), channel_id=1, source_target_pairs={{0,4},{4,0},{8,12},{12,8},{16,20},{20,16},{24,28},{28,24},{32,36},... | collective-permute-start | bytes 6193160 | tf_op jit(solution)/shard_map/ppermute | solution.py:406
  73.1 29.3 %collective-permute-start.10 = (bf16[576,1792]{1,0:T(8,128)(2,1)}, bf16[576,1792]{1,0:T(8,128)(2,1)}, u32[]{:S(2)}, u32[]{:S(2)}) collective-permute-start(bf16[576,1792]{1,0:T(8,128)(2,1)} %bitcast.36), channel_id=1, source_target_pairs={{0,4},{4,0},{8,12},{12,8},{16,20},{20,16},{24,28},{28,24},{32,36},... | collective-permute-start | bytes 6193160 | tf_op jit(solution)/shard_map/ppermute | solution.py:406
  97.2 1.4 copy-start.4
  98.5 28.3 %all-to-all-start.3 = ((bf16[16,32,1920]{2,1,0:T(8,128)(2,1)}), bf16[16,32,1920]{2,1,0:T(8,128)(2,1)S(1)}, u32[]{:S(2)}, u32[]{:S(2)}) async-start(bf16[16,32,1920]{2,1,0:T(8,128)(2,1)} %copy-done.4), calls=%async_computation.3 | async-start | bytes 3932160 | tf_op jit(solution)/shard_map/all_to_all | solution.py:415
  102.3 61.2 %collective-permute-start.20 = (bf16[576,1792]{1,0:T(8,128)(2,1)}, bf16[576,1792]{1,0:T(8,128)(2,1)}, u32[]{:S(2)}, u32[]{:S(2)}) collective-permute-start(bf16[576,1792]{1,0:T(8,128)(2,1)} %w_own.7), channel_id=1, source_target_pairs={{0,4},{4,0},{8,12},{12,8},{16,20},{20,16},{24,28},{28,24},{32,36},... | collective-permute-start | bytes 6193160 | tf_op jit(solution)/shard_map/ppermute | solution.py:406
  135.0 38.6 %copy-start.3 = (bf16[576,1792]{1,0:T(8,128)(2,1)S(1)}, bf16[576,1792]{1,0:T(8,128)(2,1)}, u32[]{:S(2)}) copy-start(bf16[576,1792]{1,0:T(8,128)(2,1)} %w_own.7) | copy-start | bytes 6193156
  135.0 10.7 %collective-permute-start.11 = (bf16[64,2432]{1,0:T(8,128)(2,1)S(1)}, bf16[64,2432]{1,0:T(8,128)(2,1)S(1)}, u32[]{:S(2)}, u32[]{:S(2)}) collective-permute-start(bf16[64,2432]{1,0:T(8,128)(2,1)S(1)} %get-tuple-element.19), channel_id=1, source_target_pairs={{0,1},{1,2},{2,3},{3,0},{4,5},{5,6},{6,7},{7,4},{8,9},{9,10},{10,1... | collective-permute-start | bytes 933896 | tf_op jit(solution)/shard_map/ppermute | solution.py:410
  135.1 10.6 %collective-permute-start.12 = (bf16[64,2432]{1,0:T(8,128)(2,1)S(1)}, bf16[64,2432]{1,0:T(8,128)(2,1)S(1)}, u32[]{:S(2)}, u32[]{:S(2)}) collective-permute-start(bf16[64,2432]{1,0:T(8,128)(2,1)S(1)} %get-tuple-element.21), channel_id=1, source_target_pairs={{0,3},{1,0},{2,1},{3,2},{4,7},{5,4},{6,5},{7,6},{8,11},{9,8},{10,9... | collective-permute-start | bytes 933896 | tf_op jit(solution)/shard_map/ppermute | solution.py:410
  138.3 10.8 %collective-permute-start.14 = (bf16[64,2432]{1,0:T(8,128)(2,1)S(1)}, bf16[64,2432]{1,0:T(8,128)(2,1)S(1)}, u32[]{:S(2)}, u32[]{:S(2)}) collective-permute-start(bf16[64,2432]{1,0:T(8,128)(2,1)S(1)} %get-tuple-element.23), channel_id=1, source_target_pairs={{0,1},{1,2},{2,3},{3,0},{4,5},{5,6},{6,7},{7,4},{8,9},{9,10},{10,1... | collective-permute-start | bytes 933896 | tf_op jit(solution)/shard_map/ppermute | solution.py:410
  138.3 10.8 %collective-permute-start.15 = (bf16[64,2432]{1,0:T(8,128)(2,1)S(1)}, bf16[64,2432]{1,0:T(8,128)(2,1)S(1)}, u32[]{:S(2)}, u32[]{:S(2)}) collective-permute-start(bf16[64,2432]{1,0:T(8,128)(2,1)S(1)} %get-tuple-element.24), channel_id=1, source_target_pairs={{0,3},{1,0},{2,1},{3,2},{4,7},{5,4},{6,5},{7,6},{8,11},{9,8},{10,9... | collective-permute-start | bytes 933896 | tf_op jit(solution)/shard_map/ppermute | solution.py:410
  145.8 12.7 %collective-permute-start.13 = (bf16[64,2432]{1,0:T(8,128)(2,1)S(1)}, bf16[64,2432]{1,0:T(8,128)(2,1)S(1)}, u32[]{:S(2)}, u32[]{:S(2)}) collective-permute-start(bf16[64,2432]{1,0:T(8,128)(2,1)S(1)} %get-tuple-element.22), channel_id=1, source_target_pairs={{0,1},{1,2},{2,3},{3,0},{4,5},{5,6},{6,7},{7,4},{8,9},{9,10},{10,1... | collective-permute-start | bytes 933896 | tf_op jit(solution)/shard_map/ppermute | solution.py:410
  145.9 12.6 %collective-permute-start.16 = (bf16[64,2432]{1,0:T(8,128)(2,1)S(1)}, bf16[64,2432]{1,0:T(8,128)(2,1)S(1)}, u32[]{:S(2)}, u32[]{:S(2)}) collective-permute-start(bf16[64,2432]{1,0:T(8,128)(2,1)S(1)} %get-tuple-element.25), channel_id=1, source_target_pairs={{0,3},{1,0},{2,1},{3,2},{4,7},{5,4},{6,5},{7,6},{8,11},{9,8},{10,9... | collective-permute-start | bytes 933896 | tf_op jit(solution)/shard_map/ppermute | solution.py:410
  159.1 10.8 %collective-permute-start.19 = (bf16[128,1152]{1,0:T(8,128)(2,1)S(1)}, bf16[128,1152]{1,0:T(8,128)(2,1)S(1)}, u32[]{:S(2)}, u32[]{:S(2)}) collective-permute-start(bf16[128,1152]{1,0:T(8,128)(2,1)S(1)} %shard_map.136.h0), channel_id=1, source_target_pairs={{0,3},{1,0},{2,1},{3,2},{4,7},{5,4},{6,5},{7,6},{8,11},{9,8},{10,9... | collective-permute-start | bytes 884744 | tf_op jit(solution)/shard_map/ppermute | solution.py:410
  162.5 8.3 %collective-permute-start.18 = (bf16[128,1152]{1,0:T(8,128)(2,1)S(1)}, bf16[128,1152]{1,0:T(8,128)(2,1)S(1)}, u32[]{:S(2)}, u32[]{:S(2)}) collective-permute-start(bf16[128,1152]{1,0:T(8,128)(2,1)S(1)} %shard_map.136.h0), channel_id=1, source_target_pairs={{0,2},{1,3},{2,0},{3,1},{4,6},{5,7},{6,4},{7,5},{8,10},{9,11},{10,... | collective-permute-start | bytes 884744 | tf_op jit(solution)/shard_map/ppermute | solution.py:410
  162.5 11.1 %collective-permute-start.17 = (bf16[128,1152]{1,0:T(8,128)(2,1)S(1)}, bf16[128,1152]{1,0:T(8,128)(2,1)S(1)}, u32[]{:S(2)}, u32[]{:S(2)}) collective-permute-start(bf16[128,1152]{1,0:T(8,128)(2,1)S(1)} %shard_map.136.h0), channel_id=1, source_target_pairs={{0,1},{1,2},{2,3},{3,0},{4,5},{5,6},{6,7},{7,4},{8,9},{9,10},{10,1... | collective-permute-start | bytes 884744 | tf_op jit(solution)/shard_map/ppermute | solution.py:410

commit v4 on v3

--- a/solution.py
+++ b/solution.py
@@ -272,29 +272,21 @@
 
 
 def gate_up_body(ids, x_in, g_own, g_sib, u_own, u_sib, *refs):
-    outs, (x_ref, w_ref, sems) = refs[: len(PIECES)], refs[len(PIECES) :]
-    groups = []
-    for n in range(2 * FFW // 768):
-        group = []
-        at, end = n * 768, (n + 1) * 768
-        while at < end:
-            which, row = divmod(at, 576)
-            count = min(end - at, 576 - row)
-            source = (g_own, g_sib, u_own, u_sib)[which].at[pl.ds(row, count), :]
-            group.append(copy_of(source, w_ref.at[pl.ds(at, count), :], sems.at[n, len(group)]))
-            at += count
-        start(group)
-        groups.append(group)
+    outs, x_ref = refs[: len(PIECES)], refs[len(PIECES)]
     for s in range(4):
         first = ((ids[0] + s) & 3) * 4
         for i in range(4):
             x_ref[s * 128 + i * 32 : s * 128 + i * 32 + 32, :] = x_in[first + i]
-    for n in range(2 * FFW // 768):
-        finished(groups[n])
-        cols = slice(n * 768, (n + 1) * 768)
-        out = dot_t(x_ref[:, :DCOL], w_ref[cols, :]).astype(BF)
-        for piece, (s, top, end) in zip(outs, PIECES):
-            piece[:, cols] = out[s * 128 + top : s * 128 + end]
+    x = x_ref[:, :DCOL]
+    for n, (own, sib) in enumerate(((g_own, g_sib), (u_own, u_sib))):
+        rest = jnp.concatenate([own[512:, :], sib[512:, :]], axis=0)
+        at = n * FFW
+        for w in (own[:512, :], sib[:512, :], rest):
+            cols = slice(at, at + w.shape[0])
+            out = dot_t(x, w).astype(BF)
+            for piece, (s, top, end) in zip(outs, PIECES):
+                piece[:, cols] = out[s * 128 + top : s * 128 + end]
+            at += w.shape[0]
     for piece, (s, top, end) in zip(outs, PIECES):
         piece[:, 2 * FFW :] = x_ref[s * 128 + top : s * 128 + end, DCOL:]
 
@@ -303,14 +295,10 @@
     return pl.pallas_call(
         gate_up_body,
         out_shape=tuple(shape((end - top, GW)) for _, top, end in PIECES),
-        in_specs=[SMEM, VMEM] + [HBM] * 4,
+        in_specs=[SMEM] + [VMEM] * 5,
         out_specs=(VMEM,) * len(PIECES),
-        scratch_shapes=[
-            pltpu.VMEM((512, DCOL + 128), BF),
-            pltpu.VMEM((2 * FFW, DCOL), BF),
-            pltpu.SemaphoreType.DMA((2 * FFW // 768, 2)),
-        ],
-        compiler_params=params(),
+        scratch_shapes=[pltpu.VMEM((512, DCOL + 128), BF)],
+        compiler_params=params(32),
     )(ids, x, *weights)
 
 
@@ -356,7 +344,10 @@
         h_ref[(ids[0] - s) & 3] = h[...]
     for n, (at, end) in enumerate(SPANS):
         finished(groups[n])
-        out = dot(h_ref[...].reshape(512, FFW), w_ref[:, at:end]).astype(BF)
+        h = h_ref[...].reshape(512, FFW)
+        rest = jnp.concatenate([w_ref[512:576, at:end], w_ref[1088:, at:end]], axis=0)
+        out = dot(h[:, :512], w_ref[:512, at:end]) + dot(h[:, 512:1024], w_ref[576:1088, at:end])
+        out = (out + dot(h[:, 1024:], rest)).astype(BF)
         o_ref[:, :, at:end] = out.reshape(CHIPS, 32, end - at)
 
 

time: 202 us -> 205 us (1.015)
  local copies, waits for them, and re-layouts: 6.26 us -> 9.42 us
    unnamed x24 -> x28, local copies, waits for them, and re-layouts: 4.59 us -> 7.75 us
  transfers between devices with their start and end apart: 25 -> 25, of which waited for: 13 -> 13; matrix products, arithmetic and copies ran while one was open for 1% -> 1% of each run, Pallas kernels for 14% -> 13%
where the time goes in v4:
time: 205 us; the launch traced here: 204 us
  waiting for transfers between devices  85.6 us (42%)
  starting transfers between devices  50.5 us (25%)
  Pallas kernels  36.6 us (18%)
  blocking collectives  21.5 us (10%)
  local copies, waits for them, and re-layouts  9.42 us (5%)
    all_to_all x4, waiting for transfers between devices, traded(): lax.all_to_all(blocks, 'dp', 0, 0, tiled=True, axis_index_groups=same_core)  53.6 us
    ppermute x15, waiting for transfers between devices, turned(): return lax.ppermute(block, 'grp', [(i, (i + s) % 4) for i in range(4)])  29.8 us
    ppermute x15, starting transfers between devices, turned(): return lax.ppermute(block, 'grp', [(i, (i + s) % 4) for i in range(4)])  23.8 us
    all_to_all x4, starting transfers between devices, traded(): lax.all_to_all(blocks, 'dp', 0, 0, tiled=True, axis_index_groups=same_core)  21.8 us
    all_to_all x1, blocking collectives, traded(): lax.all_to_all(blocks, 'dp', 0, 0, tiled=True, axis_index_groups=same_core)  21.5 us
    pallas_call x2, Pallas kernels, attend(): pl.pallas_call(functools.partial(attend_body, moved), out_shape=shape((CH...  14.6 us
    unnamed x28, local copies, waits for them, and re-layouts  7.75 us
    pallas_call x1, Pallas kernels, gate_up(): pl.pallas_call(gate_up_body, out_shape=tuple((shape((end - top, GW)) for...  7.14 us
  transfers between devices with their start and end apart: 25, of which 13 were waited for; matrix products, arithmetic and copies ran while one was open for 1% of the time, Pallas kernels for 13%

profile of v4, /device:TPU:0, one launch (start us, length us, event | category | flops | bytes accessed | tf_op | source)
XLA Modules:
  0.0 204.4 jit_solution(101936955518976914)
XLA Ops:
  0.0 0.7 pad.4
  0.7 0.1 reshape.100
  0.9 0.1 stack.36.ids
  0.9 1.3 copy-done.1
  2.2 0.7 copy-done.8
  2.9 0.6 shard_map.128
  3.5 0.0 copy-start.2
  3.5 4.1 %collective-permute-start.1 = (bf16[1,2384,128]{2,1,0:T(8,128)(2,1)S(1)}, bf16[1,2384,128]{2,1,0:T(8,128)(2,1)S(1)}, u32[]{:S(2)}, u32[]{:S(2)}) collective-permute-start(bf16[1,2384,128]{2,1,0:T(8,128)(2,1)S(1)} %shard_map.128), channel_id=1, source_target_pairs={{0,64},{4,68},{8,72},{12,76},{16,80},{20,84},{24,88},{28,92},{32,9... | collective-permute-start | bytes 1830920 | tf_op jit(solution)/shard_map/ppermute | solution.py:397
  7.6 7.3 %shard_map.127.refs_0_ = bf16[16,32,512]{2,1,0:T(8,128)(2,1)} custom-call(s32[8]{0:T(128)S(1)} %stack.36.ids, s32[128]{0:T(128)S(1)} %copy-done.8, s32[2,32]{1,0:T(2,128)S(1)} %copy-done.10, s32[256]{0:T(256)S(1)} %copy-done.11, bf16[2,2304,128]{2,1,0:T(8,128)(2,1)S(1)} %bitcast.31, bf16[2,80,128]{2,1,0:T(8,128)(2,1)S(1)} %bitcast.37, bf16[64,64,576]{2,1,0:T(8,128)(2,1)} %cache.3), custom_call_target="tpu_custom_call" | custom-call | tf_op jit(solution)/shard_map/pallas_call | solution.py:153
  14.9 4.9 %all-to-all-start = ((bf16[16,32,512]{2,1,0:T(8,128)(2,1)}), bf16[16,32,512]{2,1,0:T(8,128)(2,1)S(1)}, u32[]{:S(2)}, u32[]{:S(2)}) async-start(bf16[16,32,512]{2,1,0:T(8,128)(2,1)} %shard_map.127.refs_0_), calls=%async_computation | async-start | bytes 1048576 | tf_op jit(solution)/shard_map/all_to_all | solution.py:406
  19.8 0.1 collective-permute-start
  19.9 2.1 %collective-permute-done.1.q_ref.f_ref = bf16[1,2384,128]{2,1,0:T(8,128)(2,1)S(1)} collective-permute-done((bf16[1,2384,128]{2,1,0:T(8,128)(2,1)S(1)}, bf16[1,2384,128]{2,1,0:T(8,128)(2,1)S(1)}, u32[]{:S(2)}, u32[]{:S(2)}) %collective-permute-start.1) | collective-permute-done | bytes 610336 | tf_op jit(solution)/shard_map/ppermute | solution.py:397
  21.9 7.3 %shard_map.129.refs_0_ = bf16[16,32,512]{2,1,0:T(8,128)(2,1)} custom-call(s32[8]{0:T(128)S(1)} %stack.36.ids, s32[128]{0:T(128)S(1)} %copy-done.9, s32[2,32]{1,0:T(2,128)S(1)} %copy-done.10, s32[256]{0:T(256)S(1)} %copy-done.11, bf16[1,2384,128]{2,1,0:T(8,128)(2,1)S(1)} %collective-permute-done.1.q_ref.f_ref, ...), custom_call_target="tpu_custom_call" | custom-call | tf_op jit(solution)/shard_map/pallas_call | solution.py:153
  29.3 2.4 %all-to-all-done.r_ref = bf16[16,32,512]{2,1,0:T(8,128)(2,1)S(1)} async-done(((bf16[16,32,512]{2,1,0:T(8,128)(2,1)}), bf16[16,32,512]{2,1,0:T(8,128)(2,1)S(1)}, u32[]{:S(2)}, u32[]{:S(2)}) %all-to-all-start) | async-done | bytes 524320 | tf_op jit(solution)/shard_map/all_to_all | solution.py:406
  31.6 9.4 %all-to-all-start.1 = ((bf16[16,32,512]{2,1,0:T(8,128)(2,1)}), bf16[16,32,512]{2,1,0:T(8,128)(2,1)S(1)}, u32[]{:S(2)}, u32[]{:S(2)}) async-start(bf16[16,32,512]{2,1,0:T(8,128)(2,1)} %shard_map.129.refs_0_), calls=%async_computation.1 | async-start | bytes 1048576 | tf_op jit(solution)/shard_map/all_to_all | solution.py:406
  41.1 1.6 shard_map.130.refs_0_.k0
  42.6 3.1 %collective-permute-start.4 = (bf16[64,1024]{1,0:T(8,128)(2,1)S(1)}, bf16[64,1024]{1,0:T(8,128)(2,1)S(1)}, u32[]{:S(2)}, u32[]{:S(2)}) collective-permute-start(bf16[64,1024]{1,0:T(8,128)(2,1)S(1)} %shard_map.130.refs_0_.k0), channel_id=1, source_target_pairs={{0,3},{1,0},{2,1},{3,2},{4,7},{5,4},{6,5},{7,6},{8,11},{9,8},{10,9... | collective-permute-start | bytes 393224 | tf_op jit(solution)/shard_map/ppermute | solution.py:401
  45.7 0.6 collective-permute-start.3
  46.3 1.0 collective-permute-start.2
  47.3 3.9 %all-to-all-done.1.r_ref = bf16[16,32,512]{2,1,0:T(8,128)(2,1)S(1)} async-done(((bf16[16,32,512]{2,1,0:T(8,128)(2,1)}), bf16[16,32,512]{2,1,0:T(8,128)(2,1)S(1)}, u32[]{:S(2)}, u32[]{:S(2)}) %all-to-all-start.1) | async-done | bytes 524320 | tf_op jit(solution)/shard_map/all_to_all | solution.py:406
  51.2 1.6 shard_map.131.m0
  52.7 3.2 %collective-permute-start.7 = (bf16[64,1024]{1,0:T(8,128)(2,1)S(1)}, bf16[64,1024]{1,0:T(8,128)(2,1)S(1)}, u32[]{:S(2)}, u32[]{:S(2)}) collective-permute-start(bf16[64,1024]{1,0:T(8,128)(2,1)S(1)} %shard_map.131.m0), channel_id=1, source_target_pairs={{0,3},{1,0},{2,1},{3,2},{4,7},{5,4},{6,5},{7,6},{8,11},{9,8},{10,9... | collective-permute-start | bytes 393224 | tf_op jit(solution)/shard_map/ppermute | solution.py:401
  56.0 0.6 collective-permute-start.6
  56.6 1.0 collective-permute-start.5
  57.6 2.3 %collective-permute-done.7.m3 = bf16[64,1024]{1,0:T(8,128)(2,1)S(1)} collective-permute-done((bf16[64,1024]{1,0:T(8,128)(2,1)S(1)}, bf16[64,1024]{1,0:T(8,128)(2,1)S(1)}, u32[]{:S(2)}, u32[]{:S(2)}) %collective-permute-start.7) | collective-permute-done | bytes 131104 | tf_op jit(solution)/shard_map/ppermute | solution.py:401
  59.9 2.7 %collective-permute-done.6.m2 = bf16[64,1024]{1,0:T(8,128)(2,1)S(1)} collective-permute-done((bf16[64,1024]{1,0:T(8,128)(2,1)S(1)}, bf16[64,1024]{1,0:T(8,128)(2,1)S(1)}, u32[]{:S(2)}, u32[]{:S(2)}) %collective-permute-start.6) | collective-permute-done | bytes 131104 | tf_op jit(solution)/shard_map/ppermute | solution.py:401
  62.6 1.3 collective-permute-done.5.m1
  63.9 4.0 %shard_map.132 = bf16[16,32,1792]{2,1,0:T(8,128)(2,1)S(1)} custom-call(s32[8]{0:T(128)S(1)} %stack.36.ids, bf16[64,1024]{1,0:T(8,128)(2,1)S(1)} %shard_map.130.refs_0_.k0, bf16[64,1024]{1,0:T(8,128)(2,1)S(1)} %collective-permute-done.2.k1, bf16[64,1024]{1,0:T(8,128)(2,1)S(1)} %collective-permute-done.3.k2, bf16[64,1024]{1,0:T(8,128)(2,1)S(1)} %collective-permute-done.4.k3, ...), custom_call_target="tpu_custom_call" | custom-call | tf_op jit(solution)/shard_map/pallas_call | solution.py:231
  67.9 1.3 copy-done
  69.2 3.8 %all-to-all-start.2 = ((bf16[16,32,1792]{2,1,0:T(8,128)(2,1)}), bf16[16,32,1792]{2,1,0:T(8,128)(2,1)S(1)}, u32[]{:S(2)}, u32[]{:S(2)}) async-start(bf16[16,32,1792]{2,1,0:T(8,128)(2,1)} %copy-done), calls=%async_computation.2 | async-start | bytes 3670016 | tf_op jit(solution)/shard_map/all_to_all | solution.py:406
  73.0 0.1 collective-permute-start.9
  73.1 0.5 collective-permute-start.10
  73.6 0.1 broadcast_compare_fusion
  73.7 0.1 broadcast_select_fusion.2
  73.8 0.1 pad_maximum_fusion
  73.9 22.8 %all-to-all-done.2.r_ref = bf16[16,32,1792]{2,1,0:T(8,128)(2,1)S(1)} async-done(((bf16[16,32,1792]{2,1,0:T(8,128)(2,1)}), bf16[16,32,1792]{2,1,0:T(8,128)(2,1)S(1)}, u32[]{:S(2)}, u32[]{:S(2)}) %all-to-all-start.2) | async-done | bytes 1835040 | tf_op jit(solution)/shard_map/all_to_all | solution.py:406
  96.8 0.4 shard_map.133
  97.2 1.3 copy-done.6
  98.6 3.7 %all-to-all-start.3 = ((bf16[16,32,1920]{2,1,0:T(8,128)(2,1)}), bf16[16,32,1920]{2,1,0:T(8,128)(2,1)S(1)}, u32[]{:S(2)}, u32[]{:S(2)}) async-start(bf16[16,32,1920]{2,1,0:T(8,128)(2,1)} %copy-done.6), calls=%async_computation.3 | async-start | bytes 3932160 | tf_op jit(solution)/shard_map/all_to_all | solution.py:406
  102.3 0.1 collective-permute-start.20
  102.4 24.5 %all-to-all-done.3.x_in = bf16[16,32,1920]{2,1,0:T(8,128)(2,1)S(1)} async-done(((bf16[16,32,1920]{2,1,0:T(8,128)(2,1)}), bf16[16,32,1920]{2,1,0:T(8,128)(2,1)S(1)}, u32[]{:S(2)}, u32[]{:S(2)}) %all-to-all-start.3) | async-done | bytes 1966112 | tf_op jit(solution)/shard_map/all_to_all | solution.py:406
  126.9 1.6 copy-done.4
  128.5 1.6 copy-done.5
  130.0 7.1 %shard_map.134 = (bf16[128,2432]{1,0:T(8,128)(2,1)S(1)}, bf16[64,2432]{1,0:T(8,128)(2,1)S(1)}, bf16[64,2432]{1,0:T(8,128)(2,1)S(1)}, bf16[64,2432]{1,0:T(8,128)(...) custom-call(s32[8]{0:T(128)S(1)} %stack.36.ids, ...), custom_call_target="tpu_custom_call" | custom-call | tf_op jit(solution)/shard_map/pallas_call | solution.py:295
  137.2 0.1 collective-permute-start.11
  137.3 3.2 %collective-permute-start.12 = (bf16[64,2432]{1,0:T(8,128)(2,1)S(1)}, bf16[64,2432]{1,0:T(8,128)(2,1)S(1)}, u32[]{:S(2)}, u32[]{:S(2)}) collective-permute-start(bf16[64,2432]{1,0:T(8,128)(2,1)S(1)} %get-tuple-element.21), channel_id=1, source_target_pairs={{0,3},{1,0},{2,1},{3,2},{4,7},{5,4},{6,5},{7,6},{8,11},{9,8},{10,9... | collective-permute-start | bytes 933896 | tf_op jit(solution)/shard_map/ppermute | solution.py:401
  140.5 3.2 %collective-permute-start.15 = (bf16[64,2432]{1,0:T(8,128)(2,1)S(1)}, bf16[64,2432]{1,0:T(8,128)(2,1)S(1)}, u32[]{:S(2)}, u32[]{:S(2)}) collective-permute-start(bf16[64,2432]{1,0:T(8,128)(2,1)S(1)} %get-tuple-element.24), channel_id=1, source_target_pairs={{0,3},{1,0},{2,1},{3,2},{4,7},{5,4},{6,5},{7,6},{8,11},{9,8},{10,9... | collective-permute-start | bytes 933896 | tf_op jit(solution)/shard_map/ppermute | solution.py:401
  143.7 4.2 %collective-permute-done.11.b = bf16[64,2432]{1,0:T(8,128)(2,1)S(1)} collective-permute-done((bf16[64,2432]{1,0:T(8,128)(2,1)S(1)}, bf16[64,2432]{1,0:T(8,128)(2,1)S(1)}, u32[]{:S(2)}, u32[]{:S(2)}) %collective-permute-start.11) | collective-permute-done | bytes 311328 | tf_op jit(solution)/shard_map/ppermute | solution.py:401
  147.9 0.1 shard_map.135
  148.1 0.1 collective-permute-start.13
  148.1 3.2 %collective-permute-start.16 = (bf16[64,2432]{1,0:T(8,128)(2,1)S(1)}, bf16[64,2432]{1,0:T(8,128)(2,1)S(1)}, u32[]{:S(2)}, u32[]{:S(2)}) collective-permute-start(bf16[64,2432]{1,0:T(8,128)(2,1)S(1)} %get-tuple-element.25), channel_id=1, source_target_pairs={{0,3},{1,0},{2,1},{3,2},{4,7},{5,4},{6,5},{7,6},{8,11},{9,8},{10,9... | collective-permute-start | bytes 933896 | tf_op jit(solution)/shard_map/ppermute | solution.py:401
  151.4 9.2 %collective-permute-done.13.a_low = bf16[64,2432]{1,0:T(8,128)(2,1)S(1)} collective-permute-done((bf16[64,2432]{1,0:T(8,128)(2,1)S(1)}, bf16[64,2432]{1,0:T(8,128)(2,1)S(1)}, u32[]{:S(2)}, u32[]{:S(2)}) %collective-permute-start.13) | collective-permute-done | bytes 311328 | tf_op jit(solution)/shard_map/ppermute | solution.py:401
  160.6 0.5 shard_map.136.h0
  161.2 3.6 %collective-permute-start.19 = (bf16[128,1152]{1,0:T(8,128)(2,1)S(1)}, bf16[128,1152]{1,0:T(8,128)(2,1)S(1)}, u32[]{:S(2)}, u32[]{:S(2)}) collective-permute-start(bf16[128,1152]{1,0:T(8,128)(2,1)S(1)} %shard_map.136.h0), channel_id=1, source_target_pairs={{0,3},{1,0},{2,1},{3,2},{4,7},{5,4},{6,5},{7,6},{8,11},{9,8},{10,9... | collective-permute-start | bytes 884744 | tf_op jit(solution)/shard_map/ppermute | solution.py:401
  164.7 0.9 collective-permute-start.17
  165.7 6.4 %collective-permute-done.19.h3 = bf16[128,1152]{1,0:T(8,128)(2,1)S(1)} collective-permute-done((bf16[128,1152]{1,0:T(8,128)(2,1)S(1)}, bf16[128,1152]{1,0:T(8,128)(2,1)S(1)}, u32[]{:S(2)}, u32[]{:S(2)}) %collective-permute-start.19) | collective-permute-done | bytes 294944 | tf_op jit(solution)/shard_map/ppermute | solution.py:401
  172.1 0.9 collective-permute-done.18.h2
  173.1 2.8 %collective-permute-done.17.h1 = bf16[128,1152]{1,0:T(8,128)(2,1)S(1)} collective-permute-done((bf16[128,1152]{1,0:T(8,128)(2,1)S(1)}, bf16[128,1152]{1,0:T(8,128)(2,1)S(1)}, u32[]{:S(2)}, u32[]{:S(2)}) %collective-permute-start.17) | collective-permute-done | bytes 294944 | tf_op jit(solution)/shard_map/ppermute | solution.py:401
  175.8 5.8 %shard_map.137 = bf16[16,32,1792]{2,1,0:T(8,128)(2,1)S(1)} custom-call(s32[8]{0:T(128)S(1)} %stack.36.ids, bf16[128,1152]{1,0:T(8,128)(2,1)S(1)} %shard_map.136.h0, bf16[128,1152]{1,0:T(8,128)(2,1)S(1)} %collective-permute-done.17.h1, bf16[128,1152]{1,0:T(8,128)(2,1)S(1)} %collective-permute-done.18.h2, bf16[128,1152]{1,0:T(8,128)(2,1)S(1)} %collective-permute-done.19.h3, ...), custom_call_target="tpu_custom_call" | custom-call | tf_op jit(solution)/shard_map/pallas_call | solution.py:355
  181.7 21.5 %all_to_all.25.r_ref = bf16[16,32,1792]{2,1,0:T(8,128)(2,1)S(1)} all-to-all(bf16[16,32,1792]{2,1,0:T(8,128)(2,1)S(1)} %shard_map.137), channel_id=1, replica_groups={{0,8,16,24,32,40,48,56,64,72,80,88,96,104,112,120},{4,12,20,28,36,44,52..., dimensions={0} | all-to-all | bytes 3670016 | tf_op jit(solution)/shard_map/all_to_all | solution.py:406
  203.1 0.2 shard_map.138
  203.5 0.1 broadcast_select_fusion.3
  203.6 0.1 pad_maximum_fusion.1
  203.7 0.7 copy.21
  (42 shorter events, 0.2 us)
Async XLA Ops:
  0.0 7.6 %copy-start.11 = (s32[256]{0:T(256)S(1)}, s32[256]{0:T(256)}, u32[]{:S(2)}) copy-start(s32[256]{0:T(256)} %lengths.3) | copy-start | bytes 3076
  0.0 7.6 %copy-start.10 = (s32[2,32]{1,0:T(2,128)S(1)}, s32[2,32]{1,0:T(2,128)}, u32[]{:S(2)}) copy-start(s32[2,32]{1,0:T(2,128)} %table.3) | copy-start | bytes 772
  0.0 63.9 %collective-permute-start.8 = (bf16[512,1792]{1,0:T(8,128)(2,1)}, bf16[512,1792]{1,0:T(8,128)(2,1)}, u32[]{:S(2)}, u32[]{:S(2)}) collective-permute-start(bf16[512,1792]{1,0:T(8,128)(2,1)} %w_own.6), channel_id=1, source_target_pairs={{0,4},{4,0},{8,12},{12,8},{16,20},{20,16},{24,28},{28,24},{32,36},... | collective-permute-start | bytes 5505032 | tf_op jit(solution)/shard_map/ppermute | solution.py:397
  0.9 1.3 copy-start.1
  2.2 0.7 copy-start.8
  3.5 16.3 %copy-start.2 = (bf16[4,512,128]{2,1,0:T(8,128)(2,1)S(1)}, bf16[4,512,128]{2,1,0:T(8,128)(2,1)}, u32[]{:S(2)}) copy-start(bf16[4,512,128]{2,1,0:T(8,128)(2,1)} %w_own.5) | copy-start | bytes 1572868
  3.5 18.5 %copy-start.9 = (s32[128]{0:T(128)S(1)}, s32[128]{0:T(128)}, u32[]{:S(2)}) copy-start(s32[128]{0:T(128)} %mig.5) | copy-start | bytes 1540
  3.5 18.5 %collective-permute-start.1 = (bf16[1,2384,128]{2,1,0:T(8,128)(2,1)S(1)}, bf16[1,2384,128]{2,1,0:T(8,128)(2,1)S(1)}, u32[]{:S(2)}, u32[]{:S(2)}) collective-permute-start(bf16[1,2384,128]{2,1,0:T(8,128)(2,1)S(1)} %shard_map.128), channel_id=1, source_target_pairs={{0,64},{4,68},{8,72},{12,76},{16,80},{20,84},{24,88},{28,92},{32,9... | collective-permute-start | bytes 1830920 | tf_op jit(solution)/shard_map/ppermute | solution.py:397
  14.9 16.8 %all-to-all-start = ((bf16[16,32,512]{2,1,0:T(8,128)(2,1)}), bf16[16,32,512]{2,1,0:T(8,128)(2,1)S(1)}, u32[]{:S(2)}, u32[]{:S(2)}) async-start(bf16[16,32,512]{2,1,0:T(8,128)(2,1)} %shard_map.127.refs_0_), calls=%async_computation | async-start | bytes 1048576 | tf_op jit(solution)/shard_map/all_to_all | solution.py:406
  19.8 21.3 %collective-permute-start = (bf16[4,512,128]{2,1,0:T(8,128)(2,1)S(1)}, bf16[4,512,128]{2,1,0:T(8,128)(2,1)S(1)}, u32[]{:S(2)}, u32[]{:S(2)}) collective-permute-start(bf16[4,512,128]{2,1,0:T(8,128)(2,1)S(1)} %copy-done.2), channel_id=1, source_target_pairs={{0,4},{4,0},{8,12},{12,8},{16,20},{20,16},{24,28},{28,24},{32,36},... | collective-permute-start | bytes 1572872 | tf_op jit(solution)/shard_map/ppermute | solution.py:397
  31.6 19.5 %all-to-all-start.1 = ((bf16[16,32,512]{2,1,0:T(8,128)(2,1)}), bf16[16,32,512]{2,1,0:T(8,128)(2,1)S(1)}, u32[]{:S(2)}, u32[]{:S(2)}) async-start(bf16[16,32,512]{2,1,0:T(8,128)(2,1)} %shard_map.129.refs_0_), calls=%async_computation.1 | async-start | bytes 1048576 | tf_op jit(solution)/shard_map/all_to_all | solution.py:406
  42.6 13.4 %collective-permute-start.4 = (bf16[64,1024]{1,0:T(8,128)(2,1)S(1)}, bf16[64,1024]{1,0:T(8,128)(2,1)S(1)}, u32[]{:S(2)}, u32[]{:S(2)}) collective-permute-start(bf16[64,1024]{1,0:T(8,128)(2,1)S(1)} %shard_map.130.refs_0_.k0), channel_id=1, source_target_pairs={{0,3},{1,0},{2,1},{3,2},{4,7},{5,4},{6,5},{7,6},{8,11},{9,8},{10,9... | collective-permute-start | bytes 393224 | tf_op jit(solution)/shard_map/ppermute | solution.py:401
  45.7 11.0 %collective-permute-start.3 = (bf16[64,1024]{1,0:T(8,128)(2,1)S(1)}, bf16[64,1024]{1,0:T(8,128)(2,1)S(1)}, u32[]{:S(2)}, u32[]{:S(2)}) collective-permute-start(bf16[64,1024]{1,0:T(8,128)(2,1)S(1)} %shard_map.130.refs_0_.k0), channel_id=1, source_target_pairs={{0,2},{1,3},{2,0},{3,1},{4,6},{5,7},{6,4},{7,5},{8,10},{9,11},{10,... | collective-permute-start | bytes 393224 | tf_op jit(solution)/shard_map/ppermute | solution.py:401
  46.3 11.3 %collective-permute-start.2 = (bf16[64,1024]{1,0:T(8,128)(2,1)S(1)}, bf16[64,1024]{1,0:T(8,128)(2,1)S(1)}, u32[]{:S(2)}, u32[]{:S(2)}) collective-permute-start(bf16[64,1024]{1,0:T(8,128)(2,1)S(1)} %shard_map.130.refs_0_.k0), channel_id=1, source_target_pairs={{0,1},{1,2},{2,3},{3,0},{4,5},{5,6},{6,7},{7,4},{8,9},{9,10},{10,1... | collective-permute-start | bytes 393224 | tf_op jit(solution)/shard_map/ppermute | solution.py:401
  51.2 12.7 %copy-start.7 = (bf16[512,1792]{1,0:T(8,128)(2,1)S(1)}, bf16[512,1792]{1,0:T(8,128)(2,1)}, u32[]{:S(2)}) copy-start(bf16[512,1792]{1,0:T(8,128)(2,1)} %w_own.6) | copy-start | bytes 5505028
  52.7 7.2 %collective-permute-start.7 = (bf16[64,1024]{1,0:T(8,128)(2,1)S(1)}, bf16[64,1024]{1,0:T(8,128)(2,1)S(1)}, u32[]{:S(2)}, u32[]{:S(2)}) collective-permute-start(bf16[64,1024]{1,0:T(8,128)(2,1)S(1)} %shard_map.131.m0), channel_id=1, source_target_pairs={{0,3},{1,0},{2,1},{3,2},{4,7},{5,4},{6,5},{7,6},{8,11},{9,8},{10,9... | collective-permute-start | bytes 393224 | tf_op jit(solution)/shard_map/ppermute | solution.py:401
  56.0 6.6 %collective-permute-start.6 = (bf16[64,1024]{1,0:T(8,128)(2,1)S(1)}, bf16[64,1024]{1,0:T(8,128)(2,1)S(1)}, u32[]{:S(2)}, u32[]{:S(2)}) collective-permute-start(bf16[64,1024]{1,0:T(8,128)(2,1)S(1)} %shard_map.131.m0), channel_id=1, source_target_pairs={{0,2},{1,3},{2,0},{3,1},{4,6},{5,7},{6,4},{7,5},{8,10},{9,11},{10,... | collective-permute-start | bytes 393224 | tf_op jit(solution)/shard_map/ppermute | solution.py:401
  56.6 7.2 %collective-permute-start.5 = (bf16[64,1024]{1,0:T(8,128)(2,1)S(1)}, bf16[64,1024]{1,0:T(8,128)(2,1)S(1)}, u32[]{:S(2)}, u32[]{:S(2)}) collective-permute-start(bf16[64,1024]{1,0:T(8,128)(2,1)S(1)} %shard_map.131.m0), channel_id=1, source_target_pairs={{0,1},{1,2},{2,3},{3,0},{4,5},{5,6},{6,7},{7,4},{8,9},{9,10},{10,1... | collective-permute-start | bytes 393224 | tf_op jit(solution)/shard_map/ppermute | solution.py:401
  67.9 1.3 copy-start
  69.2 4.4 %copy-start.13 = (bf16[1792]{0:T(1024)(128)(2,1)S(1)}, bf16[1792]{0:T(1024)(128)(2,1)}, u32[]{:S(2)}) copy-start(bf16[1792]{0:T(1024)(128)(2,1)} %param.22) | copy-start | bytes 10756
  69.2 4.5 %copy-start.12 = (bf16[8,4,1792]{2,1,0:T(4,128)(2,1)S(1)}, bf16[8,4,1792]{2,1,0:T(4,128)(2,1)}, u32[]{:S(2)}) copy-start(bf16[8,4,1792]{2,1,0:T(4,128)(2,1)} %param.19) | copy-start | bytes 344068
  69.2 27.6 %all-to-all-start.2 = ((bf16[16,32,1792]{2,1,0:T(8,128)(2,1)}), bf16[16,32,1792]{2,1,0:T(8,128)(2,1)S(1)}, u32[]{:S(2)}, u32[]{:S(2)}) async-start(bf16[16,32,1792]{2,1,0:T(8,128)(2,1)} %copy-done), calls=%async_computation.2 | async-start | bytes 3670016 | tf_op jit(solution)/shard_map/all_to_all | solution.py:406
  73.0 29.4 %collective-permute-start.9 = (bf16[576,1792]{1,0:T(8,128)(2,1)}, bf16[576,1792]{1,0:T(8,128)(2,1)}, u32[]{:S(2)}, u32[]{:S(2)}) collective-permute-start(bf16[576,1792]{1,0:T(8,128)(2,1)} %bitcast.32), channel_id=1, source_target_pairs={{0,4},{4,0},{8,12},{12,8},{16,20},{20,16},{24,28},{28,24},{32,36},... | collective-permute-start | bytes 6193160 | tf_op jit(solution)/shard_map/ppermute | solution.py:397
  73.1 29.3 %collective-permute-start.10 = (bf16[576,1792]{1,0:T(8,128)(2,1)}, bf16[576,1792]{1,0:T(8,128)(2,1)}, u32[]{:S(2)}, u32[]{:S(2)}) collective-permute-start(bf16[576,1792]{1,0:T(8,128)(2,1)} %bitcast.34), channel_id=1, source_target_pairs={{0,4},{4,0},{8,12},{12,8},{16,20},{20,16},{24,28},{28,24},{32,36},... | collective-permute-start | bytes 6193160 | tf_op jit(solution)/shard_map/ppermute | solution.py:397
  97.2 1.4 copy-start.6
  98.6 28.3 %all-to-all-start.3 = ((bf16[16,32,1920]{2,1,0:T(8,128)(2,1)}), bf16[16,32,1920]{2,1,0:T(8,128)(2,1)S(1)}, u32[]{:S(2)}, u32[]{:S(2)}) async-start(bf16[16,32,1920]{2,1,0:T(8,128)(2,1)} %copy-done.6), calls=%async_computation.3 | async-start | bytes 3932160 | tf_op jit(solution)/shard_map/all_to_all | solution.py:406
  102.3 63.4 %collective-permute-start.20 = (bf16[576,1792]{1,0:T(8,128)(2,1)}, bf16[576,1792]{1,0:T(8,128)(2,1)}, u32[]{:S(2)}, u32[]{:S(2)}) collective-permute-start(bf16[576,1792]{1,0:T(8,128)(2,1)} %w_own.7), channel_id=1, source_target_pairs={{0,4},{4,0},{8,12},{12,8},{16,20},{20,16},{24,28},{28,24},{32,36},... | collective-permute-start | bytes 6193160 | tf_op jit(solution)/shard_map/ppermute | solution.py:397
  126.9 1.6 copy-start.4
  128.5 1.6 copy-start.5
  137.2 38.6 %copy-start.3 = (bf16[576,1792]{1,0:T(8,128)(2,1)S(1)}, bf16[576,1792]{1,0:T(8,128)(2,1)}, u32[]{:S(2)}) copy-start(bf16[576,1792]{1,0:T(8,128)(2,1)} %w_own.7) | copy-start | bytes 6193156
  137.2 10.7 %collective-permute-start.11 = (bf16[64,2432]{1,0:T(8,128)(2,1)S(1)}, bf16[64,2432]{1,0:T(8,128)(2,1)S(1)}, u32[]{:S(2)}, u32[]{:S(2)}) collective-permute-start(bf16[64,2432]{1,0:T(8,128)(2,1)S(1)} %get-tuple-element.19), channel_id=1, source_target_pairs={{0,1},{1,2},{2,3},{3,0},{4,5},{5,6},{6,7},{7,4},{8,9},{9,10},{10,1... | collective-permute-start | bytes 933896 | tf_op jit(solution)/shard_map/ppermute | solution.py:401
  137.3 10.6 %collective-permute-start.12 = (bf16[64,2432]{1,0:T(8,128)(2,1)S(1)}, bf16[64,2432]{1,0:T(8,128)(2,1)S(1)}, u32[]{:S(2)}, u32[]{:S(2)}) collective-permute-start(bf16[64,2432]{1,0:T(8,128)(2,1)S(1)} %get-tuple-element.21), channel_id=1, source_target_pairs={{0,3},{1,0},{2,1},{3,2},{4,7},{5,4},{6,5},{7,6},{8,11},{9,8},{10,9... | collective-permute-start | bytes 933896 | tf_op jit(solution)/shard_map/ppermute | solution.py:401
  140.5 10.9 %collective-permute-start.14 = (bf16[64,2432]{1,0:T(8,128)(2,1)S(1)}, bf16[64,2432]{1,0:T(8,128)(2,1)S(1)}, u32[]{:S(2)}, u32[]{:S(2)}) collective-permute-start(bf16[64,2432]{1,0:T(8,128)(2,1)S(1)} %get-tuple-element.23), channel_id=1, source_target_pairs={{0,1},{1,2},{2,3},{3,0},{4,5},{5,6},{6,7},{7,4},{8,9},{9,10},{10,1... | collective-permute-start | bytes 933896 | tf_op jit(solution)/shard_map/ppermute | solution.py:401
  140.5 10.9 %collective-permute-start.15 = (bf16[64,2432]{1,0:T(8,128)(2,1)S(1)}, bf16[64,2432]{1,0:T(8,128)(2,1)S(1)}, u32[]{:S(2)}, u32[]{:S(2)}) collective-permute-start(bf16[64,2432]{1,0:T(8,128)(2,1)S(1)} %get-tuple-element.24), channel_id=1, source_target_pairs={{0,3},{1,0},{2,1},{3,2},{4,7},{5,4},{6,5},{7,6},{8,11},{9,8},{10,9... | collective-permute-start | bytes 933896 | tf_op jit(solution)/shard_map/ppermute | solution.py:401
  148.1 12.6 %collective-permute-start.13 = (bf16[64,2432]{1,0:T(8,128)(2,1)S(1)}, bf16[64,2432]{1,0:T(8,128)(2,1)S(1)}, u32[]{:S(2)}, u32[]{:S(2)}) collective-permute-start(bf16[64,2432]{1,0:T(8,128)(2,1)S(1)} %get-tuple-element.22), channel_id=1, source_target_pairs={{0,1},{1,2},{2,3},{3,0},{4,5},{5,6},{6,7},{7,4},{8,9},{9,10},{10,1... | collective-permute-start | bytes 933896 | tf_op jit(solution)/shard_map/ppermute | solution.py:401
  148.1 12.5 %collective-permute-start.16 = (bf16[64,2432]{1,0:T(8,128)(2,1)S(1)}, bf16[64,2432]{1,0:T(8,128)(2,1)S(1)}, u32[]{:S(2)}, u32[]{:S(2)}) collective-permute-start(bf16[64,2432]{1,0:T(8,128)(2,1)S(1)} %get-tuple-element.25), channel_id=1, source_target_pairs={{0,3},{1,0},{2,1},{3,2},{4,7},{5,4},{6,5},{7,6},{8,11},{9,8},{10,9... | collective-permute-start | bytes 933896 | tf_op jit(solution)/shard_map/ppermute | solution.py:401
  161.2 11.0 %collective-permute-start.19 = (bf16[128,1152]{1,0:T(8,128)(2,1)S(1)}, bf16[128,1152]{1,0:T(8,128)(2,1)S(1)}, u32[]{:S(2)}, u32[]{:S(2)}) collective-permute-start(bf16[128,1152]{1,0:T(8,128)(2,1)S(1)} %shard_map.136.h0), channel_id=1, source_target_pairs={{0,3},{1,0},{2,1},{3,2},{4,7},{5,4},{6,5},{7,6},{8,11},{9,8},{10,9... | collective-permute-start | bytes 884744 | tf_op jit(solution)/shard_map/ppermute | solution.py:401
  164.7 8.3 %collective-permute-start.18 = (bf16[128,1152]{1,0:T(8,128)(2,1)S(1)}, bf16[128,1152]{1,0:T(8,128)(2,1)S(1)}, u32[]{:S(2)}, u32[]{:S(2)}) collective-permute-start(bf16[128,1152]{1,0:T(8,128)(2,1)S(1)} %shard_map.136.h0), channel_id=1, source_target_pairs={{0,2},{1,3},{2,0},{3,1},{4,6},{5,7},{6,4},{7,5},{8,10},{9,11},{10,... | collective-permute-start | bytes 884744 | tf_op jit(solution)/shard_map/ppermute | solution.py:401
  164.7 11.1 %collective-permute-start.17 = (bf16[128,1152]{1,0:T(8,128)(2,1)S(1)}, bf16[128,1152]{1,0:T(8,128)(2,1)S(1)}, u32[]{:S(2)}, u32[]{:S(2)}) collective-permute-start(bf16[128,1152]{1,0:T(8,128)(2,1)S(1)} %shard_map.136.h0), channel_id=1, source_target_pairs={{0,1},{1,2},{2,3},{3,0},{4,5},{5,6},{6,7},{7,4},{8,9},{9,10},{10,1... | collective-permute-start | bytes 884744 | tf_op jit(solution)/shard_map/ppermute | solution.py:401

commit v5 on v3

--- a/solution.py
+++ b/solution.py
@@ -271,27 +271,32 @@
 PIECES = ((0, 0, 128), (1, 0, 64), (1, 64, 128), (2, 0, 64), (2, 64, 128), (3, 0, 64), (3, 64, 128))
 
 
+FF_SPANS = ((0, 256), (256, 1280), (1280, 2 * FFW))
+
+
 def gate_up_body(ids, x_in, g_own, g_sib, u_own, u_sib, *refs):
     outs, (x_ref, w_ref, sems) = refs[: len(PIECES)], refs[len(PIECES) :]
     groups = []
-    for n in range(2 * FFW // 768):
+    for at, end in FF_SPANS:
         group = []
-        at, end = n * 768, (n + 1) * 768
         while at < end:
             which, row = divmod(at, 576)
             count = min(end - at, 576 - row)
             source = (g_own, g_sib, u_own, u_sib)[which].at[pl.ds(row, count), :]
-            group.append(copy_of(source, w_ref.at[pl.ds(at, count), :], sems.at[n, len(group)]))
+            group.append(copy_of(source, w_ref.at[pl.ds(at, count), :], sems.at[len(groups), len(group)]))
             at += count
-        start(group)
         groups.append(group)
+    start(groups[0])
+    start(groups[1])
     for s in range(4):
         first = ((ids[0] + s) & 3) * 4
         for i in range(4):
             x_ref[s * 128 + i * 32 : s * 128 + i * 32 + 32, :] = x_in[first + i]
-    for n in range(2 * FFW // 768):
+    for n, (at, end) in enumerate(FF_SPANS):
         finished(groups[n])
-        cols = slice(n * 768, (n + 1) * 768)
+        if n + 2 < len(groups):
+            start(groups[n + 2])
+        cols = slice(at, end)
         out = dot_t(x_ref[:, :DCOL], w_ref[cols, :]).astype(BF)
         for piece, (s, top, end) in zip(outs, PIECES):
             piece[:, cols] = out[s * 128 + top : s * 128 + end]
@@ -308,7 +313,7 @@
         scratch_shapes=[
             pltpu.VMEM((512, DCOL + 128), BF),
             pltpu.VMEM((2 * FFW, DCOL), BF),
-            pltpu.SemaphoreType.DMA((2 * FFW // 768, 2)),
+            pltpu.SemaphoreType.DMA((len(FF_SPANS), 3)),
         ],
         compiler_params=params(),
     )(ids, x, *weights)

time: 202 us -> 201 us (level)
  transfers between devices with their start and end apart: 25 -> 25, of which waited for: 13 -> 13; matrix products, arithmetic and copies ran while one was open for 1% -> 1% of each run, Pallas kernels for 14% -> 13%
where the time goes in v5:
time: 201 us; the launch traced here: 200 us
  waiting for transfers between devices  85.6 us (43%)
  starting transfers between devices  50.3 us (25%)
  Pallas kernels  35.3 us (18%)
  blocking collectives  21.5 us (11%)
  local copies, waits for them, and re-layouts  6.26 us (3%)
    all_to_all x4, waiting for transfers between devices, traded(): lax.all_to_all(blocks, 'dp', 0, 0, tiled=True, axis_index_groups=same_core)  53.6 us
    ppermute x15, waiting for transfers between devices, turned(): return lax.ppermute(block, 'grp', [(i, (i + s) % 4) for i in range(4)])  30 us
    ppermute x15, starting transfers between devices, turned(): return lax.ppermute(block, 'grp', [(i, (i + s) % 4) for i in range(4)])  23.7 us
    all_to_all x4, starting transfers between devices, traded(): lax.all_to_all(blocks, 'dp', 0, 0, tiled=True, axis_index_groups=same_core)  21.8 us
    all_to_all x1, blocking collectives, traded(): lax.all_to_all(blocks, 'dp', 0, 0, tiled=True, axis_index_groups=same_core)  21.5 us
    pallas_call x2, Pallas kernels, attend(): pl.pallas_call(functools.partial(attend_body, moved), out_shape=shape((CH...  14.6 us
    pallas_call x1, Pallas kernels, gate_up(): pl.pallas_call(gate_up_body, out_shape=tuple((shape((end - top, GW)) for...  7.08 us
    ppermute x6, starting transfers between devices, sent(): return lax.ppermute(block, 'dp', route(dz, dx, flip))  4.83 us
  transfers between devices with their start and end apart: 25, of which 13 were waited for; matrix products, arithmetic and copies ran while one was open for 1% of the time, Pallas kernels for 13%

profile of v5, /device:TPU:0, one launch (start us, length us, event | category | flops | bytes accessed | tf_op | source)
XLA Modules:
  0.0 199.8 jit_solution(15646898327477584922)
XLA Ops:
  0.0 0.7 pad.4
  0.7 0.1 reshape.100
  0.9 0.1 stack.36.ids
  0.9 1.3 copy-done.1
  2.2 0.7 copy-done.6
  2.9 0.6 shard_map.128
  3.5 0.0 copy-start.2
  3.5 0.0 copy-start.7
  3.5 4.1 %collective-permute-start.1 = (bf16[1,2384,128]{2,1,0:T(8,128)(2,1)S(1)}, bf16[1,2384,128]{2,1,0:T(8,128)(2,1)S(1)}, u32[]{:S(2)}, u32[]{:S(2)}) collective-permute-start(bf16[1,2384,128]{2,1,0:T(8,128)(2,1)S(1)} %shard_map.128), channel_id=1, source_target_pairs={{0,64},{4,68},{8,72},{12,76},{16,80},{20,84},{24,88},{28,92},{32,9... | collective-permute-start | bytes 1830920 | tf_op jit(solution)/shard_map/ppermute | solution.py:411
  7.6 7.3 %shard_map.127.refs_0_ = bf16[16,32,512]{2,1,0:T(8,128)(2,1)} custom-call(s32[8]{0:T(128)S(1)} %stack.36.ids, s32[128]{0:T(128)S(1)} %copy-done.6, s32[2,32]{1,0:T(2,128)S(1)} %copy-done.8, s32[256]{0:T(256)S(1)} %copy-done.9, bf16[2,2304,128]{2,1,0:T(8,128)(2,1)S(1)} %bitcast.31, bf16[2,80,128]{2,1,0:T(8,128)(2,1)S(1)} %bitcast.33, bf16[64,64,576]{2,1,0:T(8,128)(2,1)} %cache.3), custom_call_target="tpu_custom_call" | custom-call | tf_op jit(solution)/shard_map/pallas_call | solution.py:153
  14.9 4.9 %all-to-all-start = ((bf16[16,32,512]{2,1,0:T(8,128)(2,1)}), bf16[16,32,512]{2,1,0:T(8,128)(2,1)S(1)}, u32[]{:S(2)}, u32[]{:S(2)}) async-start(bf16[16,32,512]{2,1,0:T(8,128)(2,1)} %shard_map.127.refs_0_), calls=%async_computation | async-start | bytes 1048576 | tf_op jit(solution)/shard_map/all_to_all | solution.py:420
  19.8 0.1 collective-permute-start
  19.9 2.1 %collective-permute-done.1.q_ref.f_ref = bf16[1,2384,128]{2,1,0:T(8,128)(2,1)S(1)} collective-permute-done((bf16[1,2384,128]{2,1,0:T(8,128)(2,1)S(1)}, bf16[1,2384,128]{2,1,0:T(8,128)(2,1)S(1)}, u32[]{:S(2)}, u32[]{:S(2)}) %collective-permute-start.1) | collective-permute-done | bytes 610336 | tf_op jit(solution)/shard_map/ppermute | solution.py:411
  21.9 7.3 %shard_map.129.refs_0_ = bf16[16,32,512]{2,1,0:T(8,128)(2,1)} custom-call(s32[8]{0:T(128)S(1)} %stack.36.ids, s32[128]{0:T(128)S(1)} %copy-done.7, s32[2,32]{1,0:T(2,128)S(1)} %copy-done.8, s32[256]{0:T(256)S(1)} %copy-done.9, bf16[1,2384,128]{2,1,0:T(8,128)(2,1)S(1)} %collective-permute-done.1.q_ref.f_ref, ...), custom_call_target="tpu_custom_call" | custom-call | tf_op jit(solution)/shard_map/pallas_call | solution.py:153
  29.3 2.4 %all-to-all-done.r_ref = bf16[16,32,512]{2,1,0:T(8,128)(2,1)S(1)} async-done(((bf16[16,32,512]{2,1,0:T(8,128)(2,1)}), bf16[16,32,512]{2,1,0:T(8,128)(2,1)S(1)}, u32[]{:S(2)}, u32[]{:S(2)}) %all-to-all-start) | async-done | bytes 524320 | tf_op jit(solution)/shard_map/all_to_all | solution.py:420
  31.7 9.4 %all-to-all-start.1 = ((bf16[16,32,512]{2,1,0:T(8,128)(2,1)}), bf16[16,32,512]{2,1,0:T(8,128)(2,1)S(1)}, u32[]{:S(2)}, u32[]{:S(2)}) async-start(bf16[16,32,512]{2,1,0:T(8,128)(2,1)} %shard_map.129.refs_0_), calls=%async_computation.1 | async-start | bytes 1048576 | tf_op jit(solution)/shard_map/all_to_all | solution.py:420
  41.1 1.6 shard_map.130.refs_0_.k0
  42.6 3.1 %collective-permute-start.4 = (bf16[64,1024]{1,0:T(8,128)(2,1)S(1)}, bf16[64,1024]{1,0:T(8,128)(2,1)S(1)}, u32[]{:S(2)}, u32[]{:S(2)}) collective-permute-start(bf16[64,1024]{1,0:T(8,128)(2,1)S(1)} %shard_map.130.refs_0_.k0), channel_id=1, source_target_pairs={{0,3},{1,0},{2,1},{3,2},{4,7},{5,4},{6,5},{7,6},{8,11},{9,8},{10,9... | collective-permute-start | bytes 393224 | tf_op jit(solution)/shard_map/ppermute | solution.py:415
  45.7 0.6 collective-permute-start.3
  46.3 1.0 collective-permute-start.2
  47.3 3.9 %all-to-all-done.1.r_ref = bf16[16,32,512]{2,1,0:T(8,128)(2,1)S(1)} async-done(((bf16[16,32,512]{2,1,0:T(8,128)(2,1)}), bf16[16,32,512]{2,1,0:T(8,128)(2,1)S(1)}, u32[]{:S(2)}, u32[]{:S(2)}) %all-to-all-start.1) | async-done | bytes 524320 | tf_op jit(solution)/shard_map/all_to_all | solution.py:420
  51.2 1.6 shard_map.131.m0
  52.7 3.2 %collective-permute-start.7 = (bf16[64,1024]{1,0:T(8,128)(2,1)S(1)}, bf16[64,1024]{1,0:T(8,128)(2,1)S(1)}, u32[]{:S(2)}, u32[]{:S(2)}) collective-permute-start(bf16[64,1024]{1,0:T(8,128)(2,1)S(1)} %shard_map.131.m0), channel_id=1, source_target_pairs={{0,3},{1,0},{2,1},{3,2},{4,7},{5,4},{6,5},{7,6},{8,11},{9,8},{10,9... | collective-permute-start | bytes 393224 | tf_op jit(solution)/shard_map/ppermute | solution.py:415
  56.0 0.6 collective-permute-start.6
  56.6 1.0 collective-permute-start.5
  57.6 2.3 %collective-permute-done.7.m3 = bf16[64,1024]{1,0:T(8,128)(2,1)S(1)} collective-permute-done((bf16[64,1024]{1,0:T(8,128)(2,1)S(1)}, bf16[64,1024]{1,0:T(8,128)(2,1)S(1)}, u32[]{:S(2)}, u32[]{:S(2)}) %collective-permute-start.7) | collective-permute-done | bytes 131104 | tf_op jit(solution)/shard_map/ppermute | solution.py:415
  59.9 2.7 %collective-permute-done.6.m2 = bf16[64,1024]{1,0:T(8,128)(2,1)S(1)} collective-permute-done((bf16[64,1024]{1,0:T(8,128)(2,1)S(1)}, bf16[64,1024]{1,0:T(8,128)(2,1)S(1)}, u32[]{:S(2)}, u32[]{:S(2)}) %collective-permute-start.6) | collective-permute-done | bytes 131104 | tf_op jit(solution)/shard_map/ppermute | solution.py:415
  62.6 1.3 collective-permute-done.5.m1
  63.9 4.0 %shard_map.132 = bf16[16,32,1792]{2,1,0:T(8,128)(2,1)S(1)} custom-call(s32[8]{0:T(128)S(1)} %stack.36.ids, bf16[64,1024]{1,0:T(8,128)(2,1)S(1)} %shard_map.130.refs_0_.k0, bf16[64,1024]{1,0:T(8,128)(2,1)S(1)} %collective-permute-done.2.k1, bf16[64,1024]{1,0:T(8,128)(2,1)S(1)} %collective-permute-done.3.k2, bf16[64,1024]{1,0:T(8,128)(2,1)S(1)} %collective-permute-done.4.k3, ...), custom_call_target="tpu_custom_call" | custom-call | tf_op jit(solution)/shard_map/pallas_call | solution.py:231
  67.9 1.3 copy-done
  69.2 3.8 %all-to-all-start.2 = ((bf16[16,32,1792]{2,1,0:T(8,128)(2,1)}), bf16[16,32,1792]{2,1,0:T(8,128)(2,1)S(1)}, u32[]{:S(2)}, u32[]{:S(2)}) async-start(bf16[16,32,1792]{2,1,0:T(8,128)(2,1)} %copy-done), calls=%async_computation.2 | async-start | bytes 3670016 | tf_op jit(solution)/shard_map/all_to_all | solution.py:420
  73.0 0.1 collective-permute-start.9
  73.1 0.5 collective-permute-start.10
  73.6 0.1 broadcast_compare_fusion
  73.7 0.1 broadcast_select_fusion.2
  73.8 0.1 pad_maximum_fusion
  73.9 22.8 %all-to-all-done.2.r_ref = bf16[16,32,1792]{2,1,0:T(8,128)(2,1)S(1)} async-done(((bf16[16,32,1792]{2,1,0:T(8,128)(2,1)}), bf16[16,32,1792]{2,1,0:T(8,128)(2,1)S(1)}, u32[]{:S(2)}, u32[]{:S(2)}) %all-to-all-start.2) | async-done | bytes 1835040 | tf_op jit(solution)/shard_map/all_to_all | solution.py:420
  96.8 0.4 shard_map.133
  97.2 1.4 copy-done.4
  98.5 3.7 %all-to-all-start.3 = ((bf16[16,32,1920]{2,1,0:T(8,128)(2,1)}), bf16[16,32,1920]{2,1,0:T(8,128)(2,1)S(1)}, u32[]{:S(2)}, u32[]{:S(2)}) async-start(bf16[16,32,1920]{2,1,0:T(8,128)(2,1)} %copy-done.4), calls=%async_computation.3 | async-start | bytes 3932160 | tf_op jit(solution)/shard_map/all_to_all | solution.py:420
  102.3 0.1 collective-permute-start.20
  102.4 24.5 %all-to-all-done.3.x_in = bf16[16,32,1920]{2,1,0:T(8,128)(2,1)S(1)} async-done(((bf16[16,32,1920]{2,1,0:T(8,128)(2,1)}), bf16[16,32,1920]{2,1,0:T(8,128)(2,1)S(1)}, u32[]{:S(2)}, u32[]{:S(2)}) %all-to-all-start.3) | async-done | bytes 1966112 | tf_op jit(solution)/shard_map/all_to_all | solution.py:420
  126.9 7.1 %shard_map.134 = (bf16[128,2432]{1,0:T(8,128)(2,1)S(1)}, bf16[64,2432]{1,0:T(8,128)(2,1)S(1)}, bf16[64,2432]{1,0:T(8,128)(2,1)S(1)}, bf16[64,2432]{1,0:T(8,128)(...) custom-call(s32[8]{0:T(128)S(1)} %stack.36.ids, ...), custom_call_target="tpu_custom_call" | custom-call | tf_op jit(solution)/shard_map/pallas_call | solution.py:308
  133.9 0.0 copy-start.3
  134.0 0.1 collective-permute-start.11
  134.0 3.2 %collective-permute-start.12 = (bf16[64,2432]{1,0:T(8,128)(2,1)S(1)}, bf16[64,2432]{1,0:T(8,128)(2,1)S(1)}, u32[]{:S(2)}, u32[]{:S(2)}) collective-permute-start(bf16[64,2432]{1,0:T(8,128)(2,1)S(1)} %get-tuple-element.21), channel_id=1, source_target_pairs={{0,3},{1,0},{2,1},{3,2},{4,7},{5,4},{6,5},{7,6},{8,11},{9,8},{10,9... | collective-permute-start | bytes 933896 | tf_op jit(solution)/shard_map/ppermute | solution.py:415
  137.3 3.2 %collective-permute-start.15 = (bf16[64,2432]{1,0:T(8,128)(2,1)S(1)}, bf16[64,2432]{1,0:T(8,128)(2,1)S(1)}, u32[]{:S(2)}, u32[]{:S(2)}) collective-permute-start(bf16[64,2432]{1,0:T(8,128)(2,1)S(1)} %get-tuple-element.24), channel_id=1, source_target_pairs={{0,3},{1,0},{2,1},{3,2},{4,7},{5,4},{6,5},{7,6},{8,11},{9,8},{10,9... | collective-permute-start | bytes 933896 | tf_op jit(solution)/shard_map/ppermute | solution.py:415
  140.5 4.1 %collective-permute-done.11.b = bf16[64,2432]{1,0:T(8,128)(2,1)S(1)} collective-permute-done((bf16[64,2432]{1,0:T(8,128)(2,1)S(1)}, bf16[64,2432]{1,0:T(8,128)(2,1)S(1)}, u32[]{:S(2)}, u32[]{:S(2)}) %collective-permute-start.11) | collective-permute-done | bytes 311328 | tf_op jit(solution)/shard_map/ppermute | solution.py:415
  144.6 0.1 shard_map.135
  144.8 0.1 collective-permute-start.13
  144.9 3.2 %collective-permute-start.16 = (bf16[64,2432]{1,0:T(8,128)(2,1)S(1)}, bf16[64,2432]{1,0:T(8,128)(2,1)S(1)}, u32[]{:S(2)}, u32[]{:S(2)}) collective-permute-start(bf16[64,2432]{1,0:T(8,128)(2,1)S(1)} %get-tuple-element.25), channel_id=1, source_target_pairs={{0,3},{1,0},{2,1},{3,2},{4,7},{5,4},{6,5},{7,6},{8,11},{9,8},{10,9... | collective-permute-start | bytes 933896 | tf_op jit(solution)/shard_map/ppermute | solution.py:415
  148.1 9.4 %collective-permute-done.13.a_low = bf16[64,2432]{1,0:T(8,128)(2,1)S(1)} collective-permute-done((bf16[64,2432]{1,0:T(8,128)(2,1)S(1)}, bf16[64,2432]{1,0:T(8,128)(2,1)S(1)}, u32[]{:S(2)}, u32[]{:S(2)}) %collective-permute-start.13) | collective-permute-done | bytes 311328 | tf_op jit(solution)/shard_map/ppermute | solution.py:415
  157.5 0.5 shard_map.136.h0
  158.1 3.4 %collective-permute-start.19 = (bf16[128,1152]{1,0:T(8,128)(2,1)S(1)}, bf16[128,1152]{1,0:T(8,128)(2,1)S(1)}, u32[]{:S(2)}, u32[]{:S(2)}) collective-permute-start(bf16[128,1152]{1,0:T(8,128)(2,1)S(1)} %shard_map.136.h0), channel_id=1, source_target_pairs={{0,3},{1,0},{2,1},{3,2},{4,7},{5,4},{6,5},{7,6},{8,11},{9,8},{10,9... | collective-permute-start | bytes 884744 | tf_op jit(solution)/shard_map/ppermute | solution.py:415
  161.5 0.9 collective-permute-start.17
  162.4 6.4 %collective-permute-done.19.h3 = bf16[128,1152]{1,0:T(8,128)(2,1)S(1)} collective-permute-done((bf16[128,1152]{1,0:T(8,128)(2,1)S(1)}, bf16[128,1152]{1,0:T(8,128)(2,1)S(1)}, u32[]{:S(2)}, u32[]{:S(2)}) %collective-permute-start.19) | collective-permute-done | bytes 294944 | tf_op jit(solution)/shard_map/ppermute | solution.py:415
  168.9 0.9 collective-permute-done.18.h2
  169.8 2.8 %collective-permute-done.17.h1 = bf16[128,1152]{1,0:T(8,128)(2,1)S(1)} collective-permute-done((bf16[128,1152]{1,0:T(8,128)(2,1)S(1)}, bf16[128,1152]{1,0:T(8,128)(2,1)S(1)}, u32[]{:S(2)}, u32[]{:S(2)}) %collective-permute-start.17) | collective-permute-done | bytes 294944 | tf_op jit(solution)/shard_map/ppermute | solution.py:415
  172.6 4.5 %shard_map.137 = bf16[16,32,1792]{2,1,0:T(8,128)(2,1)S(1)} custom-call(s32[8]{0:T(128)S(1)} %stack.36.ids, bf16[128,1152]{1,0:T(8,128)(2,1)S(1)} %shard_map.136.h0, bf16[128,1152]{1,0:T(8,128)(2,1)S(1)} %collective-permute-done.17.h1, bf16[128,1152]{1,0:T(8,128)(2,1)S(1)} %collective-permute-done.18.h2, bf16[128,1152]{1,0:T(8,128)(2,1)S(1)} %collective-permute-done.19.h3, ...), custom_call_target="tpu_custom_call" | custom-call | tf_op jit(solution)/shard_map/pallas_call | solution.py:369
  177.1 21.5 %all_to_all.25.r_ref = bf16[16,32,1792]{2,1,0:T(8,128)(2,1)S(1)} all-to-all(bf16[16,32,1792]{2,1,0:T(8,128)(2,1)S(1)} %shard_map.137), channel_id=1, replica_groups={{0,8,16,24,32,40,48,56,64,72,80,88,96,104,112,120},{4,12,20,28,36,44,52..., dimensions={0} | all-to-all | bytes 3670016 | tf_op jit(solution)/shard_map/all_to_all | solution.py:420
  198.6 0.3 shard_map.138
  198.9 0.1 broadcast_select_fusion.3
  199.0 0.1 pad_maximum_fusion.1
  199.1 0.7 copy.21
  (38 shorter events, 0.2 us)
Async XLA Ops:
  0.0 7.6 %copy-start.9 = (s32[256]{0:T(256)S(1)}, s32[256]{0:T(256)}, u32[]{:S(2)}) copy-start(s32[256]{0:T(256)} %lengths.3) | copy-start | bytes 3076
  0.0 7.6 %copy-start.8 = (s32[2,32]{1,0:T(2,128)S(1)}, s32[2,32]{1,0:T(2,128)}, u32[]{:S(2)}) copy-start(s32[2,32]{1,0:T(2,128)} %table.3) | copy-start | bytes 772
  0.0 63.9 %collective-permute-start.8 = (bf16[512,1792]{1,0:T(8,128)(2,1)}, bf16[512,1792]{1,0:T(8,128)(2,1)}, u32[]{:S(2)}, u32[]{:S(2)}) collective-permute-start(bf16[512,1792]{1,0:T(8,128)(2,1)} %w_own.6), channel_id=1, source_target_pairs={{0,4},{4,0},{8,12},{12,8},{16,20},{20,16},{24,28},{28,24},{32,36},... | collective-permute-start | bytes 5505032 | tf_op jit(solution)/shard_map/ppermute | solution.py:411
  0.9 1.3 copy-start.1
  2.2 0.7 copy-start.6
  3.5 16.3 %copy-start.2 = (bf16[4,512,128]{2,1,0:T(8,128)(2,1)S(1)}, bf16[4,512,128]{2,1,0:T(8,128)(2,1)}, u32[]{:S(2)}) copy-start(bf16[4,512,128]{2,1,0:T(8,128)(2,1)} %w_own.5) | copy-start | bytes 1572868
  3.5 18.5 %copy-start.7 = (s32[128]{0:T(128)S(1)}, s32[128]{0:T(128)}, u32[]{:S(2)}) copy-start(s32[128]{0:T(128)} %mig.5) | copy-start | bytes 1540
  3.5 18.5 %collective-permute-start.1 = (bf16[1,2384,128]{2,1,0:T(8,128)(2,1)S(1)}, bf16[1,2384,128]{2,1,0:T(8,128)(2,1)S(1)}, u32[]{:S(2)}, u32[]{:S(2)}) collective-permute-start(bf16[1,2384,128]{2,1,0:T(8,128)(2,1)S(1)} %shard_map.128), channel_id=1, source_target_pairs={{0,64},{4,68},{8,72},{12,76},{16,80},{20,84},{24,88},{28,92},{32,9... | collective-permute-start | bytes 1830920 | tf_op jit(solution)/shard_map/ppermute | solution.py:411
  14.9 16.8 %all-to-all-start = ((bf16[16,32,512]{2,1,0:T(8,128)(2,1)}), bf16[16,32,512]{2,1,0:T(8,128)(2,1)S(1)}, u32[]{:S(2)}, u32[]{:S(2)}) async-start(bf16[16,32,512]{2,1,0:T(8,128)(2,1)} %shard_map.127.refs_0_), calls=%async_computation | async-start | bytes 1048576 | tf_op jit(solution)/shard_map/all_to_all | solution.py:420
  19.8 21.3 %collective-permute-start = (bf16[4,512,128]{2,1,0:T(8,128)(2,1)S(1)}, bf16[4,512,128]{2,1,0:T(8,128)(2,1)S(1)}, u32[]{:S(2)}, u32[]{:S(2)}) collective-permute-start(bf16[4,512,128]{2,1,0:T(8,128)(2,1)S(1)} %copy-done.2), channel_id=1, source_target_pairs={{0,4},{4,0},{8,12},{12,8},{16,20},{20,16},{24,28},{28,24},{32,36},... | collective-permute-start | bytes 1572872 | tf_op jit(solution)/shard_map/ppermute | solution.py:411
  31.7 19.5 %all-to-all-start.1 = ((bf16[16,32,512]{2,1,0:T(8,128)(2,1)}), bf16[16,32,512]{2,1,0:T(8,128)(2,1)S(1)}, u32[]{:S(2)}, u32[]{:S(2)}) async-start(bf16[16,32,512]{2,1,0:T(8,128)(2,1)} %shard_map.129.refs_0_), calls=%async_computation.1 | async-start | bytes 1048576 | tf_op jit(solution)/shard_map/all_to_all | solution.py:420
  42.6 13.4 %collective-permute-start.4 = (bf16[64,1024]{1,0:T(8,128)(2,1)S(1)}, bf16[64,1024]{1,0:T(8,128)(2,1)S(1)}, u32[]{:S(2)}, u32[]{:S(2)}) collective-permute-start(bf16[64,1024]{1,0:T(8,128)(2,1)S(1)} %shard_map.130.refs_0_.k0), channel_id=1, source_target_pairs={{0,3},{1,0},{2,1},{3,2},{4,7},{5,4},{6,5},{7,6},{8,11},{9,8},{10,9... | collective-permute-start | bytes 393224 | tf_op jit(solution)/shard_map/ppermute | solution.py:415
  45.7 10.9 %collective-permute-start.3 = (bf16[64,1024]{1,0:T(8,128)(2,1)S(1)}, bf16[64,1024]{1,0:T(8,128)(2,1)S(1)}, u32[]{:S(2)}, u32[]{:S(2)}) collective-permute-start(bf16[64,1024]{1,0:T(8,128)(2,1)S(1)} %shard_map.130.refs_0_.k0), channel_id=1, source_target_pairs={{0,2},{1,3},{2,0},{3,1},{4,6},{5,7},{6,4},{7,5},{8,10},{9,11},{10,... | collective-permute-start | bytes 393224 | tf_op jit(solution)/shard_map/ppermute | solution.py:415
  46.3 11.3 %collective-permute-start.2 = (bf16[64,1024]{1,0:T(8,128)(2,1)S(1)}, bf16[64,1024]{1,0:T(8,128)(2,1)S(1)}, u32[]{:S(2)}, u32[]{:S(2)}) collective-permute-start(bf16[64,1024]{1,0:T(8,128)(2,1)S(1)} %shard_map.130.refs_0_.k0), channel_id=1, source_target_pairs={{0,1},{1,2},{2,3},{3,0},{4,5},{5,6},{6,7},{7,4},{8,9},{9,10},{10,1... | collective-permute-start | bytes 393224 | tf_op jit(solution)/shard_map/ppermute | solution.py:415
  51.2 12.7 %copy-start.5 = (bf16[512,1792]{1,0:T(8,128)(2,1)S(1)}, bf16[512,1792]{1,0:T(8,128)(2,1)}, u32[]{:S(2)}) copy-start(bf16[512,1792]{1,0:T(8,128)(2,1)} %w_own.6) | copy-start | bytes 5505028
  52.7 7.2 %collective-permute-start.7 = (bf16[64,1024]{1,0:T(8,128)(2,1)S(1)}, bf16[64,1024]{1,0:T(8,128)(2,1)S(1)}, u32[]{:S(2)}, u32[]{:S(2)}) collective-permute-start(bf16[64,1024]{1,0:T(8,128)(2,1)S(1)} %shard_map.131.m0), channel_id=1, source_target_pairs={{0,3},{1,0},{2,1},{3,2},{4,7},{5,4},{6,5},{7,6},{8,11},{9,8},{10,9... | collective-permute-start | bytes 393224 | tf_op jit(solution)/shard_map/ppermute | solution.py:415
  56.0 6.6 %collective-permute-start.6 = (bf16[64,1024]{1,0:T(8,128)(2,1)S(1)}, bf16[64,1024]{1,0:T(8,128)(2,1)S(1)}, u32[]{:S(2)}, u32[]{:S(2)}) collective-permute-start(bf16[64,1024]{1,0:T(8,128)(2,1)S(1)} %shard_map.131.m0), channel_id=1, source_target_pairs={{0,2},{1,3},{2,0},{3,1},{4,6},{5,7},{6,4},{7,5},{8,10},{9,11},{10,... | collective-permute-start | bytes 393224 | tf_op jit(solution)/shard_map/ppermute | solution.py:415
  56.6 7.2 %collective-permute-start.5 = (bf16[64,1024]{1,0:T(8,128)(2,1)S(1)}, bf16[64,1024]{1,0:T(8,128)(2,1)S(1)}, u32[]{:S(2)}, u32[]{:S(2)}) collective-permute-start(bf16[64,1024]{1,0:T(8,128)(2,1)S(1)} %shard_map.131.m0), channel_id=1, source_target_pairs={{0,1},{1,2},{2,3},{3,0},{4,5},{5,6},{6,7},{7,4},{8,9},{9,10},{10,1... | collective-permute-start | bytes 393224 | tf_op jit(solution)/shard_map/ppermute | solution.py:415
  67.9 1.3 copy-start
  69.2 4.4 %copy-start.11 = (bf16[1792]{0:T(1024)(128)(2,1)S(1)}, bf16[1792]{0:T(1024)(128)(2,1)}, u32[]{:S(2)}) copy-start(bf16[1792]{0:T(1024)(128)(2,1)} %param.22) | copy-start | bytes 10756
  69.2 4.5 %copy-start.10 = (bf16[8,4,1792]{2,1,0:T(4,128)(2,1)S(1)}, bf16[8,4,1792]{2,1,0:T(4,128)(2,1)}, u32[]{:S(2)}) copy-start(bf16[8,4,1792]{2,1,0:T(4,128)(2,1)} %param.19) | copy-start | bytes 344068
  69.2 27.6 %all-to-all-start.2 = ((bf16[16,32,1792]{2,1,0:T(8,128)(2,1)}), bf16[16,32,1792]{2,1,0:T(8,128)(2,1)S(1)}, u32[]{:S(2)}, u32[]{:S(2)}) async-start(bf16[16,32,1792]{2,1,0:T(8,128)(2,1)} %copy-done), calls=%async_computation.2 | async-start | bytes 3670016 | tf_op jit(solution)/shard_map/all_to_all | solution.py:420
  73.0 29.4 %collective-permute-start.9 = (bf16[576,1792]{1,0:T(8,128)(2,1)}, bf16[576,1792]{1,0:T(8,128)(2,1)}, u32[]{:S(2)}, u32[]{:S(2)}) collective-permute-start(bf16[576,1792]{1,0:T(8,128)(2,1)} %bitcast.34), channel_id=1, source_target_pairs={{0,4},{4,0},{8,12},{12,8},{16,20},{20,16},{24,28},{28,24},{32,36},... | collective-permute-start | bytes 6193160 | tf_op jit(solution)/shard_map/ppermute | solution.py:411
  73.1 29.3 %collective-permute-start.10 = (bf16[576,1792]{1,0:T(8,128)(2,1)}, bf16[576,1792]{1,0:T(8,128)(2,1)}, u32[]{:S(2)}, u32[]{:S(2)}) collective-permute-start(bf16[576,1792]{1,0:T(8,128)(2,1)} %bitcast.36), channel_id=1, source_target_pairs={{0,4},{4,0},{8,12},{12,8},{16,20},{20,16},{24,28},{28,24},{32,36},... | collective-permute-start | bytes 6193160 | tf_op jit(solution)/shard_map/ppermute | solution.py:411
  97.2 1.4 copy-start.4
  98.5 28.3 %all-to-all-start.3 = ((bf16[16,32,1920]{2,1,0:T(8,128)(2,1)}), bf16[16,32,1920]{2,1,0:T(8,128)(2,1)S(1)}, u32[]{:S(2)}, u32[]{:S(2)}) async-start(bf16[16,32,1920]{2,1,0:T(8,128)(2,1)} %copy-done.4), calls=%async_computation.3 | async-start | bytes 3932160 | tf_op jit(solution)/shard_map/all_to_all | solution.py:420
  102.3 60.1 %collective-permute-start.20 = (bf16[576,1792]{1,0:T(8,128)(2,1)}, bf16[576,1792]{1,0:T(8,128)(2,1)}, u32[]{:S(2)}, u32[]{:S(2)}) collective-permute-start(bf16[576,1792]{1,0:T(8,128)(2,1)} %w_own.7), channel_id=1, source_target_pairs={{0,4},{4,0},{8,12},{12,8},{16,20},{20,16},{24,28},{28,24},{32,36},... | collective-permute-start | bytes 6193160 | tf_op jit(solution)/shard_map/ppermute | solution.py:411
  133.9 38.6 %copy-start.3 = (bf16[576,1792]{1,0:T(8,128)(2,1)S(1)}, bf16[576,1792]{1,0:T(8,128)(2,1)}, u32[]{:S(2)}) copy-start(bf16[576,1792]{1,0:T(8,128)(2,1)} %w_own.7) | copy-start | bytes 6193156
  134.0 10.7 %collective-permute-start.11 = (bf16[64,2432]{1,0:T(8,128)(2,1)S(1)}, bf16[64,2432]{1,0:T(8,128)(2,1)S(1)}, u32[]{:S(2)}, u32[]{:S(2)}) collective-permute-start(bf16[64,2432]{1,0:T(8,128)(2,1)S(1)} %get-tuple-element.19), channel_id=1, source_target_pairs={{0,1},{1,2},{2,3},{3,0},{4,5},{5,6},{6,7},{7,4},{8,9},{9,10},{10,1... | collective-permute-start | bytes 933896 | tf_op jit(solution)/shard_map/ppermute | solution.py:415
  134.0 10.6 %collective-permute-start.12 = (bf16[64,2432]{1,0:T(8,128)(2,1)S(1)}, bf16[64,2432]{1,0:T(8,128)(2,1)S(1)}, u32[]{:S(2)}, u32[]{:S(2)}) collective-permute-start(bf16[64,2432]{1,0:T(8,128)(2,1)S(1)} %get-tuple-element.21), channel_id=1, source_target_pairs={{0,3},{1,0},{2,1},{3,2},{4,7},{5,4},{6,5},{7,6},{8,11},{9,8},{10,9... | collective-permute-start | bytes 933896 | tf_op jit(solution)/shard_map/ppermute | solution.py:415
  137.3 10.8 %collective-permute-start.14 = (bf16[64,2432]{1,0:T(8,128)(2,1)S(1)}, bf16[64,2432]{1,0:T(8,128)(2,1)S(1)}, u32[]{:S(2)}, u32[]{:S(2)}) collective-permute-start(bf16[64,2432]{1,0:T(8,128)(2,1)S(1)} %get-tuple-element.23), channel_id=1, source_target_pairs={{0,1},{1,2},{2,3},{3,0},{4,5},{5,6},{6,7},{7,4},{8,9},{9,10},{10,1... | collective-permute-start | bytes 933896 | tf_op jit(solution)/shard_map/ppermute | solution.py:415
  137.3 10.8 %collective-permute-start.15 = (bf16[64,2432]{1,0:T(8,128)(2,1)S(1)}, bf16[64,2432]{1,0:T(8,128)(2,1)S(1)}, u32[]{:S(2)}, u32[]{:S(2)}) collective-permute-start(bf16[64,2432]{1,0:T(8,128)(2,1)S(1)} %get-tuple-element.24), channel_id=1, source_target_pairs={{0,3},{1,0},{2,1},{3,2},{4,7},{5,4},{6,5},{7,6},{8,11},{9,8},{10,9... | collective-permute-start | bytes 933896 | tf_op jit(solution)/shard_map/ppermute | solution.py:415
  144.8 12.7 %collective-permute-start.13 = (bf16[64,2432]{1,0:T(8,128)(2,1)S(1)}, bf16[64,2432]{1,0:T(8,128)(2,1)S(1)}, u32[]{:S(2)}, u32[]{:S(2)}) collective-permute-start(bf16[64,2432]{1,0:T(8,128)(2,1)S(1)} %get-tuple-element.22), channel_id=1, source_target_pairs={{0,1},{1,2},{2,3},{3,0},{4,5},{5,6},{6,7},{7,4},{8,9},{9,10},{10,1... | collective-permute-start | bytes 933896 | tf_op jit(solution)/shard_map/ppermute | solution.py:415
  144.9 12.6 %collective-permute-start.16 = (bf16[64,2432]{1,0:T(8,128)(2,1)S(1)}, bf16[64,2432]{1,0:T(8,128)(2,1)S(1)}, u32[]{:S(2)}, u32[]{:S(2)}) collective-permute-start(bf16[64,2432]{1,0:T(8,128)(2,1)S(1)} %get-tuple-element.25), channel_id=1, source_target_pairs={{0,3},{1,0},{2,1},{3,2},{4,7},{5,4},{6,5},{7,6},{8,11},{9,8},{10,9... | collective-permute-start | bytes 933896 | tf_op jit(solution)/shard_map/ppermute | solution.py:415
  158.1 10.8 %collective-permute-start.19 = (bf16[128,1152]{1,0:T(8,128)(2,1)S(1)}, bf16[128,1152]{1,0:T(8,128)(2,1)S(1)}, u32[]{:S(2)}, u32[]{:S(2)}) collective-permute-start(bf16[128,1152]{1,0:T(8,128)(2,1)S(1)} %shard_map.136.h0), channel_id=1, source_target_pairs={{0,3},{1,0},{2,1},{3,2},{4,7},{5,4},{6,5},{7,6},{8,11},{9,8},{10,9... | collective-permute-start | bytes 884744 | tf_op jit(solution)/shard_map/ppermute | solution.py:415
  161.5 8.3 %collective-permute-start.18 = (bf16[128,1152]{1,0:T(8,128)(2,1)S(1)}, bf16[128,1152]{1,0:T(8,128)(2,1)S(1)}, u32[]{:S(2)}, u32[]{:S(2)}) collective-permute-start(bf16[128,1152]{1,0:T(8,128)(2,1)S(1)} %shard_map.136.h0), channel_id=1, source_target_pairs={{0,2},{1,3},{2,0},{3,1},{4,6},{5,7},{6,4},{7,5},{8,10},{9,11},{10,... | collective-permute-start | bytes 884744 | tf_op jit(solution)/shard_map/ppermute | solution.py:415
  161.5 11.1 %collective-permute-start.17 = (bf16[128,1152]{1,0:T(8,128)(2,1)S(1)}, bf16[128,1152]{1,0:T(8,128)(2,1)S(1)}, u32[]{:S(2)}, u32[]{:S(2)}) collective-permute-start(bf16[128,1152]{1,0:T(8,128)(2,1)S(1)} %shard_map.136.h0), channel_id=1, source_target_pairs={{0,1},{1,2},{2,3},{3,0},{4,5},{5,6},{6,7},{7,4},{8,9},{9,10},{10,1... | collective-permute-start | bytes 884744 | tf_op jit(solution)/shard_map/ppermute | solution.py:415
